TPU v7x, 32 devices: a whole 2x2x4 slice. The times are simulated.
32 devices in a mesh: dp: 8 (over z, y), fsdp: 4 (over x, core).
Axes of the slice: x: 2, y: 2, z: 4, core: 2. Of those that a mesh axis runs over, the one named last changes fastest.
Arguments:
- images: bfloat16 [128, 32, 32, 256], P(('dp', 'fsdp')), may hold values from -6 to 6
- image_sizes: int32 [128, 2], P(('dp', 'fsdp')), may hold values from 16 to 32, as said below
- out_grad: bfloat16 [128, 16, 16, 256], P(('dp', 'fsdp')), may hold values from -6 to 6
- weight_one: float32 [147456], P(('dp', 'fsdp')), may hold values from -0.125 to 0.125
- first_one: float32 [147456], P(('dp', 'fsdp')), may hold values from -6 to 6
- second_one: float32 [147456], P(('dp', 'fsdp')), may hold values from 0.4194304 to 1.6777216
- weight_two: float32 [36864], P(('dp', 'fsdp')), may hold values from -0.25 to 0.25
- first_two: float32 [36864], P(('dp', 'fsdp')), may hold values from -16 to 16
- second_two: float32 [36864], P(('dp', 'fsdp')), may hold values from 0.5308416 to 2.1233664
- weight_three: float32 [36864], P(('dp', 'fsdp')), may hold values from -0.25 to 0.25
- first_three: float32 [36864], P(('dp', 'fsdp')), may hold values from -24 to 24
- second_three: float32 [36864], P(('dp', 'fsdp')), may hold values from 1.47456 to 5.89824
- weight_four: float32 [16384], P(('dp', 'fsdp')), may hold values from -48 to 48
- first_four: float32 [16384], P(('dp', 'fsdp')), may hold values from -0.875 to 0.875
- second_four: float32 [16384], P(('dp', 'fsdp')), may hold values from 0.000262144 to 0.001048576
- biases: float32 [448], replicated
- first_bias: float32 [448], replicated
- second_bias: float32 [448], replicated, as said below
Outputs:
- block_out: bfloat16 [128, 16, 16, 256], P(('dp', 'fsdp'))
- image_grad: bfloat16 [128, 32, 32, 256], P(('dp', 'fsdp'))
- first_one_new: float32 [147456], P(('dp', 'fsdp'))
- second_one_new: float32 [147456], P(('dp', 'fsdp'))
- weight_one_new: float32 [147456], P(('dp', 'fsdp'))
- copy_one: bfloat16 [147456], P(('dp', 'fsdp'))
- first_two_new: float32 [36864], P(('dp', 'fsdp'))
- second_two_new: float32 [36864], P(('dp', 'fsdp'))
- weight_two_new: float32 [36864], P(('dp', 'fsdp'))
- copy_two: bfloat16 [36864], P(('dp', 'fsdp'))
- first_three_new: float32 [36864], P(('dp', 'fsdp'))
- second_three_new: float32 [36864], P(('dp', 'fsdp'))
- weight_three_new: float32 [36864], P(('dp', 'fsdp'))
- copy_three: bfloat16 [36864], P(('dp', 'fsdp'))
- first_four_new: float32 [16384], P(('dp', 'fsdp'))
- second_four_new: float32 [16384], P(('dp', 'fsdp'))
- weight_four_new: float32 [16384], P(('dp', 'fsdp'))
- copy_four: bfloat16 [16384], P(('dp', 'fsdp'))
- first_bias_new: float32 [448], replicated
- second_bias_new: float32 [448], replicated
- biases_new: float32 [448], replicated
- copy_bias: bfloat16 [448], replicated
Inputs may be any that keep to these rules, and one draw needn't show every extreme that they name: `image_sizes`: each height and width is 16, 24 or 32; the first image is 32 x 32. `second_bias`: Positive.
All inputs are finite; a program needn't handle non-finite values.
Results may differ from a plain program's by a relative error of at most 0.0069.
Values may be sent and summed in bfloat16 or wider, within the bound.
No kernel may reach another device: no remote copies, remote signals or barrier semaphores. Data moves between devices by JAX's collectives and lax.ppermute only.
A program may use at most 192 MiB of HBM per device.

v0:
```python
import jax
import jax.numpy as jnp
from jax import lax
from jax.sharding import PartitionSpec as P

C = 256
HID = 64
STEP = 10


GAIN = 1.0 / 64.0
BETA_ONE = 0.9
BETA_TWO = 0.999
DECAY = 0.01
EPSILON = 1e-08


def silu_slope(value):
    sigma = jax.nn.sigmoid(value)
    return sigma * (1.0 + value * (1.0 - sigma))


def conv_same(active, kernel):
    return lax.conv_general_dilated(
        active,
        kernel,
        (1, 1),
        "SAME",
        dimension_numbers=("NHWC", "HWIO", "NHWC"),
        preferred_element_type=jnp.float32,
    )


def conv_back(grad_low, kernel):
    turned = jnp.transpose(jnp.flip(kernel, (0, 1)), (0, 1, 3, 2))
    return conv_same(grad_low, turned)


def tap_grads(active, grad_low):
    side_h = active.shape[1]
    side_w = active.shape[2]
    padded = jnp.pad(active, ((0, 0), (1, 1), (1, 1), (0, 0)))
    tap_rows = []
    for row_tap in range(3):
        tap_cols = []
        for col_tap in range(3):
            window = padded[:, row_tap : row_tap + side_h, col_tap : col_tap + side_w, :]
            tap_cols.append(
                jnp.einsum("nhwc,nhwo->co", window, grad_low, preferred_element_type=jnp.float32)
            )
        tap_rows.append(jnp.stack(tap_cols))
    return jnp.stack(tap_rows)


def image_masks(image_sizes, side_len):
    places = jnp.arange(side_len, dtype=jnp.int32)
    inside = (places[None, :, None] < image_sizes[:, 0, None, None]) & (
        places[None, None, :] < image_sizes[:, 1, None, None]
    )
    halves = jnp.arange(side_len // 2, dtype=jnp.int32)
    pooled = (halves[None, :, None] < (image_sizes[:, 0] // 2)[:, None, None]) & (
        halves[None, None, :] < (image_sizes[:, 1] // 2)[:, None, None]
    )
    return (inside.astype(jnp.float32)[..., None], pooled.astype(jnp.float32)[..., None])


def adamw_update(weight, gradient, first_old, second_old, step_rate):
    first_new = BETA_ONE * first_old + (1.0 - BETA_ONE) * gradient
    second_new = BETA_TWO * second_old + (1.0 - BETA_TWO) * gradient * gradient
    first_hat = first_new / (1.0 - BETA_ONE**STEP)
    second_hat = second_new / (1.0 - BETA_TWO**STEP)
    weight_new = weight - step_rate * (
        first_hat / (jnp.sqrt(second_hat) + EPSILON) + DECAY * weight
    )
    return (first_new, second_new, weight_new, weight_new.astype(jnp.bfloat16))


def shape_kernels(full_one, full_two, full_three, full_four):
    return (
        full_one.reshape(3, 3, C, HID),
        full_two.reshape(3, 3, HID, HID),
        full_three.reshape(3, 3, HID, HID),
        full_four.reshape(HID, C),
    )


def local(
    images,
    image_sizes,
    out_grad,
    weight_one,
    first_one,
    second_one,
    weight_two,
    first_two,
    second_two,
    weight_three,
    first_three,
    second_three,
    weight_four,
    first_four,
    second_four,
    biases,
    first_bias,
    second_bias,
):
    low_one = weight_one.astype(jnp.bfloat16)
    low_two = weight_two.astype(jnp.bfloat16)
    low_three = weight_three.astype(jnp.bfloat16)
    low_four = weight_four.astype(jnp.bfloat16)
    full_one, full_two, full_three, full_four = (
        lax.all_gather(low_one, ("dp", "fsdp"), axis=0, tiled=True),
        lax.all_gather(low_two, ("dp", "fsdp"), axis=0, tiled=True),
        lax.all_gather(low_three, ("dp", "fsdp"), axis=0, tiled=True),
        lax.all_gather(low_four, ("dp", "fsdp"), axis=0, tiled=True),
    )
    kernel_one, kernel_two, kernel_three, kernel_four = shape_kernels(
        full_one, full_two, full_three, full_four
    )
    inside, pooled = image_masks(image_sizes, images.shape[1])
    base = images.astype(jnp.float32) * inside
    act_base = jax.nn.silu(base).astype(jnp.bfloat16)
    conv_one = conv_same(act_base, kernel_one) + biases[0:HID]
    act_one = (jax.nn.silu(conv_one) * inside).astype(jnp.bfloat16)
    conv_two = conv_same(act_one, kernel_two) + biases[HID : 2 * HID]
    act_two = (jax.nn.silu(conv_two) * inside).astype(jnp.bfloat16)
    conv_three = conv_same(act_two, kernel_three) + biases[2 * HID : 3 * HID]
    act_three = (jax.nn.silu(conv_three) * inside).astype(jnp.bfloat16)
    conv_four = (
        jnp.einsum("nhwc,co->nhwo", act_three, kernel_four, preferred_element_type=jnp.float32)
        + biases[3 * HID :]
    )
    summed = base + GAIN * conv_four
    count, side_h, side_w, width = summed.shape
    block_out = (
        jnp.mean(summed.reshape(count, side_h // 2, 2, side_w // 2, 2, width), axis=(2, 4)) * pooled
    ).astype(jnp.bfloat16)
    back_one, back_two, back_three, back_four = (
        lax.all_gather(low_one, ("dp", "fsdp"), axis=0, tiled=True),
        lax.all_gather(low_two, ("dp", "fsdp"), axis=0, tiled=True),
        lax.all_gather(low_three, ("dp", "fsdp"), axis=0, tiled=True),
        lax.all_gather(low_four, ("dp", "fsdp"), axis=0, tiled=True),
    )
    kernel_one, kernel_two, kernel_three, kernel_four = shape_kernels(
        back_one, back_two, back_three, back_four
    )
    spread = out_grad.astype(jnp.float32) * pooled * 0.25
    spread = jnp.broadcast_to(
        spread[:, :, None, :, None, :], (count, side_h // 2, 2, side_w // 2, 2, width)
    ).reshape(count, side_h, side_w, width)
    grad_four = (GAIN * spread).astype(jnp.bfloat16)
    weight_grad_four = jnp.einsum(
        "nhwc,nhwo->co", act_three, grad_four, preferred_element_type=jnp.float32
    )
    bias_grad_four = jnp.sum(grad_four.astype(jnp.float32), axis=(0, 1, 2))
    back_three = jnp.einsum(
        "nhwo,co->nhwc", grad_four, kernel_four, preferred_element_type=jnp.float32
    )
    grad_three = (back_three * inside * silu_slope(conv_three)).astype(jnp.bfloat16)
    weight_grad_three = tap_grads(act_two, grad_three)
    bias_grad_three = jnp.sum(grad_three.astype(jnp.float32), axis=(0, 1, 2))
    back_two = conv_back(grad_three, kernel_three)
    grad_two = (back_two * inside * silu_slope(conv_two)).astype(jnp.bfloat16)
    weight_grad_two = tap_grads(act_one, grad_two)
    bias_grad_two = jnp.sum(grad_two.astype(jnp.float32), axis=(0, 1, 2))
    back_one = conv_back(grad_two, kernel_two)
    grad_one = (back_one * inside * silu_slope(conv_one)).astype(jnp.bfloat16)
    weight_grad_one = tap_grads(act_base, grad_one)
    bias_grad_one = jnp.sum(grad_one.astype(jnp.float32), axis=(0, 1, 2))
    back_base = conv_back(grad_one, kernel_one)
    image_grad = ((spread + back_base * silu_slope(base)) * inside).astype(jnp.bfloat16)
    flat_one = weight_grad_one.reshape(-1)
    flat_two = weight_grad_two.reshape(-1)
    flat_three = weight_grad_three.reshape(-1)
    flat_four = weight_grad_four.reshape(-1)
    sum_one, sum_two, sum_three, sum_four = (
        lax.psum_scatter(flat_one, ("dp", "fsdp"), scatter_dimension=0, tiled=True),
        lax.psum_scatter(flat_two, ("dp", "fsdp"), scatter_dimension=0, tiled=True),
        lax.psum_scatter(flat_three, ("dp", "fsdp"), scatter_dimension=0, tiled=True),
        lax.psum_scatter(flat_four, ("dp", "fsdp"), scatter_dimension=0, tiled=True),
    )
    bias_local = jnp.concatenate([bias_grad_one, bias_grad_two, bias_grad_three, bias_grad_four])
    bias_total = lax.psum(bias_local, ("dp", "fsdp"))
    bias_rates = jnp.where(jnp.arange(3 * HID + C) < 3 * HID, 0.5, 32.0)
    upd_one = adamw_update(weight_one, sum_one, first_one, second_one, (9.0 * C) ** (-0.5))
    upd_two = adamw_update(weight_two, sum_two, first_two, second_two, (9.0 * HID) ** (-0.5))
    upd_three = adamw_update(
        weight_three, sum_three, first_three, second_three, (9.0 * HID) ** (-0.5)
    )
    upd_four = adamw_update(weight_four, sum_four, first_four, second_four, 8.0)
    upd_bias = adamw_update(biases, bias_total, first_bias, second_bias, bias_rates)
    return (
        block_out,
        image_grad,
        upd_one[0],
        upd_one[1],
        upd_one[2],
        upd_one[3],
        upd_two[0],
        upd_two[1],
        upd_two[2],
        upd_two[3],
        upd_three[0],
        upd_three[1],
        upd_three[2],
        upd_three[3],
        upd_four[0],
        upd_four[1],
        upd_four[2],
        upd_four[3],
        upd_bias[0],
        upd_bias[1],
        upd_bias[2],
        upd_bias[3],
    )


def solution(mesh):
    return jax.shard_map(
        local,
        mesh=mesh,
        in_specs=(
            P(("dp", "fsdp"), None, None, None),
            P(("dp", "fsdp"), None),
            P(("dp", "fsdp"), None, None, None),
            P(("dp", "fsdp")),
            P(("dp", "fsdp")),
            P(("dp", "fsdp")),
            P(("dp", "fsdp")),
            P(("dp", "fsdp")),
            P(("dp", "fsdp")),
            P(("dp", "fsdp")),
            P(("dp", "fsdp")),
            P(("dp", "fsdp")),
            P(("dp", "fsdp")),
            P(("dp", "fsdp")),
            P(("dp", "fsdp")),
            P(),
            P(),
            P(),
        ),
        out_specs=(
            P(("dp", "fsdp"), None, None, None),
            P(("dp", "fsdp"), None, None, None),
            P(("dp", "fsdp")),
            P(("dp", "fsdp")),
            P(("dp", "fsdp")),
            P(("dp", "fsdp")),
            P(("dp", "fsdp")),
            P(("dp", "fsdp")),
            P(("dp", "fsdp")),
            P(("dp", "fsdp")),
            P(("dp", "fsdp")),
            P(("dp", "fsdp")),
            P(("dp", "fsdp")),
            P(("dp", "fsdp")),
            P(("dp", "fsdp")),
            P(("dp", "fsdp")),
            P(("dp", "fsdp")),
            P(("dp", "fsdp")),
            P(),
            P(),
            P(),
            P(),
        ),
        check_vma=False,
    )
```

profile of v0, /device:TPU:0, one launch (start us, length us, event | category | flops | bytes accessed | tf_op | source)
XLA Modules:
  0.0 484.9 jit_solution(4907513272570414096)
XLA Ops:
  8.9 3.6 multiply_convert_fusion.1
  12.6 2.2 fusion.184
  14.9 44.8 %all-gather = bf16[32,1,4608]{2,1,0:T(2,128)(2,1)S(1)} all-gather(bf16[1,1,4608]{2,1,0:T(2,128)(2,1)S(1)} %reshape.319), channel_id=1, replica_groups=mesh['dp'=8,'fsdp'=4] {'dp','fsdp'}, dimensions={0}, use_global_device_ids=true | all-gather | bytes 304128 | tf_op jit(solution)/shard_map/all_gather | solution.py:112
  59.7 1.7 reduce.1
  61.8 3.0 copy.491
  65.9 10.8 %add_multiply_fusion.2 = (f32[32,32,5,64]{3,1,2,0:T(8,128)}, f32[32,32,5,64]{3,1,2,0:T(8,128)S(1)}) fusion(f32[64]{0:T(128)S(1)} %get-tuple-element.88, pred[32,5]{0,1:T(8,128)(4,1)S(1)} %copy-done.67, bf16[3,3,256,64]{3,2,1,0:T(8,128)(2,1)S(1)} %reshape.240, bf16[32,4,8,7,256]{4,0,3,2,1:T(8,128)(2,1)S(1)} %fusion.5), kind=kOutput, calls=%fused_computation.39 | convolution fusion | flops 1481768960 | bytes 6586784 | tf_op jit(solution)/shard_map/conv_general_dilated | solution.py:24
  76.7 1.5 copy.368
  79.8 2.6 fusion.183
  82.3 37.0 %all-gather.1 = bf16[32,1,1152]{2,1,0:T(2,128)(2,1)S(1)} all-gather(bf16[1,1,1152]{2,1,0:T(2,128)(2,1)S(1)} %reshape.321), channel_id=1, replica_groups=mesh['dp'=8,'fsdp'=4] {'dp','fsdp'}, dimensions={0}, use_global_device_ids=true | all-gather | bytes 76032 | tf_op jit(solution)/shard_map/all_gather | solution.py:113
  120.0 1.7 copy.492
  122.4 4.4 add_multiply_fusion.1
  126.8 1.5 copy.372
  128.5 2.2 fusion.28
  130.7 2.2 fusion.182
  132.9 38.1 %all-gather.3 = bf16[32,1,512]{2,1,0:T(2,128)(2,1)S(1)} all-gather(bf16[1,1,512]{2,1,0:T(2,128)(2,1)S(1)} %reshape.325), channel_id=1, replica_groups=mesh['dp'=8,'fsdp'=4] {'dp','fsdp'}, dimensions={0}, use_global_device_ids=true | all-gather | bytes 33792 | tf_op jit(solution)/shard_map/all_gather | solution.py:115
  171.3 37.0 %all-gather.2 = bf16[32,1,1152]{2,1,0:T(2,128)(2,1)S(1)} all-gather(bf16[1,1,1152]{2,1,0:T(2,128)(2,1)S(1)} %reshape.323), channel_id=1, replica_groups=mesh['dp'=8,'fsdp'=4] {'dp','fsdp'}, dimensions={0}, use_global_device_ids=true | all-gather | bytes 76032 | tf_op jit(solution)/shard_map/all_gather | solution.py:114
  208.9 3.3 copy.390
  213.8 1.6 fusion.164
  215.4 3.6 broadcast_in_dim.13
  219.0 4.3 convert_element_type.118
  223.2 3.3 copy.384
  228.8 3.0 add_multiply_fusion
  231.9 1.5 copy.378
  234.6 4.3 pad_slice_fusion.15
  238.9 2.4 convert_reduce_fusion
  243.5 3.5 fusion.70
  247.0 1.5 copy.382
  248.7 4.2 pad_slice_fusion.23
  252.8 3.0 convert_reduce_fusion.1
  257.9 3.4 fusion.73
  261.4 1.5 copy.388
  263.1 1.5 copy.376
  266.2 9.8 %pad_slice_fusion.7 = (bf16[4,32,32,256]{3,2,1,0:T(8,128)(2,1)}, bf16[4,32,32,256]{3,2,1,0:T(8,128)(2,1)}, bf16[4,32,32,256]{3,2,1,0:T(8,128)(2,1)}, bf16[4,32,3...) fusion(bf16[4,32,32,256]{3,2,1,0:T(8,128)(2,1)S(1)} %copy-done.1), kind=kLoop, calls=%fused_computation.29 | loop fusion | bytes 18874368 | tf_op jit(solution)/shard_map/slice | solution.py:47
  276.0 5.2 %convert_reduce_fusion.2 = (f32[64]{0:T(128)}, bf16[4,32,32,64]{3,2,1,0:T(8,128)(2,1)S(1)}, bf16[4,32,32,64]{3,2,1,0:T(8,128)(2,1)}) fusion(f32[32,4,32,64]{3,0,2,1:T(8,128)S(1)} %copy-done.3, f32[4,32,32]{2,1,0:T(8,128)S(1)} %and_convert_fusion, f32[32,4,32,64]{3,0,2,1:T(8,128)S(1)} %slice.154, f32[32,4,32,64]{3,0,2,1:T(8,128)S(1)} %slice.148), kind=kLoop, calls=%fused_computation.88 | loop fusion | flops 1834944 | bytes 4210944 | tf_op jit(solution)/shard_map/reduce_sum | solution.py:169
  284.0 4.0 broadcast_select_fusion
  288.0 3.0 copy.394
  291.1 2.3 slice.157
  293.4 4.2 broadcast_in_dim.12
  297.6 6.1 %reshape.245 = f32[4,32,32,256]{3,2,1,0:T(8,128)} reshape(f32[4,16,2,16,2,256]{5,4,3,2,1,0:T(2,128)} %broadcast_in_dim.12) | data formatting | bytes 8388608 | tf_op jit(solution)/shard_map/reshape | solution.py:150
  303.7 7.0 %multiply_convert_fusion = (bf16[4,32,32,256]{3,2,1,0:T(8,128)(2,1)S(1)}, bf16[4,32,32,256]{3,2,1,0:T(8,128)(2,1)}) fusion(f32[4,32,32,256]{3,2,1,0:T(8,128)} %reshape.245, f32[4,32,32]{2,1,0:T(8,128)S(1)} %and_convert_fusion, bf16[4,32,32,256]{3,2,1,0:T(8,128)(2,1)S(1)} %copy-done, f32[32,4,32,256]{3,0,2,1:T(8,128)} %slice.157), kind=kLoop, calls=%fused_computation.7 | loop fusion | flops 15728640 | bytes 14696448 | tf_op jit(solution)/shard_map/convert_element_type | solution.py:151
  319.4 2.1 convolution_bitcast_fusion.8
  328.2 2.3 fusion.76
  344.6 1.9 broadcast_reduce_fusion
  346.6 37.3 %psum.7 = f32[448]{0:T(512)S(1)} all-reduce(f32[448]{0:T(512)S(1)} %pad_maximum_fusion.3), channel_id=1, replica_groups=mesh['dp'=8,'fsdp'=4] {'dp','fsdp'}, use_global_device_ids=true, to_apply=%region_9.10 | all-reduce | flops 448 | bytes 3584 | tf_op jit(solution)/shard_map/psum | solution.py:183
  383.9 2.6 multiply_add_fusion
  386.5 5.9 %reshape.244 = f32[4,16,2,16,2,256]{5,4,3,2,1,0:T(2,128)} reshape(f32[4,32,32,256]{3,2,1,0:T(8,128)} %multiply_add_fusion) | data formatting | bytes 8388608 | tf_op jit(solution)/shard_map/reshape | solution.py:136
  392.5 5.6 %reduce_sum.45 = f32[4,16,16,256]{3,2,1,0:T(8,128)S(1)} reduce(f32[4,16,2,16,2,256]{5,4,3,2,1,0:T(2,128)} %reshape.244, f32[]{:T(128)} %constant.36.clone.1), dimensions={2,4}, to_apply=%region_0.1 | reduce | flops 786432 | bytes 5242884 | tf_op jit(solution)/shard_map/reduce_sum | solution.py:136
  399.7 72.3 %all-reduce.10.cloned.1.call-done = (f32[147456]{0:T(1024)}, f32[36864]{0:T(1024)}, f32[36864]{0:T(1024)}, f32[16384]{0:T(1024)}) async-done(((f32[147456]{0:T(1024)}, f32[36864]{0:T(1024)}, f32[36864]{0:T(1024)}, f32[16384]{0:T(1024)}), (f32[147456]{0:T(1024)}, f32[36864]{0:T(1024)}, f32[36864]{0:T(1024)}, f32[16384]{0:T(1024)})) %all-reduce.10.cloned.1.call-update) | async-done | bytes 950288
  (243 shorter events, 57.5 us)
Async XLA Ops:
  7.2 464.8 %all-reduce.10.cloned.1.call-start = ((), (), s32[]{:S(2)}) async-start(), calls=%async_computation | async-start | bytes 1900544
  8.9 3.6 copy-start
  12.6 2.2 copy-start.48
  12.6 2.3 copy-start.40
  61.8 4.0 copy-start.35
  79.8 2.6 copy-start.43
  119.9 2.4 copy-start.38
  130.7 2.2 copy-start.54
  130.7 2.2 copy-start.44
  212.1 1.7 copy-start.37
  213.7 5.3 %copy-start.56 = (pred[4,16]{1,0:T(4,128)(4,1)}, pred[4,16]{1,0:T(4,128)(4,1)S(1)}, u32[]{:S(2)}) copy-start(pred[4,16]{1,0:T(4,128)(4,1)S(1)} %get-tuple-element.97) | copy-start | bytes 196
  213.7 5.3 %copy-start.58 = (pred[4,16]{1,0:T(4,128)(4,1)}, pred[4,16]{1,0:T(4,128)(4,1)S(1)}, u32[]{:S(2)}) copy-start(pred[4,16]{1,0:T(4,128)(4,1)S(1)} %get-tuple-element.98) | copy-start | bytes 196
  234.6 4.3 copy-start.2
  241.3 1.5 copy-start.9
  264.6 1.6 copy-start.1
  266.2 9.8 %copy-start.3 = (f32[32,4,32,64]{3,0,2,1:T(8,128)S(1)}, f32[32,4,32,64]{3,0,2,1:T(8,128)}, u32[]{:S(2)}) copy-start(f32[32,4,32,64]{3,0,2,1:T(8,128)} %slice.155) | copy-start | bytes 3145732
  291.1 2.3 copy-start.4
  303.7 7.1 %copy-start.7 = (bf16[4,32,32,64]{3,2,1,0:T(8,128)(2,1)S(1)}, bf16[4,32,32,64]{3,2,1,0:T(8,128)(2,1)}, u32[]{:S(2)}) copy-start(bf16[4,32,32,64]{3,2,1,0:T(8,128)(2,1)} %get-tuple-element.85) | copy-start | bytes 1572868
  310.8 1.6 copy-start.34
  311.2 1.5 copy-start.33
  319.4 2.1 copy-start.10
  319.4 2.2 copy-start.26
  328.2 2.3 copy-start.19
  330.5 1.6 copy-start.18
  332.1 1.6 copy-start.17
  333.7 1.6 copy-start.16
  335.3 1.6 copy-start.15
  336.9 1.6 copy-start.14
  338.5 1.6 copy-start.13
  341.8 2.6 copy-start.49
  341.8 2.7 copy-start.57
  341.8 2.7 copy-start.59
  343.3 3.2 copy-start.60
  343.3 3.2 copy-start.61
  343.3 3.2 copy-start.62
  344.4 39.5 %copy-start.8 = (bf16[4,32,32,64]{3,2,1,0:T(8,128)(2,1)S(1)}, bf16[4,32,32,64]{3,2,1,0:T(8,128)(2,1)}, u32[]{:S(2)}) copy-start(bf16[4,32,32,64]{3,2,1,0:T(8,128)(2,1)} %get-tuple-element.85) | copy-start | bytes 1572868
  392.4 5.7 %copy-start.63 = (f32[448]{0:T(512)S(1)}, f32[448]{0:T(512)}, u32[]{:S(2)}) copy-start(f32[448]{0:T(512)} %param.35) | copy-start | bytes 5380
  392.4 5.7 %copy-start.64 = (f32[448]{0:T(512)S(1)}, f32[448]{0:T(512)}, u32[]{:S(2)}) copy-start(f32[448]{0:T(512)} %param.34) | copy-start | bytes 5380
  392.4 79.6 %copy-start.50 = (f32[1152]{0:T(1024)S(1)}, f32[1152]{0:T(1024)}, u32[]{:S(2)}) copy-start(f32[1152]{0:T(1024)} %param.26) | copy-start | bytes 13828
  392.4 79.6 %copy-start.51 = (f32[1152]{0:T(1024)S(1)}, f32[1152]{0:T(1024)}, u32[]{:S(2)}) copy-start(f32[1152]{0:T(1024)} %param.25) | copy-start | bytes 13828
  392.4 81.0 %copy-start.52 = (f32[1152]{0:T(1024)S(1)}, f32[1152]{0:T(1024)}, u32[]{:S(2)}) copy-start(f32[1152]{0:T(1024)} %param.29) | copy-start | bytes 13828
  392.4 81.0 %copy-start.53 = (f32[1152]{0:T(1024)S(1)}, f32[1152]{0:T(1024)}, u32[]{:S(2)}) copy-start(f32[1152]{0:T(1024)} %param.28) | copy-start | bytes 13828
  392.4 82.4 %copy-start.41 = (f32[4608]{0:T(1024)S(1)}, f32[4608]{0:T(1024)}, u32[]{:S(2)}) copy-start(f32[4608]{0:T(1024)} %param.21) | copy-start | bytes 55300
  392.4 82.4 %copy-start.46 = (f32[4608]{0:T(1024)S(1)}, f32[4608]{0:T(1024)}, u32[]{:S(2)}) copy-start(f32[4608]{0:T(1024)} %param.23) | copy-start | bytes 55300
  392.4 82.4 %copy-start.47 = (f32[4608]{0:T(1024)S(1)}, f32[4608]{0:T(1024)}, u32[]{:S(2)}) copy-start(f32[4608]{0:T(1024)} %param.22) | copy-start | bytes 55300
  392.5 83.8 %copy-start.55 = (f32[512]{0:T(512)S(1)}, f32[512]{0:T(512)}, u32[]{:S(2)}) copy-start(f32[512]{0:T(512)} %param.30) | copy-start | bytes 6148
  392.5 83.8 %copy-start.65 = (f32[512]{0:T(512)S(1)}, f32[512]{0:T(512)}, u32[]{:S(2)}) copy-start(f32[512]{0:T(512)} %param.32) | copy-start | bytes 6148
  392.5 83.8 %copy-start.66 = (f32[512]{0:T(512)S(1)}, f32[512]{0:T(512)}, u32[]{:S(2)}) copy-start(f32[512]{0:T(512)} %param.31) | copy-start | bytes 6148
  (21 other events, 24.3 us)
Sparse Core Ops, SparseCore 0:
  344.6 127.3 all-reduce.9
where the time goes:
time: 491 us; the launch traced here: 485 us
  blocking collectives  194 us (40%)
  local copies, waits for them, and re-layouts  97.3 us (20%)
  waiting for transfers between devices  72.3 us (15%)
  other arithmetic  53.2 us (11%)
  matrix products  52 us (11%)
  between operations  15.6 us (3%)
    unnamed x2, waiting for transfers between devices  72.3 us
    all_gather x1, blocking collectives, local(): lax.all_gather(low_one, ('dp', 'fsdp'), axis=0, tiled=True)  44.8 us
    all_gather x1, blocking collectives, local(): lax.all_gather(low_four, ('dp', 'fsdp'), axis=0, tiled=True)  38.1 us
    psum x1, blocking collectives, local(): bias_total = lax.psum(bias_local, ('dp', 'fsdp'))  37.3 us
    all_gather x1, blocking collectives, local(): lax.all_gather(low_three, ('dp', 'fsdp'), axis=0, tiled=True)  37 us
    all_gather x1, blocking collectives, local(): lax.all_gather(low_two, ('dp', 'fsdp'), axis=0, tiled=True)  37 us
    conv_general_dilated x6, matrix products, conv_same(): lax.conv_general_dilated(active, kernel, (1, 1), 'SAME', dimension_number...  29.1 us
    unnamed x147, local copies, waits for them, and re-layouts  23.9 us
  transfers between devices with their start and end apart: 1, of which 1 were waited for; matrix products, arithmetic and copies ran while one was open for 4% of the time, Pallas kernels for 0%

commit v1 on v0

v1 whole, which is shorter than its diff:
```python
import functools

import jax
import jax.numpy as jnp
from jax import lax
from jax.experimental import pallas as pl
from jax.experimental.pallas import tpu as pltpu
from jax.sharding import PartitionSpec as P

C = 256
HID = 64
STEP = 10
SIDE = 32
HALF = SIDE // 2
ROWS = HALF * SIDE
PAD = SIDE

GAIN = 1.0 / 64.0
BETA_ONE = 0.9
BETA_TWO = 0.999
DECAY = 0.01
EPSILON = 1e-08
AXES = ("dp", "fsdp")

COMPACT = (9 * C * HID // 128, 9 * HID * HID // 128, 9 * HID * HID // 128, HID * C // 128)
BIASES = 3 * HID + C

F32 = jnp.float32
BF16 = jnp.bfloat16


def sigmoid(value):
    return 0.5 * jnp.tanh(0.5 * value) + 0.5


def dot(left, right):
    return jnp.dot(left, right, preferred_element_type=F32)


def dot_rows(left, right):
    return lax.dot_general(left, right, (((0,), (0,)), ((), ())), preferred_element_type=F32)


def swap_halves(value):
    return pltpu.roll(value, HID, 1)


def low_lanes(shape):
    return lax.broadcasted_iota(jnp.int32, shape, 1) < HID


def shard_rows(shards):
    return tuple(rows // shards for rows in COMPACT)


def unpack_weights(shards, me_ref, mine_ref, stage, taps_one, taps_two, taps_three, taps_four):
    one, two, three, four = shard_rows(shards)
    total = one + two + three + four
    held = mine_ref.shape[1]
    stage[...] = mine_ref[...].reshape(shards * held, 128).astype(F32)

    def place(shard, carry):
        owner = me_ref[0] ^ place_mask(shards, shard) if shards > 1 else shard
        start = shard * held
        for taps, rows, at in (
            (taps_one, one, 0),
            (taps_two, two, one),
            (taps_three, three, one + two),
        ):
            value = stage[pl.ds(start + at, rows), :]
            first = owner * (2 * rows)
            taps[pl.ds(first, rows, stride=2), :] = value
            taps[pl.ds(first + 1, rows, stride=2), :] = swap_halves(value)
        at = start + one + two + three
        first = owner * (four // 2)
        for row in range(four // 2):
            taps_four[0, pl.ds(first + row, 1), :] = stage[pl.ds(at + 2 * row, 1), :]
            taps_four[1, pl.ds(first + row, 1), :] = stage[pl.ds(at + 2 * row + 1, 1), :]
        return carry

    lax.fori_loop(0, shards, place, 0)


def tap_blocks(taps, width, col_tap):
    rows = [taps[(row_tap * 3 + col_tap) * width : (row_tap * 3 + col_tap + 1) * width, :] for row_tap in range(3)]
    low = low_lanes((width, 128))
    zero = jnp.zeros((width, 128), F32)
    turned = [swap_halves(value) for value in rows]
    return (
        jnp.where(low, rows[0], zero),
        jnp.where(low, rows[1], turned[0]),
        jnp.where(low, rows[2], turned[1]),
        jnp.where(low, zero, turned[2]),
    )


def main_kernel(
    shards,
    me_ref,
    sizes_ref,
    mine_ref,
    bias_ref,
    img_ref,
    og_ref,
    out_ref,
    grad_ref,
    send_ref,
    bias_out_ref,
    stage,
    taps_one,
    taps_two,
    taps_three,
    taps_four,
    fwd_one,
    back_one,
    fwd_two,
    back_two,
    fwd_three,
    back_three,
    fwd_four,
    back_four,
    spread_up,
    pool_down,
    act_even,
    act_odd,
    slope_even,
    slope_odd,
    act_one,
    act_two,
    act_three,
    spread_low,
    slope_one,
    slope_two,
    turned,
    sum_even,
    sum_odd,
    sum_two,
    sum_three,
    sum_four,
    sum_bias,
):
    step = pl.program_id(0)
    steps = pl.num_programs(0)

    @pl.when(step == 0)
    def prepare():
        unpack_weights(
            shards, me_ref, mine_ref, stage, taps_one, taps_two, taps_three, taps_four
        )
        for col_tap in range(3):
            lanes = slice(col_tap * 128, (col_tap + 1) * 128)
            more = slice(384 + col_tap * 128, 384 + (col_tap + 1) * 128)
            blocks = tap_blocks(taps_one, C, col_tap)
            for place, block in enumerate(blocks):
                fwd_one[place * C : (place + 1) * C, lanes] = block.astype(BF16)
            back_one[lanes, 0:C] = blocks[1].T.astype(BF16)
            back_one[lanes, C : 2 * C] = blocks[2].T.astype(BF16)
            back_one[more, 0:C] = blocks[3].T.astype(BF16)
            back_one[more, C : 2 * C] = blocks[0].T.astype(BF16)
            for taps, fwd, back in (
                (taps_two, fwd_two, back_two),
                (taps_three, fwd_three, back_three),
            ):
                blocks = tap_blocks(taps, HID, col_tap)
                for place, which in enumerate((1, 2, 3, 0)):
                    fwd[place * HID : (place + 1) * HID, lanes] = blocks[which].astype(BF16)
                back[lanes, :] = jnp.concatenate([blocks[1], blocks[2]], axis=0).T.astype(BF16)
                back[more, :] = jnp.concatenate([blocks[3], blocks[0]], axis=0).T.astype(BF16)
        four = jnp.concatenate([taps_four[0], taps_four[1]], axis=1)
        both = jnp.concatenate([four, four], axis=0)
        fwd_four[...] = both.astype(BF16)
        back_four[...] = both.T.astype(BF16)
        pix = lax.broadcasted_iota(jnp.int32, (256, 128), 0)
        spot = lax.broadcasted_iota(jnp.int32, (256, 128), 1)
        spread_up[...] = jnp.where(pix // 2 == spot, 1.0, 0.0).astype(BF16)
        spot = lax.broadcasted_iota(jnp.int32, (128, 256), 0)
        pix = lax.broadcasted_iota(jnp.int32, (128, 256), 1)
        pool_down[...] = jnp.where(pix // 2 == spot, 0.25, 0.0).astype(BF16)
        act_even[ROWS : ROWS + PAD, :] = jnp.zeros((PAD, C), BF16)
        act_odd[0:PAD, :] = jnp.zeros((PAD, C), BF16)
        for act in (act_one, act_two):
            act[0:PAD, :] = jnp.zeros((PAD, 128), BF16)
            act[PAD + ROWS :, :] = jnp.zeros((PAD, 128), BF16)
        turned[0:PAD, :] = jnp.zeros((PAD, 384), BF16)
        turned[PAD + ROWS :, :] = jnp.zeros((PAD, 384), BF16)
        for total in (sum_even, sum_odd, sum_two, sum_three, sum_four, sum_bias):
            total[...] = jnp.zeros(total.shape, F32)

    height = sizes_ref[step, 0]
    width = sizes_ref[step, 1]
    spot = lax.broadcasted_iota(jnp.int32, (ROWS, 128), 0)
    col = jnp.bitwise_and(spot, SIDE - 1)
    inside = (spot < height * HALF) & (col < width)
    mask = jnp.where(inside, 1.0, 0.0)
    wide_mask = jnp.concatenate([mask, mask], axis=1)
    first_col = col == 0
    last_col = col == SIDE - 1
    low = low_lanes((ROWS, 128))
    low_wide = jnp.concatenate([low, low, low], axis=1)

    for parity, act, slope, at in ((0, act_even, slope_even, 0), (1, act_odd, slope_odd, PAD)):
        base = img_ref[0, :, parity].reshape(ROWS, C).astype(F32) * wide_mask
        sigma = sigmoid(base)
        active = base * sigma
        act[at : at + ROWS, :] = active.astype(BF16)
        slope[...] = (sigma + active * (1.0 - sigma)) * wide_mask

    def shift_sum(parts):
        before = jnp.where(first_col, 0.0, pltpu.roll(parts[:, 0:128], 1, 0))
        after = jnp.where(last_col, 0.0, pltpu.roll(parts[:, 256:384], ROWS - 1, 0))
        return before + parts[:, 128:256] + after

    def activate(conv):
        sigma = sigmoid(conv)
        active = conv * sigma
        return active * mask, (sigma + active * (1.0 - sigma)) * mask

    even = act_even[0:ROWS, :]
    odd = act_odd[PAD : PAD + ROWS, :]
    window = jnp.concatenate(
        [act_odd[0:ROWS, :], even, odd, act_even[PAD : PAD + ROWS, :]], axis=1
    )
    conv = shift_sum(dot(window, fwd_one[...])) + bias_ref[0:1, 0:128]
    active, slope = activate(conv)
    act_one[PAD : PAD + ROWS, :] = active.astype(BF16)
    slope_one[...] = slope

    def rows_around(act):
        here = act[PAD : PAD + ROWS, :]
        around = jnp.where(low, act[2 * PAD : 2 * PAD + ROWS, :], act[0:ROWS, :])
        return jnp.concatenate([here, around], axis=1)

    conv = shift_sum(dot(rows_around(act_one), fwd_two[...])) + bias_ref[1:2, 0:128]
    active, slope = activate(conv)
    act_two[PAD : PAD + ROWS, :] = active.astype(BF16)
    slope_two[...] = slope
    conv = shift_sum(dot(rows_around(act_two), fwd_three[...])) + bias_ref[2:3, 0:128]
    active, slope_three = activate(conv)
    act_three[...] = active.astype(BF16)

    pooled = lax.broadcasted_iota(jnp.int32, (256, C), 0)
    pooled_mask = (pooled < height * (HALF // 2)) & (
        jnp.bitwise_and(pooled, HALF - 1) < width // 2
    )
    cot = jnp.where(pooled_mask, og_ref[0].reshape(256, C).astype(F32), 0.0)
    cot_low = cot.astype(BF16)
    pieces = []
    spread = []
    for half in range(2):
        rows = slice(half * 256, (half + 1) * 256)
        base_mean = dot(pool_down[...], img_ref[0, :, 0].reshape(ROWS, C)[rows]) + dot(
            pool_down[...], img_ref[0, :, 1].reshape(ROWS, C)[rows]
        )
        act_mean = dot(pool_down[...], act_three[rows, :]).astype(BF16)
        last = dot(act_mean, fwd_four[...]) + bias_ref[3:4, :]
        pieces.append(base_mean + GAIN * last)
        spread.append(dot(spread_up[...], cot_low[half * 128 : (half + 1) * 128]))
    result = jnp.where(pooled_mask, jnp.concatenate(pieces, axis=0), 0.0)
    out_ref[0] = result.reshape(HALF, HALF, C).astype(BF16)
    spread = jnp.concatenate(spread, axis=0)
    spread_low[...] = spread.astype(BF16)

    part = dot_rows(act_three[...], spread_low[...])
    for row in range(0, 128, 64):
        sum_four[row : row + 64, :] = sum_four[row : row + 64, :] + part[row : row + 64, :]
    sum_bias[3:4, :] += jnp.sum(cot, axis=0, keepdims=True)
    grad = dot(spread_low[...], back_four[...]) * (GAIN * 0.25) * slope_three

    def turn(grad, row):
        sum_bias[row : row + 1, 0:128] += jnp.sum(grad, axis=0, keepdims=True)
        turned[PAD : PAD + ROWS, 0:128] = jnp.where(
            last_col, 0.0, pltpu.roll(grad, ROWS - 1, 0)
        ).astype(BF16)
        turned[PAD : PAD + ROWS, 128:256] = grad.astype(BF16)
        turned[PAD : PAD + ROWS, 256:384] = jnp.where(
            first_col, 0.0, pltpu.roll(grad, 1, 0)
        ).astype(BF16)
        here = turned[PAD : PAD + ROWS, :]
        around = jnp.where(low_wide, turned[2 * PAD : 2 * PAD + ROWS, :], turned[0:ROWS, :])
        return jnp.concatenate([here, around], axis=1)

    window = turn(grad, 2)
    sum_three[...] += dot_rows(act_two[PAD : PAD + ROWS, :], window)
    grad = dot(window, back_three[...]) * slope_two[...]
    window = turn(grad, 1)
    sum_two[...] += dot_rows(act_one[PAD : PAD + ROWS, :], window)
    grad = dot(window, back_two[...]) * slope_one[...]
    window = turn(grad, 0)
    sum_even[...] += dot_rows(even, window)
    sum_odd[...] += dot_rows(odd, window)
    back = dot(window, back_one[...])
    spread = 0.25 * spread
    for parity, slope in ((0, slope_even), (1, slope_odd)):
        value = spread * wide_mask + back[:, parity * C : (parity + 1) * C] * slope[...]
        grad_ref[0, :, parity] = value.reshape(HALF, SIDE, C).astype(BF16)

    @pl.when(step == steps - 1)
    def finish():
        for row_even, row_odd, taps, width_in in (
            (sum_even, sum_odd, taps_one, C),
            (sum_two.at[0:HID], sum_two.at[HID:128], taps_two, HID),
            (sum_three.at[0:HID], sum_three.at[HID:128], taps_three, HID),
        ):
            for col_tap in range(3):
                here = slice(col_tap * 128, (col_tap + 1) * 128)
                around = slice(384 + col_tap * 128, 384 + (col_tap + 1) * 128)
                even_here, even_around = row_even[:, here], row_even[:, around]
                odd_here, odd_around = row_odd[:, here], row_odd[:, around]
                for row_tap, value in (
                    (0, swap_halves(even_here) + odd_around),
                    (1, even_here + swap_halves(odd_here)),
                    (2, swap_halves(even_around) + odd_here),
                ):
                    at = (row_tap * 3 + col_tap) * width_in
                    taps[at : at + width_in, :] = value
        last = (sum_four[0:HID, :] + sum_four[HID:128, :]) * (GAIN * 0.25)
        taps_four[0] = last[:, 0:128]
        taps_four[1] = last[:, 128:256]
        sums = sum_bias[...]
        tail = sums[:, 0:128]
        bias_out_ref[...] = jnp.concatenate(
            [tail + swap_halves(tail), sums[:, 0:128], sums[:, 128:256]], axis=1
        )
        one, two, three, four = shard_rows(shards)
        held = send_ref.shape[1]

        def collect(shard, carry):
            start = shard * held
            for taps, rows, at in (
                (taps_one, one, 0),
                (taps_two, two, one),
                (taps_three, three, one + two),
            ):
                first = shard * (2 * rows)
                upper = taps[pl.ds(first, rows, stride=2), :]
                lower = taps[pl.ds(first + 1, rows, stride=2), :]
                stage[pl.ds(start + at, rows), :] = jnp.where(
                    low_lanes((rows, 128)), upper, swap_halves(lower)
                )
            at = start + one + two + three
            first = shard * (four // 2)
            for row in range(four // 2):
                stage[pl.ds(at + 2 * row, 1), :] = taps_four[0, pl.ds(first + row, 1), :]
                stage[pl.ds(at + 2 * row + 1, 1), :] = taps_four[1, pl.ds(first + row, 1), :]
            return carry

        lax.fori_loop(0, shards, collect, 0)
        send_ref[...] = stage[...].reshape(shards, held, 128).astype(BF16)


def run_main(shards, me, sizes, mine, bias_rows, images, out_grad):
    count = images.shape[0]
    held = mine.shape[1]
    images = images.reshape(count, HALF, 2, SIDE, C)
    whole = lambda shape: pl.BlockSpec(shape, lambda i: (0,) * len(shape))
    smem = pl.BlockSpec(memory_space=pltpu.SMEM)
    vmem = pltpu.VMEM
    padded = ROWS + PAD
    out, grad, send, bias = pl.pallas_call(
        functools.partial(main_kernel, shards),
        grid=(count,),
        in_specs=[
            smem,
            smem,
            whole((shards, held, 128)),
            whole((8, C)),
            pl.BlockSpec((1, HALF, 2, SIDE, C), lambda i: (i, 0, 0, 0, 0)),
            pl.BlockSpec((1, HALF, HALF, C), lambda i: (i, 0, 0, 0)),
        ],
        out_specs=[
            pl.BlockSpec((1, HALF, HALF, C), lambda i: (i, 0, 0, 0)),
            pl.BlockSpec((1, HALF, 2, SIDE, C), lambda i: (i, 0, 0, 0, 0)),
            whole((shards, held, 128)),
            whole((8, 384)),
        ],
        out_shape=[
            jax.ShapeDtypeStruct((count, HALF, HALF, C), BF16),
            jax.ShapeDtypeStruct((count, HALF, 2, SIDE, C), BF16),
            jax.ShapeDtypeStruct((shards, held, 128), BF16),
            jax.ShapeDtypeStruct((8, 384), F32),
        ],
        scratch_shapes=[
            vmem((shards * held, 128), F32),
            vmem((9 * C, 128), F32),
            vmem((9 * HID, 128), F32),
            vmem((9 * HID, 128), F32),
            vmem((2, HID, 128), F32),
            vmem((4 * C, 384), BF16),
            vmem((768, 2 * C), BF16),
            vmem((4 * HID, 384), BF16),
            vmem((768, 128), BF16),
            vmem((4 * HID, 384), BF16),
            vmem((768, 128), BF16),
            vmem((128, C), BF16),
            vmem((C, 128), BF16),
            vmem((256, 128), BF16),
            vmem((128, 256), BF16),
            vmem((padded, C), BF16),
            vmem((padded, C), BF16),
            vmem((ROWS, C), F32),
            vmem((ROWS, C), F32),
            vmem((padded + PAD, 128), BF16),
            vmem((padded + PAD, 128), BF16),
            vmem((ROWS, 128), BF16),
            vmem((ROWS, C), BF16),
            vmem((ROWS, 128), F32),
            vmem((ROWS, 128), F32),
            vmem((padded + PAD, 384), BF16),
            vmem((C, 768), F32),
            vmem((C, 768), F32),
            vmem((128, 768), F32),
            vmem((128, 768), F32),
            vmem((128, C), F32),
            vmem((8, C), F32),
        ],
        compiler_params=pltpu.CompilerParams(
            dimension_semantics=("arbitrary",), vmem_limit_bytes=56 * 1024 * 1024
        ),
        name="block",
    )(me, sizes, mine, bias_rows, images, out_grad)
    bias_part = jnp.concatenate(
        [bias[0, 0:HID], bias[1, 0:HID], bias[2, 0:HID], bias[3, 128:384] * GAIN]
    )
    return out, grad.reshape(count, SIDE, SIDE, C), send, bias_part


def adamw_update(weight, gradient, first_old, second_old, step_rate):
    first_new = BETA_ONE * first_old + (1.0 - BETA_ONE) * gradient
    second_new = BETA_TWO * second_old + (1.0 - BETA_TWO) * gradient * gradient
    first_hat = first_new / (1.0 - BETA_ONE**STEP)
    second_hat = second_new / (1.0 - BETA_TWO**STEP)
    weight_new = weight - step_rate * (
        first_hat / (jnp.sqrt(second_hat) + EPSILON) + DECAY * weight
    )
    return (first_new, second_new, weight_new, weight_new.astype(BF16))


def exchange(value, mask, count):
    return lax.ppermute(value, AXES, [(i, i ^ mask) for i in range(count)])


def gather_shards(value, devices):
    held = value[None]
    for low, top in bit_groups(devices):
        parts = [held] + [
            exchange(held, mask << low, devices) for mask in range(1, 1 << (top - low))
        ]
        held = jnp.concatenate(parts, axis=0)
    return held


def bit_groups(devices):
    groups = []
    top = devices.bit_length() - 1
    while top > 1:
        low = max(top - 2, 1)
        groups.append((low, top))
        top = low
    groups.append((0, 1))
    return groups


def place_mask(devices, place):
    mask = 0
    for low, top in bit_groups(devices):
        width = top - low
        mask = mask | ((place & ((1 << width) - 1)) << low)
        place = place >> width
    return mask


def local(devices, *args):
    (
        images,
        image_sizes,
        out_grad,
        weight_one,
        first_one,
        second_one,
        weight_two,
        first_two,
        second_two,
        weight_three,
        first_three,
        second_three,
        weight_four,
        first_four,
        second_four,
        biases,
        first_bias,
        second_bias,
    ) = args
    weights = (weight_one, weight_two, weight_three, weight_four)
    moments = (
        (first_one, second_one),
        (first_two, second_two),
        (first_three, second_three),
        (first_four, second_four),
    )
    rates = ((9.0 * C) ** (-0.5), (9.0 * HID) ** (-0.5), (9.0 * HID) ** (-0.5), 8.0)
    sizes = [weight.shape[0] for weight in weights]
    total = sum(sizes)
    packed = all(size % 128 == 0 for size in sizes) and sizes[3] % 256 == 0 and devices & (devices - 1) == 0
    low = jnp.concatenate([weight.astype(BF16) for weight in weights])
    me = lax.axis_index("dp") * lax.axis_size("fsdp") + lax.axis_index("fsdp")
    if packed:
        shards = devices
        mine = gather_shards(low.reshape(total // 128, 128), devices)
    else:
        shards = 1
        full = lax.all_gather(low, AXES, axis=0, tiled=False)
        parts = []
        at = 0
        for size in sizes:
            parts.append(full[:, at : at + size].reshape(-1))
            at += size
        mine = jnp.concatenate(parts).reshape(1, -1, 128)
    pair = lambda v: jnp.tile(v, C // HID)
    bias_rows = jnp.stack(
        [pair(biases[0:HID]), pair(biases[HID : 2 * HID]), pair(biases[2 * HID : 3 * HID]), biases[3 * HID :]]
        + [jnp.zeros((C,), F32)] * 4
    )
    me_arg = jnp.reshape(me, (1,)).astype(jnp.int32)
    block_out, image_grad, send, bias_part = run_main(
        shards, me_arg, image_sizes, mine, bias_rows, images, out_grad
    )
    if packed:
        moved = lax.all_to_all(send, AXES, 0, 0, tiled=False)
        summed = jnp.sum(moved.astype(F32), axis=0).reshape(-1)
    else:
        flat = send.reshape(-1).astype(F32)
        parts = []
        at = 0
        for size in sizes:
            parts.append(flat[at : at + size * devices].reshape(devices, size))
            at += size * devices
        summed = lax.psum_scatter(
            jnp.concatenate(parts, axis=1).reshape(-1), AXES, scatter_dimension=0, tiled=True
        )
    bias_total = lax.psum(bias_part, AXES)
    updates = []
    at = 0
    for weight, (first, second), rate, size in zip(weights, moments, rates, sizes):
        updates += list(adamw_update(weight, summed[at : at + size], first, second, rate))
        at += size
    bias_rates = jnp.where(jnp.arange(BIASES) < 3 * HID, 0.5, 32.0)
    updates += list(adamw_update(biases, bias_total, first_bias, second_bias, bias_rates))
    return (block_out, image_grad, *updates)


def solution(mesh):
    devices = mesh.shape["dp"] * mesh.shape["fsdp"]
    split = P(AXES)
    return jax.shard_map(
        functools.partial(local, devices),
        mesh=mesh,
        in_specs=(
            P(AXES, None, None, None),
            P(AXES, None),
            P(AXES, None, None, None),
            *([split] * 12),
            P(),
            P(),
            P(),
        ),
        out_specs=(
            P(AXES, None, None, None),
            P(AXES, None, None, None),
            *([split] * 16),
            P(),
            P(),
            P(),
            P(),
        ),
        check_vma=False,
    )
```

time: 491 us -> 102 us (0.21); the launches traced: 485 us -> 101 us
  blocking collectives: 194 us -> 40.7 us
  local copies, waits for them, and re-layouts: 97.3 us -> 5.65 us
  waiting for transfers between devices: 72.3 us -> 7.7 us
  matrix products: 52 us -> 0 us
  other arithmetic: 53.2 us -> 6.2 us
  Pallas kernels: 0 us -> 26.9 us
  between operations: 15.6 us -> 0.91 us
  starting transfers between devices: 0.04 us -> 12.8 us
    all_gather x4 -> x0, blocking collectives: 157 us -> none  [the longest x1 44.8 us: local(): lax.all_gather(low_one, ('dp', 'fsdp'), axis=0, tiled=True)]
    unnamed x2 -> x0, waiting for transfers between devices: 72.3 us -> none
    conv_general_dilated x6 -> x0, matrix products: 29.1 us -> none  [conv_same(): lax.conv_general_dilated(active, kernel, (1, 1), 'SAME', dimension_number...]
    pallas_call x0 -> x1, Pallas kernels: none -> 26.9 us  [run_main(): pl.pallas_call(functools.partial(main_kernel, shards), grid=(count,), in_...]
    convert_element_type x20 -> x8, other arithmetic: 30.2 us -> 5.31 us  [the longest x4 2.81 us: local(): low = jnp.concatenate([weight.astype(BF16) for weight in weights])]
    dot_general x30 -> x0, matrix products: 22.9 us -> none  [the longest x27 17.6 us: tap_grads(): jnp.einsum('nhwc,nhwo->co', window, grad_low, preferred_element_type=jnp....]
    unnamed x147 -> x39, local copies, waits for them, and re-layouts: 23.9 us -> 2.29 us
    slice x5 -> x1, local copies, waits for them, and re-layouts: 19 us -> 0.86 us  [local(): biases[2 * HID:3 * HID]]
  transfers between devices with their start and end apart: 1 -> 8, of which waited for: 1 -> 3; matrix products, arithmetic and copies ran while one was open for 4% -> 6% of each run, Pallas kernels for 0% -> 0%
where the time goes in v1:
time: 102 us; the launch traced here: 101 us
  blocking collectives  40.7 us (40%)
  Pallas kernels  26.9 us (26%)
  starting transfers between devices  12.8 us (13%)
  waiting for transfers between devices  7.7 us (8%)
  other arithmetic  6.2 us (6%)
  local copies, waits for them, and re-layouts  5.65 us (6%)
    psum x1, blocking collectives, local(): bias_total = lax.psum(bias_part, AXES)  40.7 us
    pallas_call x1, Pallas kernels, run_main(): pl.pallas_call(functools.partial(main_kernel, shards), grid=(count,), in_...  26.9 us
    ppermute x7, starting transfers between devices, exchange(): return lax.ppermute(value, AXES, [(i, i ^ mask) for i in range(count)])  9.38 us
    ppermute x7, waiting for transfers between devices, exchange(): return lax.ppermute(value, AXES, [(i, i ^ mask) for i in range(count)])  7.69 us
    all_to_all x1, starting transfers between devices, local(): moved = lax.all_to_all(send, AXES, 0, 0, tiled=False)  3.44 us
    convert_element_type x4, other arithmetic, local(): low = jnp.concatenate([weight.astype(BF16) for weight in weights])  2.81 us
    convert_element_type x4, other arithmetic, adamw_update(): return (first_new, second_new, weight_new, weight_new.astype(BF16))  2.5 us
    unnamed x39, local copies, waits for them, and re-layouts  2.29 us
  transfers between devices with their start and end apart: 8, of which 3 were waited for; matrix products, arithmetic and copies ran while one was open for 6% of the time, Pallas kernels for 0%

profile of v1, /device:TPU:0, one launch (start us, length us, event | category | flops | bytes accessed | tf_op | source)
XLA Modules:
  0.0 100.9 jit_solution(8269246311340259317)
XLA Ops:
  0.7 0.7 convert_element_type.33
  1.3 0.7 convert_element_type.31
  2.0 0.7 convert_element_type.32
  2.7 0.7 convert_element_type.30
  3.5 5.1 %collective-permute-start.2 = (bf16[1,58,128]{2,1,0:T(8,128)(2,1)S(1)}, bf16[1,58,128]{2,1,0:T(8,128)(2,1)S(1)}, u32[]{:S(2)}, u32[]{:S(2)}) collective-permute-start(bf16[1,58,128]{2,1,0:T(8,128)(2,1)S(1)} %get-tuple-element.51), channel_id=1, source_target_pairs={{0,24},{1,25},{2,26},{3,27},{4,28},{5,29},{6,30},{7,31},{8,16},{9,... | collective-permute-start | bytes 44552 | tf_op jit(solution)/shard_map/ppermute | solution.py:439
  8.6 0.0 collective-permute-start.1
  8.6 0.6 collective-permute-start
  9.2 1.1 %collective-permute-done.2 = bf16[1,58,128]{2,1,0:T(8,128)(2,1)S(1)} collective-permute-done((bf16[1,58,128]{2,1,0:T(8,128)(2,1)S(1)}, bf16[1,58,128]{2,1,0:T(8,128)(2,1)S(1)}, u32[]{:S(2)}, u32[]{:S(2)}) %collective-permute-start.2) | collective-permute-done | bytes 14880 | tf_op jit(solution)/shard_map/ppermute | solution.py:439
  10.3 2.9 %collective-permute-done.1 = bf16[1,58,128]{2,1,0:T(8,128)(2,1)S(1)} collective-permute-done((bf16[1,58,128]{2,1,0:T(8,128)(2,1)S(1)}, bf16[1,58,128]{2,1,0:T(8,128)(2,1)S(1)}, u32[]{:S(2)}, u32[]{:S(2)}) %collective-permute-start.1) | collective-permute-done | bytes 14880 | tf_op jit(solution)/shard_map/ppermute | solution.py:439
  13.3 2.5 %collective-permute-start.5 = (bf16[4,58,128]{2,1,0:T(8,128)(2,1)S(1)}, bf16[4,58,128]{2,1,0:T(8,128)(2,1)S(1)}, u32[]{:S(2)}, u32[]{:S(2)}) collective-permute-start(bf16[4,58,128]{2,1,0:T(8,128)(2,1)S(1)} %pad_maximum_fusion), channel_id=1, source_target_pairs={{0,6},{1,7},{2,4},{3,5},{4,2},{5,3},{6,0},{7,1},{8,14},{9,15},{10,... | collective-permute-start | bytes 178184 | tf_op jit(solution)/shard_map/ppermute | solution.py:439
  15.8 0.5 collective-permute-start.4
  16.3 0.5 collective-permute-start.3
  16.9 3.7 %collective-permute-done.3 = bf16[4,58,128]{2,1,0:T(8,128)(2,1)S(1)} collective-permute-done((bf16[4,58,128]{2,1,0:T(8,128)(2,1)S(1)}, bf16[4,58,128]{2,1,0:T(8,128)(2,1)S(1)}, u32[]{:S(2)}, u32[]{:S(2)}) %collective-permute-start.3) | collective-permute-done | bytes 59424 | tf_op jit(solution)/shard_map/ppermute | solution.py:439
  20.6 0.0 collective-permute-done.4
  20.6 0.0 collective-permute-done.5
  20.7 0.1 collective-permute-start.6
  20.8 0.8 slice.51
  21.5 0.9 fusion.15
  22.4 0.1 stack_tile.11
  22.5 0.1 stack_tile.10
  22.5 0.1 stack_tile.9
  22.6 1.3 %copy.40.sizes_ref = s32[4,2]{1,0:T(4,128)} copy(s32[4,2]{0,1:T(2,128)} %param.19) | data formatting | bytes 64 | tf_op args[1]
  24.0 0.6 stack.11.bias_ref
  24.6 0.0 collective-permute-done.6
  24.6 0.8 copy-done
  25.4 0.0 copy-start.14
  25.4 0.0 copy-start.15
  25.5 0.0 copy-start.1
  25.5 0.0 copy-start.4
  25.5 0.0 copy-start.5
  25.5 0.0 copy-start.2
  25.5 0.0 copy-start.3
  25.5 0.0 copy-start.8
  25.5 0.0 copy-start.9
  25.5 0.0 copy-start.10
  25.6 0.0 copy-start.11
  25.6 26.9 %block.1 = (bf16[4,16,16,256]{3,2,1,0:T(8,128)(2,1)}, bf16[4,16,2,32,256]{4,3,2,1,0:T(8,128)(2,1)}, bf16[32,58,128]{2,1,0:T(8,128)(2,1)}, f32[8,384]{1,0:T(8,128)}) custom-call(s32[1]{0:T(128)} %bitcast.me_ref, s32[4,2]{1,0:T(4,128)} %copy.40.sizes_ref, bf16[32,58,128]{2,1,0:T(8,128)(2,1)} %copy-done, f32[8,256]{1,0:T(8,128)} %stack.11.bias_ref, ...), custom_call_target="tpu_custom_call" | custom-call | tf_op jit(solution)/shard_map/block/pallas_call | solution.py:359
  52.5 3.4 %all-to-all-start = ((bf16[32,58,128]{2,1,0:T(8,128)(2,1)}), bf16[32,58,128]{2,1,0:T(8,128)(2,1)S(1)}, u32[]{:S(2)}, u32[]{:S(2)}) async-start(bf16[32,58,128]{2,1,0:T(8,128)(2,1)} %get-tuple-element.28), calls=%async_computation | async-start | bytes 1048576 | tf_op jit(solution)/shard_map/all_to_all | solution.py:528
  55.9 0.8 slice_bitcast_fusion.6
  56.7 0.7 slice_multiply_fusion
  57.4 0.1 pad_maximum_fusion.1
  57.5 40.7 %psum.7 = f32[448]{0:T(512)S(1)} all-reduce(f32[448]{0:T(512)S(1)} %pad_maximum_fusion.1), channel_id=1, replica_groups=mesh['dp'=8,'fsdp'=4] {'dp','fsdp'}, use_global_device_ids=true, to_apply=%region_1.0 | all-reduce | flops 448 | bytes 3584 | tf_op jit(solution)/shard_map/psum | solution.py:540
  98.3 0.6 fusion.5
  98.9 0.0 all-to-all-done
  98.9 0.1 convert_reduce_fusion
  99.0 0.6 fusion.7
  99.6 0.6 fusion.13
  100.3 0.6 fusion.9
  (35 shorter events, 0.2 us)
Async XLA Ops:
  3.5 6.8 %collective-permute-start.2 = (bf16[1,58,128]{2,1,0:T(8,128)(2,1)S(1)}, bf16[1,58,128]{2,1,0:T(8,128)(2,1)S(1)}, u32[]{:S(2)}, u32[]{:S(2)}) collective-permute-start(bf16[1,58,128]{2,1,0:T(8,128)(2,1)S(1)} %get-tuple-element.51), channel_id=1, source_target_pairs={{0,24},{1,25},{2,26},{3,27},{4,28},{5,29},{6,30},{7,31},{8,16},{9,... | collective-permute-start | bytes 44552 | tf_op jit(solution)/shard_map/ppermute | solution.py:439
  8.6 4.6 %collective-permute-start.1 = (bf16[1,58,128]{2,1,0:T(8,128)(2,1)S(1)}, bf16[1,58,128]{2,1,0:T(8,128)(2,1)S(1)}, u32[]{:S(2)}, u32[]{:S(2)}) collective-permute-start(bf16[1,58,128]{2,1,0:T(8,128)(2,1)S(1)} %get-tuple-element.51), channel_id=1, source_target_pairs={{0,16},{1,17},{2,18},{3,19},{4,20},{5,21},{6,22},{7,23},{8,24},{9,... | collective-permute-start | bytes 44552 | tf_op jit(solution)/shard_map/ppermute | solution.py:439
  8.6 4.6 %collective-permute-start = (bf16[1,58,128]{2,1,0:T(8,128)(2,1)S(1)}, bf16[1,58,128]{2,1,0:T(8,128)(2,1)S(1)}, u32[]{:S(2)}, u32[]{:S(2)}) collective-permute-start(bf16[1,58,128]{2,1,0:T(8,128)(2,1)S(1)} %get-tuple-element.51), channel_id=1, source_target_pairs={{0,8},{1,9},{2,10},{3,11},{4,12},{5,13},{6,14},{7,15},{8,0},{9,1},... | collective-permute-start | bytes 44552 | tf_op jit(solution)/shard_map/ppermute | solution.py:439
  13.3 7.4 %collective-permute-start.5 = (bf16[4,58,128]{2,1,0:T(8,128)(2,1)S(1)}, bf16[4,58,128]{2,1,0:T(8,128)(2,1)S(1)}, u32[]{:S(2)}, u32[]{:S(2)}) collective-permute-start(bf16[4,58,128]{2,1,0:T(8,128)(2,1)S(1)} %pad_maximum_fusion), channel_id=1, source_target_pairs={{0,6},{1,7},{2,4},{3,5},{4,2},{5,3},{6,0},{7,1},{8,14},{9,15},{10,... | collective-permute-start | bytes 178184 | tf_op jit(solution)/shard_map/ppermute | solution.py:439
  15.8 4.8 %collective-permute-start.4 = (bf16[4,58,128]{2,1,0:T(8,128)(2,1)S(1)}, bf16[4,58,128]{2,1,0:T(8,128)(2,1)S(1)}, u32[]{:S(2)}, u32[]{:S(2)}) collective-permute-start(bf16[4,58,128]{2,1,0:T(8,128)(2,1)S(1)} %pad_maximum_fusion), channel_id=1, source_target_pairs={{0,4},{1,5},{2,6},{3,7},{4,0},{5,1},{6,2},{7,3},{8,12},{9,13},{10,... | collective-permute-start | bytes 178184 | tf_op jit(solution)/shard_map/ppermute | solution.py:439
  16.3 4.3 %collective-permute-start.3 = (bf16[4,58,128]{2,1,0:T(8,128)(2,1)S(1)}, bf16[4,58,128]{2,1,0:T(8,128)(2,1)S(1)}, u32[]{:S(2)}, u32[]{:S(2)}) collective-permute-start(bf16[4,58,128]{2,1,0:T(8,128)(2,1)S(1)} %pad_maximum_fusion), channel_id=1, source_target_pairs={{0,2},{1,3},{2,0},{3,1},{4,6},{5,7},{6,4},{7,5},{8,10},{9,11},{10,... | collective-permute-start | bytes 178184 | tf_op jit(solution)/shard_map/ppermute | solution.py:439
  20.7 3.9 %collective-permute-start.6 = (bf16[16,58,128]{2,1,0:T(8,128)(2,1)S(1)}, bf16[16,58,128]{2,1,0:T(8,128)(2,1)S(1)}, u32[]{:S(2)}, u32[]{:S(2)}) collective-permute-start(bf16[16,58,128]{2,1,0:T(8,128)(2,1)S(1)} %get-tuple-element.52), channel_id=1, source_target_pairs={{0,1},{1,0},{2,3},{3,2},{4,5},{5,4},{6,7},{7,6},{8,9},{9,8},{10,11... | collective-permute-start | bytes 712712 | tf_op jit(solution)/shard_map/ppermute | solution.py:439
  24.6 0.8 copy-start
  25.4 72.8 %copy-start.6 = (f32[448]{0:T(512)S(1)}, f32[448]{0:T(512)}, u32[]{:S(2)}) copy-start(f32[448]{0:T(512)} %param.33) | copy-start | bytes 5380
  25.4 72.8 %copy-start.12 = (f32[448]{0:T(512)S(1)}, f32[448]{0:T(512)}, u32[]{:S(2)}) copy-start(f32[448]{0:T(512)} %param.35) | copy-start | bytes 5380
  25.4 72.8 %copy-start.13 = (f32[448]{0:T(512)S(1)}, f32[448]{0:T(512)}, u32[]{:S(2)}) copy-start(f32[448]{0:T(512)} %param.34) | copy-start | bytes 5380
  25.4 73.5 %copy-start.7 = (f32[512]{0:T(512)S(1)}, f32[512]{0:T(512)}, u32[]{:S(2)}) copy-start(f32[512]{0:T(512)} %param.30) | copy-start | bytes 6148
  25.4 73.5 %copy-start.14 = (f32[512]{0:T(512)S(1)}, f32[512]{0:T(512)}, u32[]{:S(2)}) copy-start(f32[512]{0:T(512)} %param.32) | copy-start | bytes 6148
  25.4 73.5 %copy-start.15 = (f32[512]{0:T(512)S(1)}, f32[512]{0:T(512)}, u32[]{:S(2)}) copy-start(f32[512]{0:T(512)} %param.31) | copy-start | bytes 6148
  25.5 74.1 %copy-start.1 = (f32[4608]{0:T(1024)S(1)}, f32[4608]{0:T(1024)}, u32[]{:S(2)}) copy-start(f32[4608]{0:T(1024)} %param.21) | copy-start | bytes 55300
  25.5 74.1 %copy-start.4 = (f32[4608]{0:T(1024)S(1)}, f32[4608]{0:T(1024)}, u32[]{:S(2)}) copy-start(f32[4608]{0:T(1024)} %param.23) | copy-start | bytes 55300
  25.5 74.1 %copy-start.5 = (f32[4608]{0:T(1024)S(1)}, f32[4608]{0:T(1024)}, u32[]{:S(2)}) copy-start(f32[4608]{0:T(1024)} %param.22) | copy-start | bytes 55300
  25.5 74.7 %copy-start.2 = (f32[1152]{0:T(1024)S(1)}, f32[1152]{0:T(1024)}, u32[]{:S(2)}) copy-start(f32[1152]{0:T(1024)} %param.27) | copy-start | bytes 13828
  25.5 74.7 %copy-start.3 = (f32[1152]{0:T(1024)S(1)}, f32[1152]{0:T(1024)}, u32[]{:S(2)}) copy-start(f32[1152]{0:T(1024)} %param.24) | copy-start | bytes 13828
  25.5 74.7 %copy-start.8 = (f32[1152]{0:T(1024)S(1)}, f32[1152]{0:T(1024)}, u32[]{:S(2)}) copy-start(f32[1152]{0:T(1024)} %param.29) | copy-start | bytes 13828
  25.5 74.7 %copy-start.9 = (f32[1152]{0:T(1024)S(1)}, f32[1152]{0:T(1024)}, u32[]{:S(2)}) copy-start(f32[1152]{0:T(1024)} %param.28) | copy-start | bytes 13828
  25.5 74.7 %copy-start.10 = (f32[1152]{0:T(1024)S(1)}, f32[1152]{0:T(1024)}, u32[]{:S(2)}) copy-start(f32[1152]{0:T(1024)} %param.26) | copy-start | bytes 13828
  25.6 74.7 %copy-start.11 = (f32[1152]{0:T(1024)S(1)}, f32[1152]{0:T(1024)}, u32[]{:S(2)}) copy-start(f32[1152]{0:T(1024)} %param.25) | copy-start | bytes 13828
  52.5 46.4 %all-to-all-start = ((bf16[32,58,128]{2,1,0:T(8,128)(2,1)}), bf16[32,58,128]{2,1,0:T(8,128)(2,1)S(1)}, u32[]{:S(2)}, u32[]{:S(2)}) async-start(bf16[32,58,128]{2,1,0:T(8,128)(2,1)} %get-tuple-element.28), calls=%async_computation | async-start | bytes 1048576 | tf_op jit(solution)/shard_map/all_to_all | solution.py:528

commit v2 on v1

v2 whole, which is shorter than its diff:
```python
import functools

import jax
import jax.numpy as jnp
from jax import lax
from jax.experimental import pallas as pl
from jax.experimental.pallas import tpu as pltpu
from jax.sharding import PartitionSpec as P

C = 256
HID = 64
STEP = 10
SIDE = 32
HALF = SIDE // 2
ROWS = HALF * SIDE
PAD = SIDE

GAIN = 1.0 / 64.0
BETA_ONE = 0.9
BETA_TWO = 0.999
DECAY = 0.01
EPSILON = 1e-08
AXES = ("dp", "fsdp")
UNROLL = 4

COMPACT = (9 * C * HID // 128, 9 * HID * HID // 128, 9 * HID * HID // 128, HID * C // 128)
BIASES = 3 * HID + C

F32 = jnp.float32
BF16 = jnp.bfloat16


def sigmoid(value):
    return 0.5 * jnp.tanh(0.5 * value) + 0.5


def dot(left, right):
    return jnp.dot(left, right, preferred_element_type=F32)


def dot_rows(left, right):
    return lax.dot_general(left, right, (((0,), (0,)), ((), ())), preferred_element_type=F32)


def swap_halves(value):
    return pltpu.roll(value, HID, 1)


def low_lanes(shape):
    return lax.broadcasted_iota(jnp.int32, shape, 1) < HID


def shard_layout(shards):
    one, two, three, four = (rows // shards for rows in COMPACT)
    first = -(-(one + 4) // 8) * 8
    return 2 * one, first, 2 * two, four


def shard_held(shards):
    _, first, two, four = shard_layout(shards)
    return -(-(first + two + four) // 16) * 16


def pack_kernel(one_ref, two_ref, three_ref, four_ref, out_ref, stage, rows_of_64):
    _, first, two, four = shard_layout(COMPACT[0] // one_ref.shape[0])
    stage[...] = jnp.zeros(stage.shape, F32)

    def spread_rows(ref):
        value = ref[...]
        rows = value.shape[0]
        rows_of_64[pl.ds(0, rows, stride=2), :] = value
        rows_of_64[pl.ds(1, rows, stride=2), :] = swap_halves(value)

    spread_rows(one_ref)
    rest = 2 * one_ref.shape[0] - first
    low = low_lanes((rest, 128))
    stage[0:rest, :] = jnp.where(
        low, rows_of_64[0:rest, :], swap_halves(rows_of_64[first : first + rest, :])
    )
    stage[rest:first, :] = rows_of_64[rest:first, :]
    spread_rows(two_ref)
    value = rows_of_64[0:two, :]
    spread_rows(three_ref)
    stage[first : first + two, :] = jnp.where(
        low_lanes((two, 128)), value, swap_halves(rows_of_64[0:two, :])
    )
    stage[first + two : first + two + four, :] = four_ref[...]
    out_ref[...] = stage[...].astype(BF16)


def run_pack(held, weights):
    return pl.pallas_call(
        pack_kernel,
        out_shape=jax.ShapeDtypeStruct((held, 128), BF16),
        scratch_shapes=[pltpu.VMEM((held, 128), F32), pltpu.VMEM((80, 128), F32)],
        cost_estimate=pl.CostEstimate(flops=8192, bytes_accessed=48 * 1024, transcendentals=0),
        name="pack",
    )(*weights)


def pair_masks(sizes_ref, step):
    height = sizes_ref[step, 0]
    width = sizes_ref[step, 1]
    spot = lax.broadcasted_iota(jnp.int32, (ROWS, 128), 0)
    col = jnp.bitwise_and(spot, SIDE - 1)
    inside = (spot < height * HALF) & (col < width)
    return jnp.where(inside, 1.0, 0.0), col == 0, col == SIDE - 1


def pooled_inside(sizes_ref, step):
    spot = lax.broadcasted_iota(jnp.int32, (HALF * HALF, C), 0)
    return (spot < sizes_ref[step, 0] * (HALF // 2)) & (
        jnp.bitwise_and(spot, HALF - 1) < sizes_ref[step, 1] // 2
    )


def prepare_kernel(
    sizes_ref, bias_ref, img_ref, og_ref, even_ref, odd_ref, spread_ref, bias_rows_ref
):
    step = pl.program_id(0)

    @pl.when(step == 0)
    def biases():
        parts = [bias_ref[:, at : at + 128] for at in (0, 128, 256)]
        last = jnp.concatenate([bias_ref[:, 384:448], jnp.zeros((1, HID), F32)], axis=1)
        parts.append(last)
        turned = [swap_halves(part) for part in parts]
        low = low_lanes((1, 128))
        zero = jnp.zeros((1, 128), F32)
        rows = [
            (jnp.where(low, parts[0], turned[0]), zero),
            (jnp.where(low, turned[0], parts[0]), zero),
            (jnp.where(low, parts[1], turned[1]), zero),
            (jnp.where(low, turned[1], turned[2]), jnp.where(low, turned[2], turned[3])),
        ]
        for row, pair in enumerate(rows):
            bias_rows_ref[row : row + 1, :] = jnp.concatenate(pair, axis=1)
        bias_rows_ref[4:8, :] = jnp.zeros((4, C), F32)

    mask, _, _ = pair_masks(sizes_ref, step)
    wide_mask = jnp.concatenate([mask, mask], axis=1)
    even_ref[0, ROWS : ROWS + PAD, :] = jnp.zeros((PAD, C), BF16)
    odd_ref[0, 0:PAD, :] = jnp.zeros((PAD, C), BF16)
    for parity, act, at in ((0, even_ref, 0), (1, odd_ref, PAD)):
        base = img_ref[0, :, parity].reshape(ROWS, C).astype(F32) * wide_mask
        act[0, at : at + ROWS, :] = (base * sigmoid(base)).astype(BF16)
    pix = lax.broadcasted_iota(jnp.int32, (256, 128), 0)
    spot = lax.broadcasted_iota(jnp.int32, (256, 128), 1)
    spread_up = jnp.where(pix // 2 == spot, 1.0, 0.0).astype(BF16)
    cot = jnp.where(
        pooled_inside(sizes_ref, step), og_ref[0].reshape(HALF * HALF, C).astype(F32), 0.0
    ).astype(BF16)
    for half in range(2):
        value = dot(spread_up, cot[half * 128 : (half + 1) * 128])
        spread_ref[0, half * 256 : (half + 1) * 256, :] = value.astype(BF16)


def block_of(shape):
    rest = (0,) * (len(shape) - 1)
    return pl.BlockSpec(shape, lambda i: (i,) + rest)


def whole(shape):
    return pl.BlockSpec(shape, lambda i: (0,) * len(shape))


def run_prepare(sizes, biases, images, out_grad):
    count = images.shape[0]
    padded = ROWS + PAD
    return pl.pallas_call(
        prepare_kernel,
        grid=(count,),
        in_specs=[
            pl.BlockSpec(memory_space=pltpu.SMEM),
            whole((1, BIASES)),
            block_of((1, HALF, 2, SIDE, C)),
            block_of((1, HALF, HALF, C)),
        ],
        out_specs=[
            block_of((1, padded, C)),
            block_of((1, padded, C)),
            block_of((1, ROWS, C)),
            whole((8, C)),
        ],
        out_shape=[
            jax.ShapeDtypeStruct((count, padded, C), BF16),
            jax.ShapeDtypeStruct((count, padded, C), BF16),
            jax.ShapeDtypeStruct((count, ROWS, C), BF16),
            jax.ShapeDtypeStruct((8, C), F32),
        ],
        compiler_params=pltpu.CompilerParams(
            dimension_semantics=("arbitrary",), vmem_limit_bytes=60 * 1024 * 1024
        ),
        cost_estimate=pl.CostEstimate(
            flops=count * 2 * 512 * 128 * 256, bytes_accessed=count * 1600 * 1024, transcendentals=count * 262144
        ),
        name="prepare",
    )(sizes, biases, images, out_grad)


def unpack_weights(shards, me_ref, pieces, stage, taps_one, taps_two, taps_three, taps_four):
    one, first, two, four = shard_layout(shards)
    held = pieces[0].shape[1]
    for which, piece in enumerate(pieces):
        group = piece.shape[0]
        stage[which * group * held : (which + 1) * group * held, :] = (
            piece[...].reshape(group * held, 128).astype(F32)
        )

    def place(shard, carry):
        owner = me_ref[0] ^ place_mask(shards, shard) if shards > 1 else shard
        start = pl.multiple_of(shard * held, 8)
        value = stage[pl.ds(start, first), :]
        at = pl.multiple_of(owner * one, 8)
        taps_one[pl.ds(at, first), :] = value
        taps_one[pl.ds(at + first, one - first), :] = swap_halves(value[0 : one - first])
        value = stage[pl.ds(start + first, two), :]
        taps_two[pl.ds(owner * two, two), :] = value
        taps_three[pl.ds(owner * two, two), :] = swap_halves(value)
        at = start + first + two
        for row in range(four // 2):
            row_at = owner * (four // 2) + row
            taps_four[0, pl.ds(row_at, 1), :] = stage[pl.ds(at + 2 * row, 1), :]
            taps_four[1, pl.ds(row_at, 1), :] = stage[pl.ds(at + 2 * row + 1, 1), :]
        return carry

    lax.fori_loop(0, shards, place, 0, unroll=UNROLL if shards > 1 else 1)


def tap_blocks(taps, width, col_tap):
    rows = [
        taps[(row_tap * 3 + col_tap) * width : (row_tap * 3 + col_tap + 1) * width, :]
        for row_tap in range(3)
    ]
    low = low_lanes((width, 128))
    zero = jnp.zeros((width, 128), F32)
    turned = [swap_halves(value) for value in rows]
    return (
        jnp.where(low, rows[0], zero),
        jnp.where(low, rows[1], turned[0]),
        jnp.where(low, rows[2], turned[1]),
        jnp.where(low, zero, turned[2]),
    )


def block_kernel(
    shards,
    pieces_count,
    me_ref,
    sizes_ref,
    bias_ref,
    even_ref,
    odd_ref,
    spread_ref,
    *refs,
):
    pieces = refs[:pieces_count]
    (
        send_ref,
        turned_ref,
        act_three_ref,
        back_one_ref,
        fwd_four_ref,
        stage,
        taps_one,
        taps_two,
        taps_three,
        taps_four,
        fwd_one,
        fwd_two,
        back_two,
        fwd_three,
        back_three,
        back_four,
        act_one,
        act_two,
        slope_one,
        slope_two,
        turned,
        sum_even,
        sum_odd,
        sum_two,
        sum_three,
        sum_four,
        sum_bias,
    ) = refs[pieces_count:]
    step = pl.program_id(0)
    steps = pl.num_programs(0)

    @pl.when(step == 0)
    def prepare():
        unpack_weights(
            shards, me_ref, pieces, stage, taps_one, taps_two, taps_three, taps_four
        )
        for col_tap in range(3):
            lanes = slice(col_tap * 128, (col_tap + 1) * 128)
            more = slice(384 + col_tap * 128, 384 + (col_tap + 1) * 128)
            blocks = tap_blocks(taps_one, C, col_tap)
            for place, block in enumerate(blocks):
                fwd_one[place * C : (place + 1) * C, lanes] = block.astype(BF16)
            back_one_ref[lanes, 0:C] = blocks[1].T.astype(BF16)
            back_one_ref[lanes, C : 2 * C] = blocks[2].T.astype(BF16)
            back_one_ref[more, 0:C] = blocks[3].T.astype(BF16)
            back_one_ref[more, C : 2 * C] = blocks[0].T.astype(BF16)
            for taps, fwd, back in (
                (taps_two, fwd_two, back_two),
                (taps_three, fwd_three, back_three),
            ):
                blocks = tap_blocks(taps, HID, col_tap)
                for place, which in enumerate((1, 2, 3, 0)):
                    fwd[place * HID : (place + 1) * HID, lanes] = blocks[which].astype(BF16)
                back[lanes, :] = jnp.concatenate([blocks[1], blocks[2]], axis=0).T.astype(BF16)
                back[more, :] = jnp.concatenate([blocks[3], blocks[0]], axis=0).T.astype(BF16)
        four = jnp.concatenate([taps_four[0], taps_four[1]], axis=1)
        both = jnp.concatenate([four, four], axis=0)
        fwd_four_ref[...] = both.astype(BF16)
        back_four[...] = both.T.astype(BF16)
        for act in (act_one, act_two):
            act[0:PAD, :] = jnp.zeros((PAD, 128), BF16)
            act[PAD + ROWS :, :] = jnp.zeros((PAD, 128), BF16)
        turned[0:PAD, :] = jnp.zeros((PAD, 384), BF16)
        turned[PAD + ROWS :, :] = jnp.zeros((PAD, 384), BF16)
        for total in (sum_even, sum_odd, sum_two, sum_three, sum_four, sum_bias):
            total[...] = jnp.zeros(total.shape, F32)

    mask, first_col, last_col = pair_masks(sizes_ref, step)
    low = low_lanes((ROWS, 128))
    low_wide = jnp.concatenate([low, low, low], axis=1)

    def shift_sum(parts):
        before = jnp.where(first_col, 0.0, pltpu.roll(parts[:, 0:128], 1, 0))
        after = jnp.where(last_col, 0.0, pltpu.roll(parts[:, 256:384], ROWS - 1, 0))
        return before + parts[:, 128:256] + after

    def activate(conv):
        sigma = sigmoid(conv)
        active = conv * sigma
        return active * mask, (sigma + active * (1.0 - sigma)) * mask

    even = even_ref[0, 0:ROWS, :]
    odd = odd_ref[0, PAD : PAD + ROWS, :]
    window = jnp.concatenate(
        [odd_ref[0, 0:ROWS, :], even, odd, even_ref[0, PAD : PAD + ROWS, :]], axis=1
    )
    conv = shift_sum(dot(window, fwd_one[...])) + bias_ref[0:1, 0:128]
    active, slope = activate(conv)
    act_one[PAD : PAD + ROWS, :] = active.astype(BF16)
    slope_one[...] = slope

    def rows_around(act):
        here = act[PAD : PAD + ROWS, :]
        around = jnp.where(low, act[2 * PAD : 2 * PAD + ROWS, :], act[0:ROWS, :])
        return jnp.concatenate([here, around], axis=1)

    conv = shift_sum(dot(rows_around(act_one), fwd_two[...])) + bias_ref[1:2, 0:128]
    active, slope = activate(conv)
    act_two[PAD : PAD + ROWS, :] = active.astype(BF16)
    slope_two[...] = slope
    conv = shift_sum(dot(rows_around(act_two), fwd_three[...])) + bias_ref[2:3, 0:128]
    active, slope_three = activate(conv)
    act_three_ref[0] = active.astype(BF16)

    part = dot_rows(act_three_ref[0], spread_ref[0])
    sum_four[0:HID, :] = sum_four[0:HID, :] + part[0:HID, :]
    sum_four[HID:128, :] = sum_four[HID:128, :] + part[HID:128, :]
    sum_bias[3:4, :] += jnp.sum(spread_ref[0].astype(F32), axis=0, keepdims=True)
    grad = dot(spread_ref[0], back_four[...]) * (GAIN * 0.25) * slope_three

    def turn(grad, row):
        sum_bias[row : row + 1, 0:128] += jnp.sum(grad, axis=0, keepdims=True)
        turned[PAD : PAD + ROWS, 0:128] = jnp.where(
            last_col, 0.0, pltpu.roll(grad, ROWS - 1, 0)
        ).astype(BF16)
        turned[PAD : PAD + ROWS, 128:256] = grad.astype(BF16)
        turned[PAD : PAD + ROWS, 256:384] = jnp.where(
            first_col, 0.0, pltpu.roll(grad, 1, 0)
        ).astype(BF16)
        here = turned[PAD : PAD + ROWS, :]
        around = jnp.where(low_wide, turned[2 * PAD : 2 * PAD + ROWS, :], turned[0:ROWS, :])
        return jnp.concatenate([here, around], axis=1)

    window = turn(grad, 2)
    sum_three[...] += dot_rows(act_two[PAD : PAD + ROWS, :], window)
    grad = dot(window, back_three[...]) * slope_two[...]
    window = turn(grad, 1)
    sum_two[...] += dot_rows(act_one[PAD : PAD + ROWS, :], window)
    grad = dot(window, back_two[...]) * slope_one[...]
    window = turn(grad, 0)
    turned_ref[0] = window
    sum_even[...] += dot_rows(even, window)
    sum_odd[...] += dot_rows(odd, window)

    @pl.when(step == steps - 1)
    def finish():
        for row_even, row_odd, taps, width_in in (
            (sum_even, sum_odd, taps_one, C),
            (sum_two.at[0:HID], sum_two.at[HID:128], taps_two, HID),
            (sum_three.at[0:HID], sum_three.at[HID:128], taps_three, HID),
        ):
            for col_tap in range(3):
                here = slice(col_tap * 128, (col_tap + 1) * 128)
                around = slice(384 + col_tap * 128, 384 + (col_tap + 1) * 128)
                even_here, even_around = row_even[:, here], row_even[:, around]
                odd_here, odd_around = row_odd[:, here], row_odd[:, around]
                for row_tap, value in (
                    (0, swap_halves(even_here) + odd_around),
                    (1, even_here + swap_halves(odd_here)),
                    (2, swap_halves(even_around) + odd_here),
                ):
                    at = (row_tap * 3 + col_tap) * width_in
                    taps[at : at + width_in, :] = value
        last = (sum_four[0:HID, :] + sum_four[HID:128, :]) * (GAIN * 0.25)
        taps_four[0] = last[:, 0:128]
        taps_four[1] = last[:, 128:256]
        sums = sum_bias[...]
        tail = sums[:, 0:128]
        tail = tail + swap_halves(tail)
        outer = sums[3:4, :] * (GAIN * 0.5)
        outer = (outer[:, 0:128], outer[:, 128:256])
        bias_high = jnp.concatenate(
            [
                tail[0:3],
                swap_halves(outer[0]),
                outer[0],
                swap_halves(outer[1]),
                outer[1],
                jnp.zeros((1, 128), F32),
            ],
            axis=0,
        )
        one, first, two, four = shard_layout(shards)
        held = send_ref.shape[1]
        gap = 2 * first - one - 8

        def collect(shard, carry):
            start = pl.multiple_of(shard * held, 8)
            at = pl.multiple_of(shard * one, 8)
            high = [swap_halves(taps_one[pl.ds(at + first, one - first), :])]
            if gap:
                high.append(jnp.zeros((gap, 128), F32))
            stage[pl.ds(start, first), :] = jnp.where(
                low_lanes((first, 128)),
                taps_one[pl.ds(at, first), :],
                jnp.concatenate(high + [bias_high], axis=0),
            )
            stage[pl.ds(start + first, two), :] = jnp.where(
                low_lanes((two, 128)),
                taps_two[pl.ds(shard * two, two), :],
                swap_halves(taps_three[pl.ds(shard * two, two), :]),
            )
            at = start + first + two
            for row in range(four // 2):
                row_at = shard * (four // 2) + row
                stage[pl.ds(at + 2 * row, 1), :] = taps_four[0, pl.ds(row_at, 1), :]
                stage[pl.ds(at + 2 * row + 1, 1), :] = taps_four[1, pl.ds(row_at, 1), :]
            return carry

        lax.fori_loop(0, shards, collect, 0, unroll=UNROLL if shards > 1 else 1)
        send_ref[...] = stage[...].reshape(shards, held, 128).astype(BF16)


def run_block(shards, me, sizes, bias_rows, even, odd, spread, pieces):
    count = even.shape[0]
    held = pieces[0].shape[1]
    smem = pl.BlockSpec(memory_space=pltpu.SMEM)
    vmem = pltpu.VMEM
    padded = ROWS + PAD
    return pl.pallas_call(
        functools.partial(block_kernel, shards, len(pieces)),
        grid=(count,),
        in_specs=[
            smem,
            smem,
            whole((8, C)),
            block_of((1, padded, C)),
            block_of((1, padded, C)),
            block_of((1, ROWS, C)),
            *[whole(piece.shape) for piece in pieces],
        ],
        out_specs=[
            whole((shards, held, 128)),
            block_of((1, ROWS, 768)),
            block_of((1, ROWS, 128)),
            whole((768, 2 * C)),
            whole((128, C)),
        ],
        out_shape=[
            jax.ShapeDtypeStruct((shards, held, 128), BF16),
            jax.ShapeDtypeStruct((count, ROWS, 768), BF16),
            jax.ShapeDtypeStruct((count, ROWS, 128), BF16),
            jax.ShapeDtypeStruct((768, 2 * C), BF16),
            jax.ShapeDtypeStruct((128, C), BF16),
        ],
        scratch_shapes=[
            vmem((shards * held, 128), F32),
            vmem((9 * C, 128), F32),
            vmem((9 * HID, 128), F32),
            vmem((9 * HID, 128), F32),
            vmem((2, HID, 128), F32),
            vmem((4 * C, 384), BF16),
            vmem((4 * HID, 384), BF16),
            vmem((768, 128), BF16),
            vmem((4 * HID, 384), BF16),
            vmem((768, 128), BF16),
            vmem((C, 128), BF16),
            vmem((padded + PAD, 128), BF16),
            vmem((padded + PAD, 128), BF16),
            vmem((ROWS, 128), F32),
            vmem((ROWS, 128), F32),
            vmem((padded + PAD, 384), BF16),
            vmem((C, 768), F32),
            vmem((C, 768), F32),
            vmem((128, 768), F32),
            vmem((128, 768), F32),
            vmem((128, C), F32),
            vmem((8, C), F32),
        ],
        compiler_params=pltpu.CompilerParams(
            dimension_semantics=("arbitrary",), vmem_limit_bytes=60 * 1024 * 1024
        ),
        cost_estimate=pl.CostEstimate(
            flops=count * 1_200_000_000, bytes_accessed=count * 2_000_000, transcendentals=count * 196608
        ),
        name="block",
    )(me, sizes, bias_rows, even, odd, spread, *pieces)


def finish_kernel(
    sizes_ref, bias_ref, img_ref, spread_ref, turned_ref, act_ref, back_ref, four_ref, out_ref, grad_ref
):
    step = pl.program_id(0)
    mask, _, _ = pair_masks(sizes_ref, step)
    wide_mask = jnp.concatenate([mask, mask], axis=1)
    spot = lax.broadcasted_iota(jnp.int32, (128, 256), 0)
    pix = lax.broadcasted_iota(jnp.int32, (128, 256), 1)
    pool_down = jnp.where(pix // 2 == spot, 0.25, 0.0).astype(BF16)
    pieces = []
    for half in range(2):
        rows = slice(half * 256, (half + 1) * 256)
        base_mean = dot(pool_down, img_ref[0, :, 0].reshape(ROWS, C)[rows]) + dot(
            pool_down, img_ref[0, :, 1].reshape(ROWS, C)[rows]
        )
        act_mean = dot(pool_down, act_ref[0, rows, :]).astype(BF16)
        pieces.append(base_mean + GAIN * (dot(act_mean, four_ref[...]) + bias_ref[3:4, :]))
    result = jnp.where(pooled_inside(sizes_ref, step), jnp.concatenate(pieces, axis=0), 0.0)
    out_ref[0] = result.reshape(HALF, HALF, C).astype(BF16)
    spread = 0.25 * spread_ref[0].astype(F32)
    back = dot(turned_ref[0], back_ref[...])
    for parity in range(2):
        base = img_ref[0, :, parity].reshape(ROWS, C).astype(F32)
        sigma = sigmoid(base)
        slope = (sigma + base * sigma * (1.0 - sigma)) * wide_mask
        value = spread + back[:, parity * C : (parity + 1) * C] * slope
        grad_ref[0, :, parity] = value.reshape(HALF, SIDE, C).astype(BF16)


def run_finish(sizes, bias_rows, images, spread, turned, act_three, back_one, fwd_four):
    count = images.shape[0]
    return pl.pallas_call(
        finish_kernel,
        grid=(count,),
        in_specs=[
            pl.BlockSpec(memory_space=pltpu.SMEM),
            whole((8, C)),
            block_of((1, HALF, 2, SIDE, C)),
            block_of((1, ROWS, C)),
            block_of((1, ROWS, 768)),
            block_of((1, ROWS, 128)),
            whole((768, 2 * C)),
            whole((128, C)),
        ],
        out_specs=[block_of((1, HALF, HALF, C)), block_of((1, HALF, 2, SIDE, C))],
        out_shape=[
            jax.ShapeDtypeStruct((count, HALF, HALF, C), BF16),
            jax.ShapeDtypeStruct((count, HALF, 2, SIDE, C), BF16),
        ],
        compiler_params=pltpu.CompilerParams(
            dimension_semantics=("arbitrary",), vmem_limit_bytes=60 * 1024 * 1024
        ),
        cost_estimate=pl.CostEstimate(
            flops=count * 450_000_000, bytes_accessed=count * 2_500_000, transcendentals=count * 262144
        ),
        name="finish",
    )(sizes, bias_rows, images, spread, turned, act_three, back_one, fwd_four)


def adamw_update(weight, gradient, first_old, second_old, step_rate):
    first_new = BETA_ONE * first_old + (1.0 - BETA_ONE) * gradient
    second_new = BETA_TWO * second_old + (1.0 - BETA_TWO) * gradient * gradient
    first_hat = first_new / (1.0 - BETA_ONE**STEP)
    second_hat = second_new / (1.0 - BETA_TWO**STEP)
    weight_new = weight - step_rate * (
        first_hat / (jnp.sqrt(second_hat) + EPSILON) + DECAY * weight
    )
    return (first_new, second_new, weight_new, weight_new.astype(BF16))


RATES = ((9.0 * C) ** (-0.5), (9.0 * HID) ** (-0.5), (9.0 * HID) ** (-0.5), 8.0)


def update_kernel(moved_ref, *refs):
    olds, news, total, rows_of_64 = refs[:15], refs[15:35], refs[35], refs[36]
    total[...] = jnp.sum(moved_ref[...].astype(F32), axis=0)
    one, first, two, four = shard_layout(COMPACT[0] // olds[0].shape[0])

    def joined(rows):
        return jnp.where(
            low_lanes((rows, 128)),
            rows_of_64[pl.ds(0, rows, stride=2), :],
            swap_halves(rows_of_64[pl.ds(1, rows, stride=2), :]),
        )

    rows_of_64[0:first, :] = total[0:first, :]
    rows_of_64[first:one, :] = swap_halves(total[0 : one - first, :])
    gradients = [joined(one // 2)]
    rows_of_64[0:two, :] = total[first : first + two, :]
    gradients.append(joined(two // 2))
    rows_of_64[0:two, :] = swap_halves(total[first : first + two, :])
    gradients.append(joined(two // 2))
    gradients.append(total[first + two : first + two + four, :])
    rows = total[first - 8 : first, :]
    turned = swap_halves(rows)
    low = low_lanes((1, 128))
    parts = [jnp.where(low, turned[row : row + 1], rows[row + 1 : row + 2]) for row in (0, 2, 4)]
    parts.append(turned[6:7])
    gradients.append(jnp.concatenate(parts, axis=1)[:, 0:BIASES])
    rate = jnp.where(lax.broadcasted_iota(jnp.int32, (1, BIASES), 1) < 3 * HID, 0.5, 32.0)
    for which, gradient in enumerate(gradients):
        weight, first_old, second_old = (ref[...] for ref in olds[3 * which : 3 * which + 3])
        values = adamw_update(
            weight, gradient, first_old, second_old, rate if which == 4 else RATES[which]
        )
        for ref, value in zip(news[4 * which : 4 * which + 4], values):
            ref[...] = value


def run_update(moved, olds):
    shapes = []
    for which in range(5):
        shape = olds[3 * which].shape
        shapes += [jax.ShapeDtypeStruct(shape, F32)] * 3 + [jax.ShapeDtypeStruct(shape, BF16)]
    return pl.pallas_call(
        update_kernel,
        out_shape=shapes,
        scratch_shapes=[pltpu.VMEM(moved.shape[1:], F32), pltpu.VMEM((80, 128), F32)],
        cost_estimate=pl.CostEstimate(flops=500_000, bytes_accessed=700_000, transcendentals=8192),
        name="update",
    )(moved, *olds)


def exchange(value, mask, count):
    return lax.ppermute(value, AXES, [(i, i ^ mask) for i in range(count)])


def gather_shards(value, devices, beside):
    groups = bit_groups(devices)
    held = value[None]
    for low, top in groups[:-2]:
        parts = [held] + [
            exchange(held, mask << low, devices) for mask in range(1, 1 << (top - low))
        ]
        if beside is not None:
            parts, beside = lax.optimization_barrier((parts, beside))
        held = jnp.concatenate(parts, axis=0)
    low, top = groups[-2]
    pieces = [held] + [exchange(held, mask << low, devices) for mask in range(1, 1 << (top - low))]
    return pieces + [exchange(piece, 1, devices) for piece in pieces], beside


def bit_groups(devices):
    groups = []
    top = devices.bit_length() - 1
    while top > 1:
        low = max(top - 2, 1)
        groups.append((low, top))
        top = low
    groups.append((0, 1))
    return groups


def place_mask(devices, place):
    mask = 0
    for low, top in bit_groups(devices):
        width = top - low
        mask = mask | ((place & ((1 << width) - 1)) << low)
        place = place >> width
    return mask


def local(devices, *args):
    (
        images,
        image_sizes,
        out_grad,
        weight_one,
        first_one,
        second_one,
        weight_two,
        first_two,
        second_two,
        weight_three,
        first_three,
        second_three,
        weight_four,
        first_four,
        second_four,
        biases,
        first_bias,
        second_bias,
    ) = args
    weights = (weight_one, weight_two, weight_three, weight_four)
    olds = (
        (weight_one, first_one, second_one),
        (weight_two, first_two, second_two),
        (weight_three, first_three, second_three),
        (weight_four, first_four, second_four),
    )
    count = images.shape[0]
    images = images.reshape(count, HALF, 2, SIDE, C)
    sizes = [weight.shape[0] for weight in weights]
    total = sum(sizes)
    packed = (
        all(size % 128 == 0 for size in sizes)
        and sizes[3] % 256 == 0
        and devices >= 8
        and devices & (devices - 1) == 0
    )
    me = lax.axis_index("dp") * lax.axis_size("fsdp") + lax.axis_index("fsdp")
    me = jnp.reshape(me, (1,)).astype(jnp.int32)
    shards = devices if packed else 1
    held = shard_held(shards)
    prepared = run_prepare(image_sizes, biases.reshape(1, BIASES), images, out_grad)
    if packed:
        mine = run_pack(held, [weight.reshape(-1, 128) for weight in weights])
        pieces, prepared = gather_shards(mine, devices, prepared)
    else:
        low = jnp.concatenate([weight.astype(BF16) for weight in weights])
        full = lax.all_gather(low, AXES, axis=0, tiled=False)
        parts = []
        at = 0
        for size in sizes:
            parts.append(full[:, at : at + size].reshape(-1))
            at += size
        one, first, two, four = shard_layout(1)
        rows = parts[0].reshape(one, HID)
        rows = jnp.concatenate(
            [rows[:first], jnp.pad(rows[first:], ((0, 2 * first - one), (0, 0)))], axis=1
        )
        both = jnp.concatenate([part.reshape(two, HID) for part in parts[1:3]], axis=1)
        full = jnp.concatenate([rows, both, parts[3].reshape(four, 128)], axis=0)
        pieces = [jnp.pad(full, ((0, held - full.shape[0]), (0, 0)))[None]]
    even, odd, spread, bias_rows = prepared
    send, turned, act_three, back_one, fwd_four = run_block(
        shards, me, image_sizes, bias_rows, even, odd, spread, pieces
    )
    if packed:
        moved = lax.all_to_all(send, AXES, 0, 0, tiled=False)
    block_out, image_grad = run_finish(
        image_sizes, bias_rows, images, spread, turned, act_three, back_one, fwd_four
    )
    image_grad = image_grad.reshape(count, SIDE, SIDE, C)
    if packed:
        flat = [array.reshape(-1, 128) for three in olds for array in three]
        flat += [array.reshape(1, BIASES) for array in (biases, first_bias, second_bias)]
        updates = [array.reshape(-1) for array in run_update(moved, flat)]
        return (block_out, image_grad, *updates)
    rows = send[0].astype(F32)
    one, first, two, four = shard_layout(1)
    parts = [
        jnp.concatenate([rows[:first, :HID], rows[: one - first, HID:]], axis=0),
        rows[first : first + two, :HID],
        rows[first : first + two, HID:],
        rows[first + two : first + two + four],
    ]
    parts = [part.reshape(devices, -1) for part in parts]
    bias_part = rows[first - 8 : first - 1, HID:].reshape(-1)
    bias_total = lax.psum(bias_part, AXES)
    summed = lax.psum_scatter(
        jnp.concatenate(parts, axis=1).reshape(-1), AXES, scatter_dimension=0, tiled=True
    )
    updates = []
    at = 0
    for (weight, first, second), rate, size in zip(olds, RATES, sizes):
        updates += list(adamw_update(weight, summed[at : at + size], first, second, rate))
        at += size
    bias_rates = jnp.where(jnp.arange(BIASES) < 3 * HID, 0.5, 32.0)
    updates += list(adamw_update(biases, bias_total, first_bias, second_bias, bias_rates))
    return (block_out, image_grad, *updates)


def solution(mesh):
    devices = mesh.shape["dp"] * mesh.shape["fsdp"]
    split = P(AXES)
    return jax.shard_map(
        functools.partial(local, devices),
        mesh=mesh,
        in_specs=(
            P(AXES, None, None, None),
            P(AXES, None),
            P(AXES, None, None, None),
            *([split] * 12),
            P(),
            P(),
            P(),
        ),
        out_specs=(
            P(AXES, None, None, None),
            P(AXES, None, None, None),
            *([split] * 16),
            P(),
            P(),
            P(),
            P(),
        ),
        check_vma=False,
    )
```

time: 102 us -> 69.1 us (0.68)
  blocking collectives: 40.7 us -> 0 us
  Pallas kernels: 26.9 us -> 36.5 us
  waiting for transfers between devices: 7.7 us -> 13.1 us
  other arithmetic: 6.2 us -> 1.25 us
  local copies, waits for them, and re-layouts: 5.65 us -> 2.77 us
  starting transfers between devices: 12.8 us -> 14.1 us
    psum x1 -> x0, blocking collectives: 40.7 us -> none  [local(): bias_total = lax.psum(bias_part, AXES)]
    pallas_call x1 -> x5, Pallas kernels: 26.9 us -> 36.5 us  [the longest x1 20.5 us: run_block(): pl.pallas_call(functools.partial(block_kernel, shards, len(pieces)), grid...]
    all_to_all x1, waiting for transfers between devices: 0.01 us -> 7.99 us  [local(): moved = lax.all_to_all(send, AXES, 0, 0, tiled=False)]
    convert_element_type x8 -> x0, other arithmetic: 5.31 us -> none  [the longest x4 2.81 us: local(): low = jnp.concatenate([weight.astype(BF16) for weight in weights])]
    ppermute x7 -> x10, waiting for transfers between devices: 7.69 us -> 5.16 us  [exchange(): return lax.ppermute(value, AXES, [(i, i ^ mask) for i in range(count)])]
    slice x2 -> x0, local copies, waits for them, and re-layouts: 1.62 us -> none  [the longest x1 0.86 us: local(): biases[2 * HID:3 * HID]]
    all_to_all x1, starting transfers between devices: 3.44 us -> 4.93 us  [local(): moved = lax.all_to_all(send, AXES, 0, 0, tiled=False)]
    pallas_call x0 -> x1, other arithmetic: none -> 1.25 us  [run_update(): pl.pallas_call(update_kernel, out_shape=shapes, scratch_shapes=[pltpu.VME...]
  transfers between devices with their start and end apart: 8 -> 11, of which waited for: 3 -> 6; matrix products, arithmetic and copies ran while one was open for 6% -> 2% of each run, Pallas kernels for 0% -> 18%
where the time goes in v2:
time: 69.1 us; the launch traced here: 68.6 us
  Pallas kernels  36.5 us (53%)
  starting transfers between devices  14.1 us (20%)
  waiting for transfers between devices  13.1 us (19%)
  local copies, waits for them, and re-layouts  2.77 us (4%)
  other arithmetic  1.25 us (2%)
  between operations  0.8 us (1%)
    pallas_call x1, Pallas kernels, run_block(): pl.pallas_call(functools.partial(block_kernel, shards, len(pieces)), grid...  20.5 us
    ppermute x10, starting transfers between devices, exchange(): return lax.ppermute(value, AXES, [(i, i ^ mask) for i in range(count)])  9.19 us
    all_to_all x1, waiting for transfers between devices, local(): moved = lax.all_to_all(send, AXES, 0, 0, tiled=False)  7.99 us
    pallas_call x1, Pallas kernels, run_finish(): pl.pallas_call(finish_kernel, grid=(count,), in_specs=[pl.BlockSpec(memor...  7.56 us
    ppermute x10, waiting for transfers between devices, exchange(): return lax.ppermute(value, AXES, [(i, i ^ mask) for i in range(count)])  5.16 us
    all_to_all x1, starting transfers between devices, local(): moved = lax.all_to_all(send, AXES, 0, 0, tiled=False)  4.93 us
    pallas_call x1, Pallas kernels, run_prepare(): pl.pallas_call(prepare_kernel, grid=(count,), in_specs=[pl.BlockSpec(memo...  4.84 us
    unnamed x24, local copies, waits for them, and re-layouts  2.76 us
  transfers between devices with their start and end apart: 11, of which 6 were waited for; matrix products, arithmetic and copies ran while one was open for 2% of the time, Pallas kernels for 18%

profile of v2, /device:TPU:0, one launch (start us, length us, event | category | flops | bytes accessed | tf_op | source)
XLA Modules:
  0.0 68.6 jit_solution(1116121664844394700)
XLA Ops:
  0.7 1.5 %pack.1 = bf16[64,128]{1,0:T(8,128)(2,1)} custom-call(f32[36,128]{1,0:T(8,128)} %bitcast.40, f32[9,128]{1,0:T(8,128)} %bitcast.46, f32[9,128]{1,0:T(8,128)} %bitcast.48, f32[4,128]{1,0:T(4,128)} %bitcast.58), custom_call_target="tpu_custom_call" | custom-call | flops 8192 | bytes 49152 | tf_op jit(solution)/shard_map/pack/pallas_call | solution.py:92
  2.2 0.0 copy-start.1
  2.2 5.0 %collective-permute-start.2 = (bf16[1,64,128]{2,1,0:T(8,128)(2,1)}, bf16[1,64,128]{2,1,0:T(8,128)(2,1)S(1)}, u32[]{:S(2)}, u32[]{:S(2)}) collective-permute-start(bf16[1,64,128]{2,1,0:T(8,128)(2,1)} %bitcast.42), channel_id=1, source_target_pairs={{0,24},{1,25},{2,26},{3,27},{4,28},{5,29},{6,30},{7,31},{8,16},{9,... | collective-permute-start | bytes 49160 | tf_op jit(solution)/shard_map/ppermute | solution.py:652
  7.2 0.0 collective-permute-start.1
  7.2 0.6 collective-permute-start
  7.8 1.3 %copy.42.sizes_ref = s32[4,2]{1,0:T(4,128)} copy(s32[4,2]{0,1:T(2,128)} %param.19) | data formatting | bytes 64 | tf_op args[1]
  9.1 4.8 %prepare.1 = (bf16[4,544,256]{2,1,0:T(8,128)(2,1)}, bf16[4,544,256]{2,1,0:T(8,128)(2,1)}, bf16[4,512,256]{2,1,0:T(8,128)(2,1)}, f32[8,256]{1,0:T(8,128)}) custom-call(s32[4,2]{1,0:T(4,128)} %copy.42.sizes_ref, f32[1,448]{1,0:T(1,128)} %bitcast.56, bf16[4,16,2,32,256]{4,3,2,1,0:T(8,128)(2,1)} %bitcast.38, bf16[4,16,16,256]{3,2,1,0:T(8,128)(2,1)} %og_ref.1), custom_call_target="tpu_custom_call" | custom-call | flops 134217728 | bytes 6553600 | tf_op jit(solution)/shard_map/prepare/pallas_call | solution.py:170
  14.0 0.0 collective-permute-done.2
  14.0 0.0 collective-permute-done.1
  14.0 0.0 collective-permute-done
  14.0 0.0 copy-done.1
  14.1 0.0 copy-start.2
  14.1 2.7 %collective-permute-start.5 = (bf16[4,64,128]{2,1,0:T(8,128)(2,1)S(1)}, bf16[4,64,128]{2,1,0:T(8,128)(2,1)S(1)}, u32[]{:S(2)}, u32[]{:S(2)}) collective-permute-start(bf16[4,64,128]{2,1,0:T(8,128)(2,1)S(1)} %constant_dynamic-update-slice_fusion.refs_0_), channel_id=1, source_target_pairs={{0,6},{1,7},{2,4},{3,5},{4,2},{5,3},{6,0},{7,1},{8,14},{9,15},{10,... | collective-permute-start | bytes 196616 | tf_op jit(solution)/shard_map/ppermute | solution.py:652
  16.8 0.5 collective-permute-start.4
  17.3 0.3 collective-permute-start.3
  17.6 0.0 collective-permute-start.6
  17.6 1.8 %collective-permute-done.5.refs_3_ = bf16[4,64,128]{2,1,0:T(8,128)(2,1)S(1)} collective-permute-done((bf16[4,64,128]{2,1,0:T(8,128)(2,1)S(1)}, bf16[4,64,128]{2,1,0:T(8,128)(2,1)S(1)}, u32[]{:S(2)}, u32[]{:S(2)}) %collective-permute-start.5) | collective-permute-done | bytes 65568 | tf_op jit(solution)/shard_map/ppermute | solution.py:652
  19.4 0.0 copy-start.3
  19.4 0.0 collective-permute-start.9
  19.4 1.7 %collective-permute-done.4.refs_2_ = bf16[4,64,128]{2,1,0:T(8,128)(2,1)S(1)} collective-permute-done((bf16[4,64,128]{2,1,0:T(8,128)(2,1)S(1)}, bf16[4,64,128]{2,1,0:T(8,128)(2,1)S(1)}, u32[]{:S(2)}, u32[]{:S(2)}) %collective-permute-start.4) | collective-permute-done | bytes 65568 | tf_op jit(solution)/shard_map/ppermute | solution.py:652
  21.1 0.0 copy-start.4
  21.1 0.0 collective-permute-start.8
  21.1 0.5 collective-permute-done.3.refs_1_
  21.6 0.0 copy-start.5
  21.6 0.0 collective-permute-start.7
  21.6 0.0 collective-permute-done.6.refs_4_
  21.6 0.0 copy-start.6
  21.6 0.0 collective-permute-done.9.refs_7_
  21.6 0.0 copy-start.7
  21.6 0.7 %collective-permute-done.8.refs_6_ = bf16[4,64,128]{2,1,0:T(8,128)(2,1)S(1)} collective-permute-done((bf16[4,64,128]{2,1,0:T(8,128)(2,1)S(1)}, bf16[4,64,128]{2,1,0:T(8,128)(2,1)S(1)}, u32[]{:S(2)}, u32[]{:S(2)}) %collective-permute-start.8) | collective-permute-done | bytes 65568 | tf_op jit(solution)/shard_map/ppermute | solution.py:652
  22.3 0.0 copy-start.8
  22.3 0.5 collective-permute-done.7.refs_5_
  22.8 0.0 copy-start.9
  22.8 0.0 copy-done.2
  22.8 0.0 copy-done.3
  22.8 0.0 copy-done.4
  22.8 0.0 copy-done.5
  22.9 0.0 copy-done.6
  22.9 0.0 copy-done.7
  22.9 0.1 copy-done.8
  22.9 0.5 copy-done.9
  23.4 20.5 %block.1 = (bf16[32,64,128]{2,1,0:T(8,128)(2,1)}, bf16[4,512,768]{2,1,0:T(8,128)(2,1)}, bf16[4,512,128]{2,1,0:T(8,128)(2,1)}, bf16[768,512]{1,0:T(8,128)(2,1)}, bf16[128,256]{1,0:T(8,128)(2,1)}) custom-call(s32[1]{0:T(128)} %bitcast.7.me_ref, s32[4,2]{1,0:T(4,128)} %copy.42.sizes_ref, f32[8,256]{1,0:T(8,128)} %get-tuple-element.65.bias_ref, ...), custom_call_target="tpu_custom_call" | custom-call | flops 4800000000 | bytes 8000000 | tf_op jit(solution)/shard_map/block/pallas_call | solution.py:468
  44.0 4.9 %all-to-all-start = ((bf16[32,64,128]{2,1,0:T(8,128)(2,1)}), bf16[32,64,128]{2,1,0:T(8,128)(2,1)S(1)}, u32[]{:S(2)}, u32[]{:S(2)}) async-start(bf16[32,64,128]{2,1,0:T(8,128)(2,1)} %get-tuple-element.79), calls=%async_computation | async-start | bytes 1048576 | tf_op jit(solution)/shard_map/all_to_all | solution.py:757
  48.9 7.6 %finish.1 = (bf16[4,16,16,256]{3,2,1,0:T(8,128)(2,1)}, bf16[4,16,2,32,256]{4,3,2,1,0:T(8,128)(2,1)}) custom-call(s32[4,2]{1,0:T(4,128)} %copy.42.sizes_ref, f32[8,256]{1,0:T(8,128)} %get-tuple-element.65.bias_ref, bf16[4,16,2,32,256]{4,3,2,1,0:T(8,128)(2,1)} %bitcast.39, bf16[4,512,256]{2,1,0:T(8,128)(2,1)} %get-tuple-element.66.spread_ref, ...), custom_call_target="tpu_custom_call" | custom-call | flops 1800000000 | bytes 10000000 | tf_op jit(solution)/shard_map/finish/pallas_call | solution.py:559
  56.5 8.0 %all-to-all-done.moved_ref = bf16[32,64,128]{2,1,0:T(8,128)(2,1)S(1)} async-done(((bf16[32,64,128]{2,1,0:T(8,128)(2,1)}), bf16[32,64,128]{2,1,0:T(8,128)(2,1)S(1)}, u32[]{:S(2)}, u32[]{:S(2)}) %all-to-all-start) | async-done | bytes 524320 | tf_op jit(solution)/shard_map/all_to_all | solution.py:757
  64.5 0.8 %copy-done = bf16[32,64,128]{2,1,0:T(8,128)(2,1)} copy-done((bf16[32,64,128]{2,1,0:T(8,128)(2,1)}, bf16[32,64,128]{2,1,0:T(8,128)(2,1)S(1)}, u32[]{:S(2)}) %copy-start) | copy-done | bytes 524312
  65.3 2.0 %update.1 = (f32[36,128]{1,0:T(8,128)}, f32[36,128]{1,0:T(8,128)}, f32[36,128]{1,0:T(8,128)}, bf16[36,128]{1,0:T(8,128)(2,1)}, f32[9,128]{1,0:T(8,128)}, /*index...) custom-call(bf16[32,64,128]{2,1,0:T(8,128)(2,1)} %copy-done, ...), custom_call_target="tpu_custom_call" | custom-call | flops 500000 | bytes 700000 | tf_op jit(solution)/shard_map/update/pallas_call | solution.py:642
  67.3 1.3 %reduce = bf16[448]{0:T(512)(128)(2,1)} reduce(bf16[1,448]{1,0:T(2,128)(2,1)} %get-tuple-element.99, bf16[]{:T(256)} %constant.14), dimensions={0}, to_apply=%get-tuple-element.99.reduce_sub_computation | reduce | bytes 1794 | tf_op jit(solution)/shard_map/update/pallas_call | solution.py:642
  (5 shorter events, 0.0 us)
Async XLA Ops:
  2.2 11.8 %copy-start.1 = (bf16[64,128]{1,0:T(8,128)(2,1)S(1)}, bf16[64,128]{1,0:T(8,128)(2,1)}, u32[]{:S(2)}) copy-start(bf16[64,128]{1,0:T(8,128)(2,1)} %pack.1) | copy-start | bytes 49156
  2.2 11.8 %collective-permute-start.2 = (bf16[1,64,128]{2,1,0:T(8,128)(2,1)}, bf16[1,64,128]{2,1,0:T(8,128)(2,1)S(1)}, u32[]{:S(2)}, u32[]{:S(2)}) collective-permute-start(bf16[1,64,128]{2,1,0:T(8,128)(2,1)} %bitcast.42), channel_id=1, source_target_pairs={{0,24},{1,25},{2,26},{3,27},{4,28},{5,29},{6,30},{7,31},{8,16},{9,... | collective-permute-start | bytes 49160 | tf_op jit(solution)/shard_map/ppermute | solution.py:652
  7.2 6.8 %collective-permute-start.1 = (bf16[1,64,128]{2,1,0:T(8,128)(2,1)}, bf16[1,64,128]{2,1,0:T(8,128)(2,1)S(1)}, u32[]{:S(2)}, u32[]{:S(2)}) collective-permute-start(bf16[1,64,128]{2,1,0:T(8,128)(2,1)} %bitcast.43), channel_id=1, source_target_pairs={{0,16},{1,17},{2,18},{3,19},{4,20},{5,21},{6,22},{7,23},{8,24},{9,... | collective-permute-start | bytes 49160 | tf_op jit(solution)/shard_map/ppermute | solution.py:652
  7.2 6.8 %collective-permute-start = (bf16[1,64,128]{2,1,0:T(8,128)(2,1)}, bf16[1,64,128]{2,1,0:T(8,128)(2,1)S(1)}, u32[]{:S(2)}, u32[]{:S(2)}) collective-permute-start(bf16[1,64,128]{2,1,0:T(8,128)(2,1)} %bitcast.44), channel_id=1, source_target_pairs={{0,8},{1,9},{2,10},{3,11},{4,12},{5,13},{6,14},{7,15},{8,0},{9,1},... | collective-permute-start | bytes 49160 | tf_op jit(solution)/shard_map/ppermute | solution.py:652
  14.1 8.8 %copy-start.2 = (bf16[4,64,128]{2,1,0:T(8,128)(2,1)}, bf16[4,64,128]{2,1,0:T(8,128)(2,1)S(1)}, u32[]{:S(2)}) copy-start(bf16[4,64,128]{2,1,0:T(8,128)(2,1)S(1)} %constant_dynamic-update-slice_fusion.refs_0_) | copy-start | bytes 196612
  14.1 5.3 %collective-permute-start.5 = (bf16[4,64,128]{2,1,0:T(8,128)(2,1)S(1)}, bf16[4,64,128]{2,1,0:T(8,128)(2,1)S(1)}, u32[]{:S(2)}, u32[]{:S(2)}) collective-permute-start(bf16[4,64,128]{2,1,0:T(8,128)(2,1)S(1)} %constant_dynamic-update-slice_fusion.refs_0_), channel_id=1, source_target_pairs={{0,6},{1,7},{2,4},{3,5},{4,2},{5,3},{6,0},{7,1},{8,14},{9,15},{10,... | collective-permute-start | bytes 196616 | tf_op jit(solution)/shard_map/ppermute | solution.py:652
  16.8 4.3 %collective-permute-start.4 = (bf16[4,64,128]{2,1,0:T(8,128)(2,1)S(1)}, bf16[4,64,128]{2,1,0:T(8,128)(2,1)S(1)}, u32[]{:S(2)}, u32[]{:S(2)}) collective-permute-start(bf16[4,64,128]{2,1,0:T(8,128)(2,1)S(1)} %constant_dynamic-update-slice_fusion.refs_0_), channel_id=1, source_target_pairs={{0,4},{1,5},{2,6},{3,7},{4,0},{5,1},{6,2},{7,3},{8,12},{9,13},{10,... | collective-permute-start | bytes 196616 | tf_op jit(solution)/shard_map/ppermute | solution.py:652
  17.3 4.3 %collective-permute-start.3 = (bf16[4,64,128]{2,1,0:T(8,128)(2,1)S(1)}, bf16[4,64,128]{2,1,0:T(8,128)(2,1)S(1)}, u32[]{:S(2)}, u32[]{:S(2)}) collective-permute-start(bf16[4,64,128]{2,1,0:T(8,128)(2,1)S(1)} %constant_dynamic-update-slice_fusion.refs_0_), channel_id=1, source_target_pairs={{0,2},{1,3},{2,0},{3,1},{4,6},{5,7},{6,4},{7,5},{8,10},{9,11},{10,... | collective-permute-start | bytes 196616 | tf_op jit(solution)/shard_map/ppermute | solution.py:652
  17.6 4.0 %collective-permute-start.6 = (bf16[4,64,128]{2,1,0:T(8,128)(2,1)S(1)}, bf16[4,64,128]{2,1,0:T(8,128)(2,1)S(1)}, u32[]{:S(2)}, u32[]{:S(2)}) collective-permute-start(bf16[4,64,128]{2,1,0:T(8,128)(2,1)S(1)} %constant_dynamic-update-slice_fusion.refs_0_), channel_id=1, source_target_pairs={{0,1},{1,0},{2,3},{3,2},{4,5},{5,4},{6,7},{7,6},{8,9},{9,8},{10,11... | collective-permute-start | bytes 196616 | tf_op jit(solution)/shard_map/ppermute | solution.py:652
  19.4 3.4 %copy-start.3 = (bf16[4,64,128]{2,1,0:T(8,128)(2,1)}, bf16[4,64,128]{2,1,0:T(8,128)(2,1)S(1)}, u32[]{:S(2)}) copy-start(bf16[4,64,128]{2,1,0:T(8,128)(2,1)S(1)} %collective-permute-done.5.refs_3_) | copy-start | bytes 196612
  19.4 2.2 %collective-permute-start.9 = (bf16[4,64,128]{2,1,0:T(8,128)(2,1)S(1)}, bf16[4,64,128]{2,1,0:T(8,128)(2,1)S(1)}, u32[]{:S(2)}, u32[]{:S(2)}) collective-permute-start(bf16[4,64,128]{2,1,0:T(8,128)(2,1)S(1)} %collective-permute-done.5.refs_3_), channel_id=1, source_target_pairs={{0,1},{1,0},{2,3},{3,2},{4,5},{5,4},{6,7},{7,6},{8,9},{9,8},{10,11... | collective-permute-start | bytes 196616 | tf_op jit(solution)/shard_map/ppermute | solution.py:652
  21.1 1.8 %copy-start.4 = (bf16[4,64,128]{2,1,0:T(8,128)(2,1)}, bf16[4,64,128]{2,1,0:T(8,128)(2,1)S(1)}, u32[]{:S(2)}) copy-start(bf16[4,64,128]{2,1,0:T(8,128)(2,1)S(1)} %collective-permute-done.4.refs_2_) | copy-start | bytes 196612
  21.1 1.3 %collective-permute-start.8 = (bf16[4,64,128]{2,1,0:T(8,128)(2,1)S(1)}, bf16[4,64,128]{2,1,0:T(8,128)(2,1)S(1)}, u32[]{:S(2)}, u32[]{:S(2)}) collective-permute-start(bf16[4,64,128]{2,1,0:T(8,128)(2,1)S(1)} %collective-permute-done.4.refs_2_), channel_id=1, source_target_pairs={{0,1},{1,0},{2,3},{3,2},{4,5},{5,4},{6,7},{7,6},{8,9},{9,8},{10,11... | collective-permute-start | bytes 196616 | tf_op jit(solution)/shard_map/ppermute | solution.py:652
  21.6 1.3 %copy-start.5 = (bf16[4,64,128]{2,1,0:T(8,128)(2,1)}, bf16[4,64,128]{2,1,0:T(8,128)(2,1)S(1)}, u32[]{:S(2)}) copy-start(bf16[4,64,128]{2,1,0:T(8,128)(2,1)S(1)} %collective-permute-done.3.refs_1_) | copy-start | bytes 196612
  21.6 1.3 %collective-permute-start.7 = (bf16[4,64,128]{2,1,0:T(8,128)(2,1)S(1)}, bf16[4,64,128]{2,1,0:T(8,128)(2,1)S(1)}, u32[]{:S(2)}, u32[]{:S(2)}) collective-permute-start(bf16[4,64,128]{2,1,0:T(8,128)(2,1)S(1)} %collective-permute-done.3.refs_1_), channel_id=1, source_target_pairs={{0,1},{1,0},{2,3},{3,2},{4,5},{5,4},{6,7},{7,6},{8,9},{9,8},{10,11... | collective-permute-start | bytes 196616 | tf_op jit(solution)/shard_map/ppermute | solution.py:652
  21.6 1.3 %copy-start.6 = (bf16[4,64,128]{2,1,0:T(8,128)(2,1)}, bf16[4,64,128]{2,1,0:T(8,128)(2,1)S(1)}, u32[]{:S(2)}) copy-start(bf16[4,64,128]{2,1,0:T(8,128)(2,1)S(1)} %collective-permute-done.6.refs_4_) | copy-start | bytes 196612
  21.6 1.3 %copy-start.7 = (bf16[4,64,128]{2,1,0:T(8,128)(2,1)}, bf16[4,64,128]{2,1,0:T(8,128)(2,1)S(1)}, u32[]{:S(2)}) copy-start(bf16[4,64,128]{2,1,0:T(8,128)(2,1)S(1)} %collective-permute-done.9.refs_7_) | copy-start | bytes 196612
  22.3 0.6 copy-start.8
  22.8 0.6 copy-start.9
  44.0 20.5 %all-to-all-start = ((bf16[32,64,128]{2,1,0:T(8,128)(2,1)}), bf16[32,64,128]{2,1,0:T(8,128)(2,1)S(1)}, u32[]{:S(2)}, u32[]{:S(2)}) async-start(bf16[32,64,128]{2,1,0:T(8,128)(2,1)} %get-tuple-element.79), calls=%async_computation | async-start | bytes 1048576 | tf_op jit(solution)/shard_map/all_to_all | solution.py:757
  64.5 0.8 %copy-start = (bf16[32,64,128]{2,1,0:T(8,128)(2,1)}, bf16[32,64,128]{2,1,0:T(8,128)(2,1)S(1)}, u32[]{:S(2)}) copy-start(bf16[32,64,128]{2,1,0:T(8,128)(2,1)S(1)} %all-to-all-done.moved_ref) | copy-start | bytes 1572868

commit v3 on v2

v3 whole, which is shorter than its diff:
```python
import functools

import jax
import jax.numpy as jnp
from jax import lax
from jax.experimental import pallas as pl
from jax.experimental.pallas import tpu as pltpu
from jax.sharding import PartitionSpec as P

C = 256
HID = 64
STEP = 10
SIDE = 32
HALF = SIDE // 2
ROWS = HALF * SIDE
PAD = SIDE

GAIN = 1.0 / 64.0
BETA_ONE = 0.9
BETA_TWO = 0.999
DECAY = 0.01
EPSILON = 1e-08
AXES = ("dp", "fsdp")
UNROLL = 8
UPDATE_MB = 60
SPREAD_BYTES = 58 * 1024 * 1024
ACTIVE_BYTES = 56 * 1024 * 1024
BLOCK_BYTES = 52 * 1024 * 1024
LAG = 1
MERGE = 2
EDGE = 8
KEEP_TYPE = jnp.float32

COMPACT = (9 * C * HID // 128, 9 * HID * HID // 128, 9 * HID * HID // 128, HID * C // 128)
BIASES = 3 * HID + C

F32 = jnp.float32
BF16 = jnp.bfloat16


def silu(value):
    half = 0.5 * value
    return half * (1.0 + jnp.tanh(half))


def silu_and_slope(value):
    half = 0.5 * value
    turn = jnp.tanh(half)
    above = 1.0 + turn
    return half * above, above + half * (1.0 - turn * turn)


def dot(left, right):
    return jnp.dot(left, right, preferred_element_type=F32)


def dot_rows(left, right):
    return lax.dot_general(left, right, (((0,), (0,)), ((), ())), preferred_element_type=F32)


def swap_halves(value):
    return pltpu.roll(value, HID, 1)


def low_lanes(shape):
    return lax.broadcasted_iota(jnp.int32, shape, 1) < HID


def shard_layout(shards):
    one, two, three, four = (rows // shards for rows in COMPACT)
    first = -(-(one + 4) // 8) * 8
    return 2 * one, first, 2 * two, four


def shard_held(shards):
    _, first, two, four = shard_layout(shards)
    return -(-(first + two + four) // 16) * 16


def pack_kernel(one_ref, two_ref, three_ref, four_ref, out_ref, stage, rows_of_64):
    _, first, two, four = shard_layout(COMPACT[0] // one_ref.shape[0])
    stage[...] = jnp.zeros(stage.shape, F32)

    def spread_rows(ref):
        value = ref[...]
        rows = value.shape[0]
        rows_of_64[pl.ds(0, rows, stride=2), :] = value
        rows_of_64[pl.ds(1, rows, stride=2), :] = swap_halves(value)

    spread_rows(one_ref)
    rest = 2 * one_ref.shape[0] - first
    low = low_lanes((rest, 128))
    stage[0:rest, :] = jnp.where(
        low, rows_of_64[0:rest, :], swap_halves(rows_of_64[first : first + rest, :])
    )
    stage[rest:first, :] = rows_of_64[rest:first, :]
    spread_rows(two_ref)
    value = rows_of_64[0:two, :]
    spread_rows(three_ref)
    stage[first : first + two, :] = jnp.where(
        low_lanes((two, 128)), value, swap_halves(rows_of_64[0:two, :])
    )
    stage[first + two : first + two + four, :] = four_ref[...]
    out_ref[...] = stage[...].astype(BF16)


def run_pack(held, weights):
    return pl.pallas_call(
        pack_kernel,
        out_shape=pltpu.VMEM((held, 128), BF16),
        scratch_shapes=[pltpu.VMEM((held, 128), F32), pltpu.VMEM((80, 128), F32)],
        cost_estimate=pl.CostEstimate(flops=8192, bytes_accessed=48 * 1024, transcendentals=0),
        name="pack",
    )(*in_hbm(*weights))


def pair_inside(sizes_ref, image):
    shape = (HALF, SIDE, 128)
    row = lax.broadcasted_iota(jnp.int32, shape, 0)
    col = lax.broadcasted_iota(jnp.int32, shape, 1)
    inside = (row < sizes_ref[0, image] // 2) & (col < sizes_ref[1, image])
    return jnp.where(inside, 1.0, 0.0).reshape(ROWS, 128)


def pooled_inside(sizes_ref, step):
    spot = lax.broadcasted_iota(jnp.int32, (HALF * HALF, C), 0)
    return (spot < sizes_ref[0, step] * (HALF // 2)) & (
        jnp.bitwise_and(spot, HALF - 1) < sizes_ref[1, step] // 2
    )


def spread_kernel(sizes_ref, bias_ref, og_ref, spread_ref, bias_rows_ref):
    parts = [bias_ref[:, at : at + 128] for at in (0, 128, 256)]
    last = jnp.concatenate([bias_ref[:, 384:448], jnp.zeros((1, HID), F32)], axis=1)
    parts.append(last)
    turned = [swap_halves(part) for part in parts]
    low = low_lanes((1, 128))
    zero = jnp.zeros((1, 128), F32)
    rows = [
        (jnp.where(low, parts[0], turned[0]), zero),
        (jnp.where(low, turned[0], parts[0]), zero),
        (jnp.where(low, parts[1], turned[1]), zero),
        (jnp.where(low, turned[1], turned[2]), jnp.where(low, turned[2], turned[3])),
    ]
    for row, pair in enumerate(rows):
        bias_rows_ref[row : row + 1, :] = jnp.concatenate(pair, axis=1)
    total = jnp.zeros((1, C), F32)
    pix = lax.broadcasted_iota(jnp.int32, (256, 128), 0)
    spot = lax.broadcasted_iota(jnp.int32, (256, 128), 1)
    spread_up = jnp.where(pix // 2 == spot, 1.0, 0.0).astype(BF16)
    for image in range(og_ref.shape[0]):
        cot = jnp.where(
            pooled_inside(sizes_ref, image),
            og_ref[image].reshape(HALF * HALF, C).astype(F32),
            0.0,
        )
        total = total + jnp.sum(cot, axis=0, keepdims=True)
        cot = cot.astype(BF16)
        for half in range(2):
            value = dot(spread_up, cot[half * 128 : (half + 1) * 128])
            spread_ref[image, half * 256 : (half + 1) * 256, :] = value.astype(BF16)
    bias_rows_ref[4:8, :] = jnp.concatenate([total * GAIN, jnp.zeros((3, C), F32)], axis=0)


def active_kernel(sizes_ref, img_ref, even_ref, odd_ref):
    step = pl.program_id(0)
    mask = pair_inside(sizes_ref, step)
    wide_mask = jnp.concatenate([mask, mask], axis=1)
    even_ref[step, ROWS : ROWS + PAD, :] = jnp.zeros((PAD, C), BF16)
    odd_ref[step, 0:PAD, :] = jnp.zeros((PAD, C), BF16)
    for parity, act, at in ((0, even_ref, 0), (1, odd_ref, PAD)):
        base = img_ref[0, :, parity].reshape(ROWS, C).astype(F32)
        act[step, at : at + ROWS, :] = (silu(base) * wide_mask).astype(BF16)


def in_vmem(*arrays):
    return [pltpu.with_memory_space_constraint(array, pltpu.VMEM) for array in arrays]


def in_hbm(*arrays):
    return [pltpu.with_memory_space_constraint(array, pltpu.HBM) for array in arrays]


def block_of(shape):
    rest = (0,) * (len(shape) - 1)
    return pl.BlockSpec(shape, lambda i: (i,) + rest)


def whole(shape):
    return pl.BlockSpec(shape, lambda i: (0,) * len(shape))


def run_spread(sizes, biases, out_grad):
    count = out_grad.shape[0]
    vmem = pl.BlockSpec(memory_space=pltpu.VMEM)
    return pl.pallas_call(
        spread_kernel,
        in_specs=[pl.BlockSpec(memory_space=pltpu.SMEM), vmem, vmem],
        out_specs=[vmem, vmem],
        out_shape=[
            pltpu.VMEM((count, ROWS, C), BF16),
            pltpu.VMEM((8, C), F32),
        ],
        compiler_params=pltpu.CompilerParams(vmem_limit_bytes=SPREAD_BYTES),
        cost_estimate=pl.CostEstimate(
            flops=count * 2 * 512 * 128 * 256, bytes_accessed=count * 400_000, transcendentals=0
        ),
        name="spread",
    )(sizes, *in_hbm(biases, out_grad))


def run_active(sizes, images):
    count = images.shape[0]
    padded = ROWS + PAD
    return pl.pallas_call(
        active_kernel,
        grid=(count,),
        in_specs=[
            pl.BlockSpec(memory_space=pltpu.SMEM),
            block_of((1, HALF, 2, SIDE, C)),
        ],
        out_specs=[pl.BlockSpec(memory_space=pltpu.VMEM)] * 2,
        out_shape=[
            pltpu.VMEM((count, padded, C), BF16),
            pltpu.VMEM((count, padded, C), BF16),
        ],
        compiler_params=pltpu.CompilerParams(
            dimension_semantics=("arbitrary",), vmem_limit_bytes=ACTIVE_BYTES
        ),
        cost_estimate=pl.CostEstimate(
            flops=count * 3_000_000, bytes_accessed=count * 1_100_000, transcendentals=count * 262144
        ),
        name="active",
    )(sizes, *in_hbm(images))


def unpack_weights(shards, me_ref, pieces, stage, taps_one, taps_two, taps_three, taps_four):
    one, first, two, four = shard_layout(shards)
    held = pieces[0].shape[1]
    for which, piece in enumerate(pieces):
        group = piece.shape[0]
        stage[which * group * held : (which + 1) * group * held, :] = (
            piece[...].reshape(group * held, 128).astype(F32)
        )

    def place(shard, carry):
        owner = me_ref[0] ^ place_mask(shards, shard) if shards > 1 else shard
        start = pl.multiple_of(shard * held, 8)
        value = stage[pl.ds(start, first), :]
        at = pl.multiple_of(owner * one, 8)
        taps_one[pl.ds(at, first), :] = value
        taps_one[pl.ds(at + first, one - first), :] = swap_halves(value[0 : one - first])
        value = stage[pl.ds(start + first, two), :]
        taps_two[pl.ds(owner * two, two), :] = value
        taps_three[pl.ds(owner * two, two), :] = swap_halves(value)
        at = start + first + two
        for row in range(four // 2):
            row_at = owner * (four // 2) + row
            taps_four[0, pl.ds(row_at, 1), :] = stage[pl.ds(at + 2 * row, 1), :]
            taps_four[1, pl.ds(row_at, 1), :] = stage[pl.ds(at + 2 * row + 1, 1), :]
        return carry

    lax.fori_loop(0, shards, place, 0, unroll=UNROLL if shards > 1 else 1)


def tap_blocks(taps, width, col_tap):
    rows = [
        taps[(row_tap * 3 + col_tap) * width : (row_tap * 3 + col_tap + 1) * width, :]
        for row_tap in range(3)
    ]
    low = low_lanes((width, 128))
    zero = jnp.zeros((width, 128), F32)
    turned = [swap_halves(value) for value in rows]
    return (
        jnp.where(low, rows[0], zero),
        jnp.where(low, rows[1], turned[0]),
        jnp.where(low, rows[2], turned[1]),
        jnp.where(low, zero, turned[2]),
    )


def block_kernel(
    shards,
    me_ref,
    sizes_ref,
    bias_ref,
    even_ref,
    odd_ref,
    spread_ref,
    *refs,
):
    outs = 6
    pieces, refs = refs[: len(refs) - BLOCK_SCRATCH - outs], refs[len(refs) - BLOCK_SCRATCH - outs :]
    keep_ref, send_ref, turned_hbm, act_three_hbm, back_one_hbm, fwd_four_ref = refs[:outs]
    (
        turned_ref,
        act_three_ref,
        back_one_ref,
        sems,
        stage,
        taps_one,
        taps_two,
        taps_three,
        taps_four,
        fwd_one,
        fwd_two,
        back_two,
        fwd_three,
        back_three,
        back_four,
        act_one,
        act_two,
        slope_one,
        slope_two,
        turned,
        masks,
        shifts,
        sum_one,
        sum_two,
        sum_three,
        sum_four,
        sum_bias,
    ) = refs[outs:]
    images = even_ref.shape[0]
    for which in range(2 * images):
        none = jnp.zeros((HALF, EDGE, 128), F32)
        shifts[which, :, 0:EDGE, :] = none
        shifts[which, :, EDGE + SIDE : 2 * EDGE + SIDE, :] = none
    stores = []

    def store(source, target):
        copy = pltpu.make_async_copy(source, target, sems.at[len(stores)])
        copy.start()
        stores.append(copy)

    unpack_weights(shards, me_ref, pieces, stage, taps_one, taps_two, taps_three, taps_four)
    for col_tap in range(3):
        lanes = slice(col_tap * 128, (col_tap + 1) * 128)
        more = slice(384 + col_tap * 128, 384 + (col_tap + 1) * 128)
        blocks = tap_blocks(taps_one, C, col_tap)
        for place, block in enumerate(blocks):
            fwd_one[place * C : (place + 1) * C, lanes] = block.astype(BF16)
        back_one_ref[lanes, 0:C] = (0.5 * blocks[1]).T.astype(BF16)
        back_one_ref[lanes, C : 2 * C] = (0.5 * blocks[2]).T.astype(BF16)
        back_one_ref[more, 0:C] = (0.5 * blocks[3]).T.astype(BF16)
        back_one_ref[more, C : 2 * C] = (0.5 * blocks[0]).T.astype(BF16)
        for taps, fwd, back in (
            (taps_two, fwd_two, back_two),
            (taps_three, fwd_three, back_three),
        ):
            blocks = tap_blocks(taps, HID, col_tap)
            for place, which in enumerate((1, 2, 3, 0)):
                fwd[place * HID : (place + 1) * HID, lanes] = blocks[which].astype(BF16)
            here = jnp.concatenate([blocks[1], blocks[2]], axis=0).T
            around = jnp.concatenate([blocks[3], blocks[0]], axis=0).T
            back[lanes, 0:128] = (0.5 * here).astype(BF16)
            back[lanes, 128:256] = (0.5 * around).astype(BF16)
    four = jnp.concatenate([taps_four[0], taps_four[1]], axis=1)
    both = jnp.concatenate([four, four], axis=0)
    fwd_four_ref[...] = both.astype(BF16)
    back_four[...] = (0.5 * both).T.astype(BF16)
    store(back_one_ref, back_one_hbm)

    low = low_lanes((ROWS, 128))
    low_wide = jnp.concatenate([low, low, low], axis=1)

    def rows_before(value):
        return jnp.concatenate([jnp.zeros((PAD, value.shape[1]), value.dtype), value[:-PAD]], axis=0)

    def rows_after(value):
        return jnp.concatenate([value[PAD:], jnp.zeros((PAD, value.shape[1]), value.dtype)], axis=0)

    def add_to(total, value, slot):
        total[...] = value if slot == 0 else total[...] + value

    def image_phases(slot):
        masks[slot] = pair_inside(sizes_ref, slot)
        first, second, around_grad = act_one.at[slot], act_two.at[slot], turned.at[slot]
        left, right = shifts.at[2 * slot], shifts.at[2 * slot + 1]

        def by_rows(value):
            return value.reshape(HALF, SIDE, 128)

        def shift_sum(parts):
            left[:, EDGE : EDGE + SIDE, :] = by_rows(parts[:, 0:128])
            right[:, EDGE : EDGE + SIDE, :] = by_rows(parts[:, 256:384])
            before = left[:, EDGE - 1 : EDGE - 1 + SIDE, :]
            after = right[:, EDGE + 1 : EDGE + 1 + SIDE, :]
            return (before + by_rows(parts[:, 128:256]) + after).reshape(ROWS, 128)

        def activate(conv):
            active, slope = silu_and_slope(conv)
            return (active * masks[slot]).astype(BF16), slope * masks[slot]

        def keep_active(act, active):
            act[:, 0:128] = active
            act[:, 128:256] = jnp.where(low, rows_after(active), rows_before(active))

        def turn(grad, row, into):
            add_to(sum_bias.at[row : row + 1, 0:128], jnp.sum(grad, axis=0, keepdims=True), slot)
            left[:, EDGE : EDGE + SIDE, :] = by_rows(grad)
            parts = (
                left[:, EDGE + 1 : EDGE + 1 + SIDE, :].reshape(ROWS, 128),
                grad,
                left[:, EDGE - 1 : EDGE - 1 + SIDE, :].reshape(ROWS, 128),
            )
            value = jnp.concatenate([part.astype(BF16) for part in parts], axis=1)
            into[:, 0:384] = value
            return value

        def back_through(window, kernel):
            parts = dot(window, kernel)
            around = parts[:, 128:256]
            return parts[:, 0:128], around

        def back_sum(pair):
            here, around = pair
            return here + jnp.where(low, rows_before(around), rows_after(around))

        window = jnp.concatenate(
            [
                odd_ref[slot, 0:ROWS, :],
                even_ref[slot, 0:ROWS, :],
                odd_ref[slot, PAD : PAD + ROWS, :],
                even_ref[slot, PAD : PAD + ROWS, :],
            ],
            axis=1,
        )
        parts = dot(window, fwd_one[...])
        yield
        active, slope = activate(shift_sum(parts) + bias_ref[0:1, 0:128])
        keep_active(first, active)
        slope_one[slot] = slope
        yield
        parts = dot(first[...], fwd_two[...])
        yield
        active, slope = activate(shift_sum(parts) + bias_ref[1:2, 0:128])
        keep_active(second, active)
        slope_two[slot] = slope
        yield
        parts = dot(second[...], fwd_three[...])
        back = dot(spread_ref[slot], back_four[...])
        yield
        active, slope = activate(shift_sum(parts) + bias_ref[2:3, 0:128])
        act_three_ref[slot] = active
        turn(back * (GAIN * 0.25) * slope, 2, around_grad)
        yield
        back = back_through(around_grad[:, 0:384], back_three[...])
        add_to(sum_four, dot_rows(spread_ref[slot], act_three_ref[slot]), slot)
        add_to(sum_three, dot_rows(second[...], around_grad[:, 0:384]), slot)
        store(act_three_ref.at[slot], act_three_hbm.at[slot])
        yield
        turn(back_sum(back) * slope_two[slot], 1, around_grad)
        yield
        back = back_through(around_grad[:, 0:384], back_two[...])
        add_to(sum_two, dot_rows(first[...], around_grad[:, 0:384]), slot)
        yield
        window = turn(back_sum(back) * slope_one[slot], 0, turned_ref.at[slot])
        turned_ref[slot, :, 384:768] = jnp.where(low_wide, rows_after(window), rows_before(window))
        yield
        store(turned_ref.at[slot], turned_hbm.at[slot])
        if slot % MERGE == MERGE - 1 or slot == images - 1:
            first_slot = slot - slot % MERGE
            slots = range(first_slot, slot + 1)
            both = jnp.concatenate(
                [
                    jnp.concatenate(
                        [even_ref[at, 0:ROWS, :], odd_ref[at, PAD : PAD + ROWS, :]], axis=1
                    )
                    for at in slots
                ],
                axis=0,
            )
            window = turned_ref[first_slot : slot + 1].reshape(len(slots) * ROWS, 768)
            add_to(sum_one, dot_rows(both, window), first_slot)

    waiting = [image_phases(slot) for slot in range(images)]
    turn_number = 0
    while waiting:
        for place, phases in enumerate(list(waiting)):
            if turn_number >= LAG * place or len(waiting) < images:
                if next(phases, waiting) is waiting:
                    waiting.remove(phases)
        turn_number += 1

    for col_tap in range(3):
        here = slice(col_tap * 128, (col_tap + 1) * 128)
        around = slice(384 + col_tap * 128, 384 + (col_tap + 1) * 128)
        even_here, even_around = sum_one[0:C, here], sum_one[0:C, around]
        odd_here, odd_around = sum_one[C : 2 * C, here], sum_one[C : 2 * C, around]
        for row_tap, value in (
            (0, swap_halves(even_here) + odd_around),
            (1, even_here + swap_halves(odd_here)),
            (2, swap_halves(even_around) + odd_here),
        ):
            at = (row_tap * 3 + col_tap) * C
            taps_one[at : at + C, :] = value
        for total, taps in ((sum_two, taps_two), (sum_three, taps_three)):
            even_here, odd_here, even_next, odd_before = (
                total[part * HID : (part + 1) * HID, here] for part in range(4)
            )
            for row_tap, value in (
                (0, swap_halves(even_here) + odd_before),
                (1, even_here + swap_halves(odd_here)),
                (2, odd_here + swap_halves(even_next)),
            ):
                at = (row_tap * 3 + col_tap) * HID
                taps[at : at + HID, :] = value
    last = sum_four[...].T * (GAIN * 0.25)
    last = last[0:HID, :] + last[HID:128, :]
    taps_four[0] = last[:, 0:128]
    taps_four[1] = last[:, 128:256]
    sums = sum_bias[...]
    tail = sums[:, 0:128]
    tail = tail + swap_halves(tail)
    outer = bias_ref[4:5, :]
    outer = (outer[:, 0:128], outer[:, 128:256])
    bias_high = jnp.concatenate(
        [
            tail[0:3],
            swap_halves(outer[0]),
            outer[0],
            swap_halves(outer[1]),
            outer[1],
            jnp.zeros((1, 128), F32),
        ],
        axis=0,
    )
    one, first, two, four = shard_layout(shards)
    held = shard_held(shards)
    gap = 2 * first - one - 8

    def collect(place, carry):
        start = pl.multiple_of(place * held, 8)
        shard = place
        if shards > 1:
            half = jnp.bitwise_xor(place // (shards // 2), jnp.bitwise_and(me_ref[0], 1))
            shard = 2 * lax.rem(place, shards // 2) + half
        at = pl.multiple_of(shard * one, 8)
        high = [swap_halves(taps_one[pl.ds(at + first, one - first), :])]
        if gap:
            high.append(jnp.zeros((gap, 128), F32))
        stage[pl.ds(start, first), :] = jnp.where(
            low_lanes((first, 128)),
            taps_one[pl.ds(at, first), :],
            jnp.concatenate(high + [bias_high], axis=0),
        )
        stage[pl.ds(start + first, two), :] = jnp.where(
            low_lanes((two, 128)),
            taps_two[pl.ds(shard * two, two), :],
            swap_halves(taps_three[pl.ds(shard * two, two), :]),
        )
        at = start + first + two
        for row in range(four // 2):
            row_at = shard * (four // 2) + row
            stage[pl.ds(at + 2 * row, 1), :] = taps_four[0, pl.ds(row_at, 1), :]
            stage[pl.ds(at + 2 * row + 1, 1), :] = taps_four[1, pl.ds(row_at, 1), :]
        return carry

    lax.fori_loop(0, shards, collect, 0, unroll=UNROLL if shards > 1 else 1)
    rows = keep_ref.shape[0] * held
    keep_ref[...] = stage[0:rows, :].reshape(keep_ref.shape).astype(keep_ref.dtype)
    send_ref[...] = stage[shards * held - rows :, :].reshape(send_ref.shape).astype(BF16)
    for copy in stores:
        copy.wait()


BLOCK_SCRATCH = 27


def run_block(shards, me, sizes, bias_rows, even, odd, spread, pieces):
    count = even.shape[0]
    held = pieces[0].shape[1]
    part = max(shards // 2, 1)
    smem = pl.BlockSpec(memory_space=pltpu.SMEM)
    hbm = pl.BlockSpec(memory_space=pl.ANY)
    inside = pl.BlockSpec(memory_space=pltpu.VMEM)
    vmem = pltpu.VMEM
    place = pltpu.VMEM if shards > 1 else pltpu.HBM
    return pl.pallas_call(
        functools.partial(block_kernel, shards),
        in_specs=[smem, smem, *[inside] * (4 + len(pieces))],
        out_specs=[inside, inside, hbm, hbm, hbm, inside],
        out_shape=[
            place((part, held, 128), KEEP_TYPE if shards > 1 else F32),
            place((part, held, 128), BF16),
            pltpu.HBM((count, ROWS, 768), BF16),
            pltpu.HBM((count, ROWS, 128), BF16),
            pltpu.HBM((768, 2 * C), BF16),
            pltpu.HBM((128, C), BF16),
        ],
        scratch_shapes=[
            vmem((count, ROWS, 768), BF16),
            vmem((count, ROWS, 128), BF16),
            vmem((768, 2 * C), BF16),
            pltpu.SemaphoreType.DMA((2 * count + 1,)),
            vmem((shards * held, 128), F32),
            vmem((9 * C, 128), F32),
            vmem((9 * HID, 128), F32),
            vmem((9 * HID, 128), F32),
            vmem((2, HID, 128), F32),
            vmem((4 * C, 384), BF16),
            vmem((4 * HID, 384), BF16),
            vmem((384, 256), BF16),
            vmem((4 * HID, 384), BF16),
            vmem((384, 256), BF16),
            vmem((C, 128), BF16),
            vmem((count, ROWS, 256), BF16),
            vmem((count, ROWS, 256), BF16),
            vmem((count, ROWS, 128), F32),
            vmem((count, ROWS, 128), F32),
            vmem((count, ROWS, 384), BF16),
            vmem((count, ROWS, 128), F32),
            vmem((2 * count, HALF, SIDE + 2 * EDGE, 128), F32),
            vmem((2 * C, 768), F32),
            vmem((256, 384), F32),
            vmem((256, 384), F32),
            vmem((C, 128), F32),
            vmem((8, C), F32),
        ],
        compiler_params=pltpu.CompilerParams(vmem_limit_bytes=BLOCK_BYTES),
        cost_estimate=pl.CostEstimate(
            flops=count * 1_200_000_000, bytes_accessed=count * 2_000_000, transcendentals=count * 196608
        ),
        name="block",
    )(me, sizes, *(in_vmem if shards > 1 else in_hbm)(bias_rows, even, odd, spread, *pieces))


def finish_kernel(
    sizes_ref, bias_ref, img_ref, spread_ref, turned_ref, act_ref, back_ref, four_ref, out_ref, grad_ref
):
    step = pl.program_id(0)
    mask = pair_inside(sizes_ref, step)
    wide_mask = jnp.concatenate([mask, mask], axis=1)
    spot = lax.broadcasted_iota(jnp.int32, (128, 256), 0)
    pix = lax.broadcasted_iota(jnp.int32, (128, 256), 1)
    pool_down = jnp.where(pix // 2 == spot, 0.25, 0.0).astype(BF16)
    pieces = []
    for half in range(2):
        rows = slice(half * 256, (half + 1) * 256)
        base_mean = dot(pool_down, img_ref[0, :, 0].reshape(ROWS, C)[rows]) + dot(
            pool_down, img_ref[0, :, 1].reshape(ROWS, C)[rows]
        )
        act_mean = dot(pool_down, act_ref[0, rows, :]).astype(BF16)
        pieces.append(base_mean + GAIN * (dot(act_mean, four_ref[...]) + bias_ref[3:4, :]))
    result = jnp.where(pooled_inside(sizes_ref, step), jnp.concatenate(pieces, axis=0), 0.0)
    out_ref[0] = result.reshape(HALF, HALF, C).astype(BF16)
    spread = 0.25 * spread_ref[0].astype(F32)
    back = dot(turned_ref[0], back_ref[...])
    for parity in range(2):
        _, slope = silu_and_slope(img_ref[0, :, parity].reshape(ROWS, C).astype(F32))
        slope = slope * wide_mask
        value = spread + back[:, parity * C : (parity + 1) * C] * slope
        grad_ref[0, :, parity] = value.reshape(HALF, SIDE, C).astype(BF16)


def run_finish(sizes, bias_rows, images, spread, turned, act_three, back_one, fwd_four):
    count = images.shape[0]
    return pl.pallas_call(
        finish_kernel,
        grid=(count,),
        in_specs=[
            pl.BlockSpec(memory_space=pltpu.SMEM),
            whole((8, C)),
            block_of((1, HALF, 2, SIDE, C)),
            block_of((1, ROWS, C)),
            block_of((1, ROWS, 768)),
            block_of((1, ROWS, 128)),
            whole((768, 2 * C)),
            whole((128, C)),
        ],
        out_specs=[block_of((1, HALF, HALF, C)), block_of((1, HALF, 2, SIDE, C))],
        out_shape=[
            jax.ShapeDtypeStruct((count, HALF, HALF, C), BF16),
            jax.ShapeDtypeStruct((count, HALF, 2, SIDE, C), BF16),
        ],
        compiler_params=pltpu.CompilerParams(
            dimension_semantics=("arbitrary",), vmem_limit_bytes=60 * 1024 * 1024
        ),
        cost_estimate=pl.CostEstimate(
            flops=count * 450_000_000, bytes_accessed=count * 2_500_000, transcendentals=count * 262144
        ),
        name="finish",
    )(sizes, *in_hbm(bias_rows, images, spread, turned, act_three, back_one, fwd_four))


def adamw_update(weight, gradient, first_old, second_old, step_rate):
    first_new = BETA_ONE * first_old + (1.0 - BETA_ONE) * gradient
    second_new = BETA_TWO * second_old + (1.0 - BETA_TWO) * gradient * gradient
    first_hat = first_new / (1.0 - BETA_ONE**STEP)
    second_hat = second_new / (1.0 - BETA_TWO**STEP)
    weight_new = weight - step_rate * (
        first_hat / (jnp.sqrt(second_hat) + EPSILON) + DECAY * weight
    )
    return (first_new, second_new, weight_new, weight_new.astype(BF16))


RATES = ((9.0 * C) ** (-0.5), (9.0 * HID) ** (-0.5), (9.0 * HID) ** (-0.5), 8.0)


def update_kernel(moved_ref, *refs):
    olds, news, total, rows_of_64 = refs[:15], refs[15:35], refs[35], refs[36]
    total[...] = jnp.sum(moved_ref[...].astype(F32), axis=0)
    one, first, two, four = shard_layout(COMPACT[0] // olds[0].shape[0])

    def joined(rows):
        return jnp.where(
            low_lanes((rows, 128)),
            rows_of_64[pl.ds(0, rows, stride=2), :],
            swap_halves(rows_of_64[pl.ds(1, rows, stride=2), :]),
        )

    rows_of_64[0:first, :] = total[0:first, :]
    rows_of_64[first:one, :] = swap_halves(total[0 : one - first, :])
    gradients = [joined(one // 2)]
    rows_of_64[0:two, :] = total[first : first + two, :]
    gradients.append(joined(two // 2))
    rows_of_64[0:two, :] = swap_halves(total[first : first + two, :])
    gradients.append(joined(two // 2))
    gradients.append(total[first + two : first + two + four, :])
    rows = total[first - 8 : first, :]
    turned = swap_halves(rows)
    low = low_lanes((1, 128))
    parts = [jnp.where(low, turned[row : row + 1], rows[row + 1 : row + 2]) for row in (0, 2, 4)]
    parts.append(turned[6:7])
    gradients.append(jnp.concatenate(parts, axis=1)[:, 0:BIASES])
    rate = jnp.where(lax.broadcasted_iota(jnp.int32, (1, BIASES), 1) < 3 * HID, 0.5, 32.0)
    for which, gradient in enumerate(gradients):
        weight, first_old, second_old = (ref[...] for ref in olds[3 * which : 3 * which + 3])
        values = adamw_update(
            weight, gradient, first_old, second_old, rate if which == 4 else RATES[which]
        )
        for ref, value in zip(news[4 * which : 4 * which + 4], values):
            ref[...] = value.reshape(ref.shape)


def run_update(moved, olds):
    shapes = []
    for which in range(5):
        shape = olds[3 * which].shape
        low_shape = shape if which < 4 else shape[1:]
        shapes += [jax.ShapeDtypeStruct(shape, F32)] * 3 + [jax.ShapeDtypeStruct(low_shape, BF16)]
    return pl.pallas_call(
        update_kernel,
        out_shape=shapes,
        scratch_shapes=[pltpu.VMEM(moved.shape[1:], F32), pltpu.VMEM((80, 128), F32)],
        compiler_params=pltpu.CompilerParams(vmem_limit_bytes=UPDATE_MB * 1024 * 1024),
        cost_estimate=pl.CostEstimate(flops=500_000, bytes_accessed=700_000, transcendentals=8192),
        name="update",
    )(*in_vmem(moved), *in_hbm(*olds))


def exchange(value, mask, count):
    return lax.ppermute(value, AXES, [(i, i ^ mask) for i in range(count)])


def gather_shards(value, devices, beside):
    groups = bit_groups(devices)
    early, late = beside
    held = value[None]
    for low, top in groups[:-2]:
        parts = [held] + [
            exchange(held, mask << low, devices) for mask in range(1, 1 << (top - low))
        ]
        parts, early = lax.optimization_barrier((parts, early))
        held = jnp.concatenate(parts, axis=0)
    low, top = groups[-2]
    pieces = [exchange(held, mask << low, devices) for mask in range(1, 1 << (top - low))]
    pieces, late = lax.optimization_barrier((pieces, late))
    pieces = [held] + pieces
    return pieces + [exchange(piece, 1, devices) for piece in pieces], early, late


def bit_groups(devices):
    groups = []
    top = devices.bit_length() - 1
    while top > 1:
        low = max(top - 2, 1)
        groups.append((low, top))
        top = low
    groups.append((0, 1))
    return groups


def place_mask(devices, place):
    mask = 0
    for low, top in bit_groups(devices):
        width = top - low
        mask = mask | ((place & ((1 << width) - 1)) << low)
        place = place >> width
    return mask


def local(devices, *args):
    (
        images,
        image_sizes,
        out_grad,
        weight_one,
        first_one,
        second_one,
        weight_two,
        first_two,
        second_two,
        weight_three,
        first_three,
        second_three,
        weight_four,
        first_four,
        second_four,
        biases,
        first_bias,
        second_bias,
    ) = args
    weights = (weight_one, weight_two, weight_three, weight_four)
    olds = (
        (weight_one, first_one, second_one),
        (weight_two, first_two, second_two),
        (weight_three, first_three, second_three),
        (weight_four, first_four, second_four),
    )
    count = images.shape[0]
    image_sizes = image_sizes.T
    images = images.reshape(count, HALF, 2, SIDE, C)
    sizes = [weight.shape[0] for weight in weights]
    total = sum(sizes)
    packed = (
        all(size % 128 == 0 for size in sizes)
        and sizes[3] % 256 == 0
        and devices >= 8
        and devices & (devices - 1) == 0
    )
    me = lax.axis_index("dp") * lax.axis_size("fsdp") + lax.axis_index("fsdp")
    me = jnp.reshape(me, (1,)).astype(jnp.int32)
    shards = devices if packed else 1
    held = shard_held(shards)
    beside = (
        run_spread(image_sizes, biases.reshape(1, BIASES), out_grad),
        run_active(image_sizes, images),
    )
    if packed:
        mine = run_pack(held, [weight.reshape(-1, 128) for weight in weights])
        pieces, *beside = gather_shards(mine, devices, beside)
    else:
        low = jnp.concatenate([weight.astype(BF16) for weight in weights])
        full = lax.all_gather(low, AXES, axis=0, tiled=False)
        parts = []
        at = 0
        for size in sizes:
            parts.append(full[:, at : at + size].reshape(-1))
            at += size
        one, first, two, four = shard_layout(1)
        rows = parts[0].reshape(one, HID)
        rows = jnp.concatenate(
            [rows[:first], jnp.pad(rows[first:], ((0, 2 * first - one), (0, 0)))], axis=1
        )
        both = jnp.concatenate([part.reshape(two, HID) for part in parts[1:3]], axis=1)
        full = jnp.concatenate([rows, both, parts[3].reshape(four, 128)], axis=0)
        pieces = [jnp.pad(full, ((0, held - full.shape[0]), (0, 0)))[None]]
    (spread, bias_rows), (even, odd) = beside
    keep, send, turned, act_three, back_one, fwd_four = run_block(
        shards, me, image_sizes, bias_rows, even, odd, spread, pieces
    )
    if packed:
        merged = (keep + exchange(send, 1, devices).astype(F32)).astype(BF16)
        merged, turned = lax.optimization_barrier((merged, turned))
        groups = [list(range(core, devices, 2)) for core in range(2)]
        moved = lax.all_to_all(merged, AXES, 0, 0, axis_index_groups=groups, tiled=False)
    block_out, image_grad = run_finish(
        image_sizes, bias_rows, images, spread, turned, act_three, back_one, fwd_four
    )
    image_grad = image_grad.reshape(count, SIDE, SIDE, C)
    if packed:
        flat = [array.reshape(-1, 128) for three in olds for array in three]
        flat += [array.reshape(1, BIASES) for array in (biases, first_bias, second_bias)]
        updates = [array.reshape(-1) for array in run_update(moved, flat)]
        return (block_out, image_grad, *updates)
    rows = keep[0]
    one, first, two, four = shard_layout(1)
    parts = [
        jnp.concatenate([rows[:first, :HID], rows[: one - first, HID:]], axis=0),
        rows[first : first + two, :HID],
        rows[first : first + two, HID:],
        rows[first + two : first + two + four],
    ]
    parts = [part.reshape(devices, -1) for part in parts]
    bias_part = rows[first - 8 : first - 1, HID:].reshape(-1)
    bias_total = lax.psum(bias_part, AXES)
    summed = lax.psum_scatter(
        jnp.concatenate(parts, axis=1).reshape(-1), AXES, scatter_dimension=0, tiled=True
    )
    updates = []
    at = 0
    for (weight, first, second), rate, size in zip(olds, RATES, sizes):
        updates += list(adamw_update(weight, summed[at : at + size], first, second, rate))
        at += size
    bias_rates = jnp.where(jnp.arange(BIASES) < 3 * HID, 0.5, 32.0)
    updates += list(adamw_update(biases, bias_total, first_bias, second_bias, bias_rates))
    return (block_out, image_grad, *updates)


def solution(mesh):
    devices = mesh.shape["dp"] * mesh.shape["fsdp"]
    split = P(AXES)
    return jax.shard_map(
        functools.partial(local, devices),
        mesh=mesh,
        in_specs=(
            P(AXES, None, None, None),
            P(AXES, None),
            P(AXES, None, None, None),
            *([split] * 12),
            P(),
            P(),
            P(),
        ),
        out_specs=(
            P(AXES, None, None, None),
            P(AXES, None, None, None),
            *([split] * 16),
            P(),
            P(),
            P(),
            P(),
        ),
        check_vma=False,
    )
```

time: 69.1 us -> 52.9 us (0.77)
  Pallas kernels: 36.5 us -> 27 us
  waiting for transfers between devices: 13.1 us -> 9.09 us
  local copies, waits for them, and re-layouts: 2.77 us -> 0.04 us
  starting transfers between devices: 14.1 us -> 14.8 us
    pallas_call x3 -> x4, Pallas kernels: 26.9 us -> 18 us  [the longest x1 12.6 us: run_block(): pl.pallas_call(functools.partial(block_kernel, shards), in_specs=[smem, s...]
    all_to_all x1, waiting for transfers between devices: 7.99 us -> 3.11 us  [local(): lax.all_to_all(merged, AXES, 0, 0, axis_index_groups=groups, tiled=False)]
    unnamed x24 -> x7, local copies, waits for them, and re-layouts: 2.76 us -> 0.03 us
    pallas_call x1 -> x0, other arithmetic: 1.25 us -> none  [run_update(): pl.pallas_call(update_kernel, out_shape=shapes, scratch_shapes=[pltpu.VME...]
    ppermute x10 -> x11, starting transfers between devices: 9.19 us -> 10.1 us  [exchange(): return lax.ppermute(value, AXES, [(i, i ^ mask) for i in range(count)])]
    ppermute x10 -> x11, waiting for transfers between devices: 5.16 us -> 5.98 us  [exchange(): return lax.ppermute(value, AXES, [(i, i ^ mask) for i in range(count)])]
    convert_element_type x0 -> x1, other arithmetic: none -> 0.79 us  [local(): merged = (keep + exchange(send, 1, devices).astype(F32)).astype(BF16)]
  transfers between devices with their start and end apart: 11 -> 12, of which waited for: 6 -> 7; matrix products, arithmetic and copies ran while one was open for 2% -> 0% of each run, Pallas kernels for 18% -> 22%
where the time goes in v3:
time: 52.9 us; the launch traced here: 52.4 us
  Pallas kernels  27 us (51%)
  starting transfers between devices  14.8 us (28%)
  waiting for transfers between devices  9.09 us (17%)
  other arithmetic  0.79 us (1%)
  between operations  0.76 us (1%)
    pallas_call x1, Pallas kernels, run_block(): pl.pallas_call(functools.partial(block_kernel, shards), in_specs=[smem, s...  12.6 us
    ppermute x11, starting transfers between devices, exchange(): return lax.ppermute(value, AXES, [(i, i ^ mask) for i in range(count)])  10.1 us
    pallas_call x1, Pallas kernels, run_finish(): pl.pallas_call(finish_kernel, grid=(count,), in_specs=[pl.BlockSpec(memor...  7.28 us
    ppermute x11, waiting for transfers between devices, exchange(): return lax.ppermute(value, AXES, [(i, i ^ mask) for i in range(count)])  5.98 us
    all_to_all x1, starting transfers between devices, local(): lax.all_to_all(merged, AXES, 0, 0, axis_index_groups=groups, tiled=False)  4.66 us
    all_to_all x1, waiting for transfers between devices, local(): lax.all_to_all(merged, AXES, 0, 0, axis_index_groups=groups, tiled=False)  3.11 us
    pallas_call x1, Pallas kernels, run_active(): pl.pallas_call(active_kernel, grid=(count,), in_specs=[pl.BlockSpec(memor...  2.91 us
    pallas_call x1, Pallas kernels, run_update(): pl.pallas_call(update_kernel, out_shape=shapes, scratch_shapes=[pltpu.VME...  1.71 us
  transfers between devices with their start and end apart: 12, of which 7 were waited for; matrix products, arithmetic and copies ran while one was open for 0% of the time, Pallas kernels for 22%

profile of v3, /device:TPU:0, one launch (start us, length us, event | category | flops | bytes accessed | tf_op | source)
XLA Modules:
  0.0 52.4 jit_solution(11384765872208173742)
XLA Ops:
  0.7 0.9 %pack.1 = bf16[64,128]{1,0:T(8,128)(2,1)S(1)} custom-call(f32[36,128]{1,0:T(8,128)} %bitcast.45, f32[9,128]{1,0:T(8,128)} %bitcast.47, f32[9,128]{1,0:T(8,128)} %bitcast.49, f32[4,128]{1,0:T(4,128)} %bitcast.59), custom_call_target="tpu_custom_call" | custom-call | flops 8192 | bytes 49152 | tf_op jit(solution)/shard_map/pack/pallas_call | solution.py:108
  1.6 5.1 %collective-permute-start.2 = (bf16[1,64,128]{2,1,0:T(8,128)(2,1)S(1)}, bf16[1,64,128]{2,1,0:T(8,128)(2,1)S(1)}, u32[]{:S(2)}, u32[]{:S(2)}) collective-permute-start(bf16[1,64,128]{2,1,0:T(8,128)(2,1)S(1)} %bitcast.39), channel_id=1, source_target_pairs={{0,24},{1,25},{2,26},{3,27},{4,28},{5,29},{6,30},{7,31},{8,16},{9,... | collective-permute-start | bytes 49160 | tf_op jit(solution)/shard_map/ppermute | solution.py:754
  6.7 0.0 collective-permute-start.1
  6.7 0.6 %collective-permute-start = (bf16[1,64,128]{2,1,0:T(8,128)(2,1)S(1)}, bf16[1,64,128]{2,1,0:T(8,128)(2,1)S(1)}, u32[]{:S(2)}, u32[]{:S(2)}) collective-permute-start(bf16[1,64,128]{2,1,0:T(8,128)(2,1)S(1)} %bitcast.41), channel_id=1, source_target_pairs={{0,8},{1,9},{2,10},{3,11},{4,12},{5,13},{6,14},{7,15},{8,0},{9,1},... | collective-permute-start | bytes 49160 | tf_op jit(solution)/shard_map/ppermute | solution.py:754
  7.3 1.6 %spread.1 = (bf16[4,512,256]{2,1,0:T(8,128)(2,1)S(1)}, f32[8,256]{1,0:T(8,128)S(1)}) custom-call(s32[2,4]{1,0:T(2,128)} %bitcast.53, f32[1,448]{1,0:T(1,128)} %bitcast.57, bf16[4,16,16,256]{3,2,1,0:T(8,128)(2,1)} %og_ref.1), custom_call_target="tpu_custom_call" | custom-call | flops 134217728 | bytes 1600000 | tf_op jit(solution)/shard_map/spread/pallas_call | solution.py:196
  8.9 0.0 copy-start
  8.9 0.0 copy-start.1
  8.9 0.0 collective-permute-done.2
  8.9 2.4 %collective-permute-done.1 = bf16[1,64,128]{2,1,0:T(8,128)(2,1)S(1)} collective-permute-done((bf16[1,64,128]{2,1,0:T(8,128)(2,1)S(1)}, bf16[1,64,128]{2,1,0:T(8,128)(2,1)S(1)}, u32[]{:S(2)}, u32[]{:S(2)}) %collective-permute-start.1) | collective-permute-done | bytes 16416 | tf_op jit(solution)/shard_map/ppermute | solution.py:754
  11.3 0.0 collective-permute-done
  11.4 2.5 %collective-permute-start.5 = (bf16[4,64,128]{2,1,0:T(8,128)(2,1)S(1)}, bf16[4,64,128]{2,1,0:T(8,128)(2,1)S(1)}, u32[]{:S(2)}, u32[]{:S(2)}) collective-permute-start(bf16[4,64,128]{2,1,0:T(8,128)(2,1)S(1)} %constant_dynamic-update-slice_fusion.refs_0_), channel_id=1, source_target_pairs={{0,6},{1,7},{2,4},{3,5},{4,2},{5,3},{6,0},{7,1},{8,14},{9,15},{10,... | collective-permute-start | bytes 196616 | tf_op jit(solution)/shard_map/ppermute | solution.py:754
  13.9 0.5 collective-permute-start.4
  14.4 0.5 %collective-permute-start.3 = (bf16[4,64,128]{2,1,0:T(8,128)(2,1)S(1)}, bf16[4,64,128]{2,1,0:T(8,128)(2,1)}, u32[]{:S(2)}, u32[]{:S(2)}) collective-permute-start(bf16[4,64,128]{2,1,0:T(8,128)(2,1)S(1)} %constant_dynamic-update-slice_fusion.refs_0_), channel_id=1, source_target_pairs={{0,2},{1,3},{2,0},{3,1},{4,6},{5,7},{6,4},{7,5},{8,10},{9,11},{10,... | collective-permute-start | bytes 196616 | tf_op jit(solution)/shard_map/ppermute | solution.py:754
  14.9 2.9 %active.1 = (bf16[4,544,256]{2,1,0:T(8,128)(2,1)S(1)}, bf16[4,544,256]{2,1,0:T(8,128)(2,1)S(1)}) custom-call(s32[2,4]{1,0:T(2,128)} %bitcast.54, bf16[4,16,2,32,256]{4,3,2,1,0:T(8,128)(2,1)} %bitcast.43), custom_call_target="tpu_custom_call" | custom-call | flops 12000000 | bytes 4400000 | tf_op jit(solution)/shard_map/active/pallas_call | solution.py:215
  17.8 0.1 collective-permute-start.6
  17.9 0.0 collective-permute-done.5.refs_3_
  17.9 0.2 collective-permute-done.4.refs_2_
  18.1 0.6 %collective-permute-done.3.refs_1_ = bf16[4,64,128]{2,1,0:T(8,128)(2,1)} collective-permute-done((bf16[4,64,128]{2,1,0:T(8,128)(2,1)S(1)}, bf16[4,64,128]{2,1,0:T(8,128)(2,1)}, u32[]{:S(2)}, u32[]{:S(2)}) %collective-permute-start.3) | collective-permute-done | bytes 65568 | tf_op jit(solution)/shard_map/ppermute | solution.py:754
  18.8 0.0 collective-permute-start.7
  18.8 0.5 collective-permute-start.8
  19.3 0.0 collective-permute-start.9
  19.3 0.0 collective-permute-done.6.refs_4_
  19.3 1.1 %collective-permute-done.7.refs_5_ = bf16[4,64,128]{2,1,0:T(8,128)(2,1)} collective-permute-done((bf16[4,64,128]{2,1,0:T(8,128)(2,1)}, bf16[4,64,128]{2,1,0:T(8,128)(2,1)}, u32[]{:S(2)}, u32[]{:S(2)}) %collective-permute-start.7) | collective-permute-done | bytes 65568 | tf_op jit(solution)/shard_map/ppermute | solution.py:754
  20.4 0.0 collective-permute-done.8.refs_6_
  20.4 0.2 collective-permute-done.9.refs_7_
  20.6 12.6 %block.1 = (f32[16,64,128]{2,1,0:T(8,128)S(1)}, bf16[16,64,128]{2,1,0:T(8,128)(2,1)S(1)}, bf16[4,512,768]{2,1,0:T(8,128)(2,1)}, bf16[4,512,128]{2,1,0:T(8,128)(2...) custom-call(s32[1]{0:T(128)} %bitcast.8.me_ref, s32[2,4]{1,0:T(2,128)} %bitcast.55, ...), custom_call_target="tpu_custom_call" | custom-call | flops 4800000000 | bytes 8000000 | tf_op jit(solution)/shard_map/block/pallas_call | solution.py:580
  33.2 0.0 copy-done
  33.2 0.0 copy-done.1
  33.3 0.2 collective-permute-start.10
  33.5 1.4 %collective-permute-done.10 = bf16[16,64,128]{2,1,0:T(8,128)(2,1)S(1)} collective-permute-done((bf16[16,64,128]{2,1,0:T(8,128)(2,1)S(1)}, bf16[16,64,128]{2,1,0:T(8,128)(2,1)S(1)}, u32[]{:S(2)}, u32[]{:S(2)}) %collective-permute-start.10) | collective-permute-done | bytes 262176 | tf_op jit(solution)/shard_map/ppermute | solution.py:754
  34.9 0.8 %add_convert_fusion = bf16[16,64,128]{2,1,0:T(8,128)(2,1)} fusion(f32[16,64,128]{2,1,0:T(8,128)S(1)} %get-tuple-element.82, bf16[16,64,128]{2,1,0:T(8,128)(2,1)S(1)} %collective-permute-done.10), kind=kLoop, calls=%fused_computation | loop fusion | flops 393216 | bytes 1048576 | tf_op jit(solution)/shard_map/convert_element_type | solution.py:865
  35.6 4.7 %all-to-all-start = ((bf16[16,64,128]{2,1,0:T(8,128)(2,1)}), bf16[16,64,128]{2,1,0:T(8,128)(2,1)S(1)}, u32[]{:S(2)}, u32[]{:S(2)}) async-start(bf16[16,64,128]{2,1,0:T(8,128)(2,1)} %add_convert_fusion), calls=%async_computation | async-start | bytes 524288 | tf_op jit(solution)/shard_map/all_to_all | solution.py:868
  40.3 7.3 %finish.1 = (bf16[4,16,16,256]{3,2,1,0:T(8,128)(2,1)}, bf16[4,16,2,32,256]{4,3,2,1,0:T(8,128)(2,1)}) custom-call(s32[2,4]{1,0:T(2,128)} %bitcast.56, f32[8,256]{1,0:T(8,128)} %copy-done.1, bf16[4,16,2,32,256]{4,3,2,1,0:T(8,128)(2,1)} %bitcast.44, bf16[4,512,256]{2,1,0:T(8,128)(2,1)} %copy-done, bf16[4,512,768]{2,1,0:T(8,128)(2,1)} %get-tuple-element.85.turned_ref, ...), custom_call_target="tpu_custom_call" | custom-call | flops 1800000000 | bytes 10000000 | tf_op jit(solution)/shard_map/finish/pallas_call | solution.py:659
  47.6 3.1 %all-to-all-done.moved_ref = bf16[16,64,128]{2,1,0:T(8,128)(2,1)S(1)} async-done(((bf16[16,64,128]{2,1,0:T(8,128)(2,1)}), bf16[16,64,128]{2,1,0:T(8,128)(2,1)S(1)}, u32[]{:S(2)}, u32[]{:S(2)}) %all-to-all-start) | async-done | bytes 262176 | tf_op jit(solution)/shard_map/all_to_all | solution.py:868
  50.7 1.7 %update.1 = (f32[36,128]{1,0:T(8,128)}, f32[36,128]{1,0:T(8,128)}, f32[36,128]{1,0:T(8,128)}, bf16[36,128]{1,0:T(8,128)(2,1)}, f32[9,128]{1,0:T(8,128)}, /*index...) custom-call(bf16[16,64,128]{2,1,0:T(8,128)(2,1)S(1)} %all-to-all-don, ...), custom_call_target="tpu_custom_call" | custom-call | flops 500000 | bytes 700000 | tf_op jit(solution)/shard_map/update/pallas_call | solution.py:743
  (4 shorter events, 0.0 us)
Async XLA Ops:
  1.6 7.4 %collective-permute-start.2 = (bf16[1,64,128]{2,1,0:T(8,128)(2,1)S(1)}, bf16[1,64,128]{2,1,0:T(8,128)(2,1)S(1)}, u32[]{:S(2)}, u32[]{:S(2)}) collective-permute-start(bf16[1,64,128]{2,1,0:T(8,128)(2,1)S(1)} %bitcast.39), channel_id=1, source_target_pairs={{0,24},{1,25},{2,26},{3,27},{4,28},{5,29},{6,30},{7,31},{8,16},{9,... | collective-permute-start | bytes 49160 | tf_op jit(solution)/shard_map/ppermute | solution.py:754
  6.7 4.6 %collective-permute-start.1 = (bf16[1,64,128]{2,1,0:T(8,128)(2,1)S(1)}, bf16[1,64,128]{2,1,0:T(8,128)(2,1)S(1)}, u32[]{:S(2)}, u32[]{:S(2)}) collective-permute-start(bf16[1,64,128]{2,1,0:T(8,128)(2,1)S(1)} %bitcast.40), channel_id=1, source_target_pairs={{0,16},{1,17},{2,18},{3,19},{4,20},{5,21},{6,22},{7,23},{8,24},{9,... | collective-permute-start | bytes 49160 | tf_op jit(solution)/shard_map/ppermute | solution.py:754
  6.7 4.6 %collective-permute-start = (bf16[1,64,128]{2,1,0:T(8,128)(2,1)S(1)}, bf16[1,64,128]{2,1,0:T(8,128)(2,1)S(1)}, u32[]{:S(2)}, u32[]{:S(2)}) collective-permute-start(bf16[1,64,128]{2,1,0:T(8,128)(2,1)S(1)} %bitcast.41), channel_id=1, source_target_pairs={{0,8},{1,9},{2,10},{3,11},{4,12},{5,13},{6,14},{7,15},{8,0},{9,1},... | collective-permute-start | bytes 49160 | tf_op jit(solution)/shard_map/ppermute | solution.py:754
  8.9 24.3 %copy-start = (bf16[4,512,256]{2,1,0:T(8,128)(2,1)}, bf16[4,512,256]{2,1,0:T(8,128)(2,1)S(1)}, u32[]{:S(2)}) copy-start(bf16[4,512,256]{2,1,0:T(8,128)(2,1)S(1)} %get-tuple-element.70.spread_ref) | copy-start | bytes 3145732
  8.9 24.3 %copy-start.1 = (f32[8,256]{1,0:T(8,128)}, f32[8,256]{1,0:T(8,128)S(1)}, u32[]{:S(2)}) copy-start(f32[8,256]{1,0:T(8,128)S(1)} %get-tuple-element.69.bias_ref) | copy-start | bytes 24580
  11.4 6.6 %collective-permute-start.5 = (bf16[4,64,128]{2,1,0:T(8,128)(2,1)S(1)}, bf16[4,64,128]{2,1,0:T(8,128)(2,1)S(1)}, u32[]{:S(2)}, u32[]{:S(2)}) collective-permute-start(bf16[4,64,128]{2,1,0:T(8,128)(2,1)S(1)} %constant_dynamic-update-slice_fusion.refs_0_), channel_id=1, source_target_pairs={{0,6},{1,7},{2,4},{3,5},{4,2},{5,3},{6,0},{7,1},{8,14},{9,15},{10,... | collective-permute-start | bytes 196616 | tf_op jit(solution)/shard_map/ppermute | solution.py:754
  13.9 4.3 %collective-permute-start.4 = (bf16[4,64,128]{2,1,0:T(8,128)(2,1)S(1)}, bf16[4,64,128]{2,1,0:T(8,128)(2,1)S(1)}, u32[]{:S(2)}, u32[]{:S(2)}) collective-permute-start(bf16[4,64,128]{2,1,0:T(8,128)(2,1)S(1)} %constant_dynamic-update-slice_fusion.refs_0_), channel_id=1, source_target_pairs={{0,4},{1,5},{2,6},{3,7},{4,0},{5,1},{6,2},{7,3},{8,12},{9,13},{10,... | collective-permute-start | bytes 196616 | tf_op jit(solution)/shard_map/ppermute | solution.py:754
  14.4 4.4 %collective-permute-start.3 = (bf16[4,64,128]{2,1,0:T(8,128)(2,1)S(1)}, bf16[4,64,128]{2,1,0:T(8,128)(2,1)}, u32[]{:S(2)}, u32[]{:S(2)}) collective-permute-start(bf16[4,64,128]{2,1,0:T(8,128)(2,1)S(1)} %constant_dynamic-update-slice_fusion.refs_0_), channel_id=1, source_target_pairs={{0,2},{1,3},{2,0},{3,1},{4,6},{5,7},{6,4},{7,5},{8,10},{9,11},{10,... | collective-permute-start | bytes 196616 | tf_op jit(solution)/shard_map/ppermute | solution.py:754
  17.8 1.5 %collective-permute-start.6 = (bf16[4,64,128]{2,1,0:T(8,128)(2,1)S(1)}, bf16[4,64,128]{2,1,0:T(8,128)(2,1)}, u32[]{:S(2)}, u32[]{:S(2)}) collective-permute-start(bf16[4,64,128]{2,1,0:T(8,128)(2,1)S(1)} %constant_dynamic-update-slice_fusion.refs_0_), channel_id=1, source_target_pairs={{0,1},{1,0},{2,3},{3,2},{4,5},{5,4},{6,7},{7,6},{8,9},{9,8},{10,11... | collective-permute-start | bytes 196616 | tf_op jit(solution)/shard_map/ppermute | solution.py:754
  18.8 1.7 %collective-permute-start.7 = (bf16[4,64,128]{2,1,0:T(8,128)(2,1)}, bf16[4,64,128]{2,1,0:T(8,128)(2,1)}, u32[]{:S(2)}, u32[]{:S(2)}) collective-permute-start(bf16[4,64,128]{2,1,0:T(8,128)(2,1)} %collective-permute-done.3.refs_1_), channel_id=1, source_target_pairs={{0,1},{1,0},{2,3},{3,2},{4,5},{5,4},{6,7},{7,6},{8,9},{9,8},{10,11... | collective-permute-start | bytes 196616 | tf_op jit(solution)/shard_map/ppermute | solution.py:754
  18.8 1.7 %collective-permute-start.8 = (bf16[4,64,128]{2,1,0:T(8,128)(2,1)S(1)}, bf16[4,64,128]{2,1,0:T(8,128)(2,1)}, u32[]{:S(2)}, u32[]{:S(2)}) collective-permute-start(bf16[4,64,128]{2,1,0:T(8,128)(2,1)S(1)} %collective-permute-done.4.refs_2_), channel_id=1, source_target_pairs={{0,1},{1,0},{2,3},{3,2},{4,5},{5,4},{6,7},{7,6},{8,9},{9,8},{10,11... | collective-permute-start | bytes 196616 | tf_op jit(solution)/shard_map/ppermute | solution.py:754
  19.3 1.4 %collective-permute-start.9 = (bf16[4,64,128]{2,1,0:T(8,128)(2,1)S(1)}, bf16[4,64,128]{2,1,0:T(8,128)(2,1)}, u32[]{:S(2)}, u32[]{:S(2)}) collective-permute-start(bf16[4,64,128]{2,1,0:T(8,128)(2,1)S(1)} %collective-permute-done.5.refs_3_), channel_id=1, source_target_pairs={{0,1},{1,0},{2,3},{3,2},{4,5},{5,4},{6,7},{7,6},{8,9},{9,8},{10,11... | collective-permute-start | bytes 196616 | tf_op jit(solution)/shard_map/ppermute | solution.py:754
  33.3 1.6 %collective-permute-start.10 = (bf16[16,64,128]{2,1,0:T(8,128)(2,1)S(1)}, bf16[16,64,128]{2,1,0:T(8,128)(2,1)S(1)}, u32[]{:S(2)}, u32[]{:S(2)}) collective-permute-start(bf16[16,64,128]{2,1,0:T(8,128)(2,1)S(1)} %get-tuple-element.83), channel_id=1, source_target_pairs={{0,1},{1,0},{2,3},{3,2},{4,5},{5,4},{6,7},{7,6},{8,9},{9,8},{10,11... | collective-permute-start | bytes 786440 | tf_op jit(solution)/shard_map/ppermute | solution.py:754
  35.6 15.1 %all-to-all-start = ((bf16[16,64,128]{2,1,0:T(8,128)(2,1)}), bf16[16,64,128]{2,1,0:T(8,128)(2,1)S(1)}, u32[]{:S(2)}, u32[]{:S(2)}) async-start(bf16[16,64,128]{2,1,0:T(8,128)(2,1)} %add_convert_fusion), calls=%async_computation | async-start | bytes 524288 | tf_op jit(solution)/shard_map/all_to_all | solution.py:868

commit v4 on v3

--- a/solution.py
+++ b/solution.py
@@ -21,11 +21,14 @@
 DECAY = 0.01
 EPSILON = 1e-08
 AXES = ("dp", "fsdp")
-UNROLL = 8
-UPDATE_MB = 60
+UNROLL = 16
 SPREAD_BYTES = 58 * 1024 * 1024
 ACTIVE_BYTES = 56 * 1024 * 1024
-BLOCK_BYTES = 52 * 1024 * 1024
+BLOCK_BYTES = 40 * 1024 * 1024
+FINISH_BYTES = 24 * 1024 * 1024
+FOLD_BYTES = 24 * 1024 * 1024
+FINISH_SPLIT = 2
+CHUNK = 64
 LAG = 1
 MERGE = 2
 EDGE = 8
@@ -162,15 +165,14 @@
     bias_rows_ref[4:8, :] = jnp.concatenate([total * GAIN, jnp.zeros((3, C), F32)], axis=0)
 
 
-def active_kernel(sizes_ref, img_ref, even_ref, odd_ref):
+def active_kernel(sizes_ref, img_ref, even_ref, odd_ref, mask_ref):
     step = pl.program_id(0)
     mask = pair_inside(sizes_ref, step)
+    mask_ref[step] = mask
     wide_mask = jnp.concatenate([mask, mask], axis=1)
-    even_ref[step, ROWS : ROWS + PAD, :] = jnp.zeros((PAD, C), BF16)
-    odd_ref[step, 0:PAD, :] = jnp.zeros((PAD, C), BF16)
-    for parity, act, at in ((0, even_ref, 0), (1, odd_ref, PAD)):
+    for parity, act in ((0, even_ref), (1, odd_ref)):
         base = img_ref[0, :, parity].reshape(ROWS, C).astype(F32)
-        act[step, at : at + ROWS, :] = (silu(base) * wide_mask).astype(BF16)
+        act[step] = (silu(base) * wide_mask).astype(BF16)
 
 
 def in_vmem(*arrays):
@@ -211,7 +213,6 @@
 
 def run_active(sizes, images):
     count = images.shape[0]
-    padded = ROWS + PAD
     return pl.pallas_call(
         active_kernel,
         grid=(count,),
@@ -219,10 +220,11 @@
             pl.BlockSpec(memory_space=pltpu.SMEM),
             block_of((1, HALF, 2, SIDE, C)),
         ],
-        out_specs=[pl.BlockSpec(memory_space=pltpu.VMEM)] * 2,
+        out_specs=[pl.BlockSpec(memory_space=pltpu.VMEM)] * 3,
         out_shape=[
-            pltpu.VMEM((count, padded, C), BF16),
-            pltpu.VMEM((count, padded, C), BF16),
+            pltpu.VMEM((count, ROWS, C), BF16),
+            pltpu.VMEM((count, ROWS, C), BF16),
+            pltpu.VMEM((count, ROWS, 128), F32),
         ],
         compiler_params=pltpu.CompilerParams(
             dimension_semantics=("arbitrary",), vmem_limit_bytes=ACTIVE_BYTES
@@ -234,7 +236,7 @@
     )(sizes, *in_hbm(images))
 
 
-def unpack_weights(shards, me_ref, pieces, stage, taps_one, taps_two, taps_three, taps_four):
+def unpack_weights(shards, me, pieces, stage, taps_one, taps_two, taps_three, taps_four):
     one, first, two, four = shard_layout(shards)
     held = pieces[0].shape[1]
     for which, piece in enumerate(pieces):
@@ -244,7 +246,7 @@
         )
 
     def place(shard, carry):
-        owner = me_ref[0] ^ place_mask(shards, shard) if shards > 1 else shard
+        owner = me ^ place_mask(shards, shard) if shards > 1 else shard
         start = pl.multiple_of(shard * held, 8)
         value = stage[pl.ds(start, first), :]
         at = pl.multiple_of(owner * one, 8)
@@ -281,21 +283,22 @@
 
 def block_kernel(
     shards,
-    me_ref,
-    sizes_ref,
+    fetched,
     bias_ref,
     even_ref,
     odd_ref,
+    masks,
     spread_ref,
+    img_hbm,
     *refs,
 ):
-    outs = 6
-    pieces, refs = refs[: len(refs) - BLOCK_SCRATCH - outs], refs[len(refs) - BLOCK_SCRATCH - outs :]
-    keep_ref, send_ref, turned_hbm, act_three_hbm, back_one_hbm, fwd_four_ref = refs[:outs]
+    olds, refs = refs[:fetched], refs[fetched:]
+    outs = 7 + fetched
+    cut = len(refs) - BLOCK_SCRATCH - outs
+    pieces, refs = refs[:cut], refs[cut:]
+    keep_ref, send_ref, turned_ref, act_three_ref, back_one_ref, fwd_four_ref, img_ref = refs[:7]
+    news = refs[7:outs]
     (
-        turned_ref,
-        act_three_ref,
-        back_one_ref,
         sems,
         stage,
         taps_one,
@@ -313,7 +316,6 @@
         slope_one,
         slope_two,
         turned,
-        masks,
         shifts,
         sum_one,
         sum_two,
@@ -322,24 +324,26 @@
         sum_bias,
     ) = refs[outs:]
     images = even_ref.shape[0]
+    fetches = [
+        pltpu.make_async_copy(source, target, sems.at[which])
+        for which, (source, target) in enumerate(zip((img_hbm, *olds), (img_ref, *news)))
+    ]
+    for fetch in fetches:
+        fetch.start()
     for which in range(2 * images):
         none = jnp.zeros((HALF, EDGE, 128), F32)
         shifts[which, :, 0:EDGE, :] = none
         shifts[which, :, EDGE + SIDE : 2 * EDGE + SIDE, :] = none
-    stores = []
-
-    def store(source, target):
-        copy = pltpu.make_async_copy(source, target, sems.at[len(stores)])
-        copy.start()
-        stores.append(copy)
-
-    unpack_weights(shards, me_ref, pieces, stage, taps_one, taps_two, taps_three, taps_four)
+    me = lax.axis_index(AXES) if shards > 1 else 0
+    unpack_weights(shards, me, pieces, stage, taps_one, taps_two, taps_three, taps_four)
     for col_tap in range(3):
         lanes = slice(col_tap * 128, (col_tap + 1) * 128)
         more = slice(384 + col_tap * 128, 384 + (col_tap + 1) * 128)
         blocks = tap_blocks(taps_one, C, col_tap)
-        for place, block in enumerate(blocks):
-            fwd_one[place * C : (place + 1) * C, lanes] = block.astype(BF16)
+        fwd_one[0:C, lanes] = blocks[1].astype(BF16)
+        fwd_one[C : 2 * C, lanes] = blocks[2].astype(BF16)
+        fwd_one[0:C, more] = blocks[3].astype(BF16)
+        fwd_one[C : 2 * C, more] = blocks[0].astype(BF16)
         back_one_ref[lanes, 0:C] = (0.5 * blocks[1]).T.astype(BF16)
         back_one_ref[lanes, C : 2 * C] = (0.5 * blocks[2]).T.astype(BF16)
         back_one_ref[more, 0:C] = (0.5 * blocks[3]).T.astype(BF16)
@@ -359,7 +363,6 @@
     both = jnp.concatenate([four, four], axis=0)
     fwd_four_ref[...] = both.astype(BF16)
     back_four[...] = (0.5 * both).T.astype(BF16)
-    store(back_one_ref, back_one_hbm)
 
     low = low_lanes((ROWS, 128))
     low_wide = jnp.concatenate([low, low, low], axis=1)
@@ -374,7 +377,6 @@
         total[...] = value if slot == 0 else total[...] + value
 
     def image_phases(slot):
-        masks[slot] = pair_inside(sizes_ref, slot)
         first, second, around_grad = act_one.at[slot], act_two.at[slot], turned.at[slot]
         left, right = shifts.at[2 * slot], shifts.at[2 * slot + 1]
 
@@ -418,16 +420,13 @@
             return here + jnp.where(low, rows_before(around), rows_after(around))
 
         window = jnp.concatenate(
-            [
-                odd_ref[slot, 0:ROWS, :],
-                even_ref[slot, 0:ROWS, :],
-                odd_ref[slot, PAD : PAD + ROWS, :],
-                even_ref[slot, PAD : PAD + ROWS, :],
-            ],
-            axis=1,
+            [even_ref[slot], odd_ref[slot]], axis=1
         )
         parts = dot(window, fwd_one[...])
         yield
+        parts = parts[:, 0:384] + jnp.where(
+            low_wide, rows_before(parts[:, 384:768]), rows_after(parts[:, 384:768])
+        )
         active, slope = activate(shift_sum(parts) + bias_ref[0:1, 0:128])
         keep_active(first, active)
         slope_one[slot] = slope
@@ -448,7 +447,6 @@
         back = back_through(around_grad[:, 0:384], back_three[...])
         add_to(sum_four, dot_rows(spread_ref[slot], act_three_ref[slot]), slot)
         add_to(sum_three, dot_rows(second[...], around_grad[:, 0:384]), slot)
-        store(act_three_ref.at[slot], act_three_hbm.at[slot])
         yield
         turn(back_sum(back) * slope_two[slot], 1, around_grad)
         yield
@@ -458,14 +456,13 @@
         window = turn(back_sum(back) * slope_one[slot], 0, turned_ref.at[slot])
         turned_ref[slot, :, 384:768] = jnp.where(low_wide, rows_after(window), rows_before(window))
         yield
-        store(turned_ref.at[slot], turned_hbm.at[slot])
         if slot % MERGE == MERGE - 1 or slot == images - 1:
             first_slot = slot - slot % MERGE
             slots = range(first_slot, slot + 1)
             both = jnp.concatenate(
                 [
                     jnp.concatenate(
-                        [even_ref[at, 0:ROWS, :], odd_ref[at, PAD : PAD + ROWS, :]], axis=1
+                        [even_ref[at], odd_ref[at]], axis=1
                     )
                     for at in slots
                 ],
@@ -534,8 +531,8 @@
         start = pl.multiple_of(place * held, 8)
         shard = place
         if shards > 1:
-            half = jnp.bitwise_xor(place // (shards // 2), jnp.bitwise_and(me_ref[0], 1))
-            shard = 2 * lax.rem(place, shards // 2) + half
+            other, rest = place // (shards // 2), lax.rem(place, shards // 2)
+            shard = me ^ (sent_mask(shards, rest) | other)
         at = pl.multiple_of(shard * one, 8)
         high = [swap_halves(taps_one[pl.ds(at + first, one - first), :])]
         if gap:
@@ -561,45 +558,43 @@
     rows = keep_ref.shape[0] * held
     keep_ref[...] = stage[0:rows, :].reshape(keep_ref.shape).astype(keep_ref.dtype)
     send_ref[...] = stage[shards * held - rows :, :].reshape(send_ref.shape).astype(BF16)
-    for copy in stores:
-        copy.wait()
-
-
-BLOCK_SCRATCH = 27
-
-
-def run_block(shards, me, sizes, bias_rows, even, odd, spread, pieces):
+    for fetch in fetches:
+        fetch.wait()
+
+
+BLOCK_SCRATCH = 23
+
+
+def run_block(shards, bias_rows, even, odd, masks, spread, images, olds, pieces):
     count = even.shape[0]
     held = pieces[0].shape[1]
     part = max(shards // 2, 1)
-    smem = pl.BlockSpec(memory_space=pltpu.SMEM)
-    hbm = pl.BlockSpec(memory_space=pl.ANY)
     inside = pl.BlockSpec(memory_space=pltpu.VMEM)
     vmem = pltpu.VMEM
+    hbm = pl.BlockSpec(memory_space=pl.ANY)
     place = pltpu.VMEM if shards > 1 else pltpu.HBM
     return pl.pallas_call(
-        functools.partial(block_kernel, shards),
-        in_specs=[smem, smem, *[inside] * (4 + len(pieces))],
-        out_specs=[inside, inside, hbm, hbm, hbm, inside],
+        functools.partial(block_kernel, shards, len(olds)),
+        in_specs=[*[inside] * 5, *[hbm] * (1 + len(olds)), *[inside] * len(pieces)],
+        out_specs=[inside] * (7 + len(olds)),
         out_shape=[
             place((part, held, 128), KEEP_TYPE if shards > 1 else F32),
             place((part, held, 128), BF16),
-            pltpu.HBM((count, ROWS, 768), BF16),
-            pltpu.HBM((count, ROWS, 128), BF16),
-            pltpu.HBM((768, 2 * C), BF16),
-            pltpu.HBM((128, C), BF16),
+            place((count, ROWS, 768), BF16),
+            place((count, ROWS, 128), BF16),
+            place((768, 2 * C), BF16),
+            place((128, C), BF16),
+            place(images.shape, BF16),
+            *[place(old.shape, F32) for old in olds],
         ],
         scratch_shapes=[
-            vmem((count, ROWS, 768), BF16),
-            vmem((count, ROWS, 128), BF16),
-            vmem((768, 2 * C), BF16),
-            pltpu.SemaphoreType.DMA((2 * count + 1,)),
+            pltpu.SemaphoreType.DMA((1 + len(olds),)),
             vmem((shards * held, 128), F32),
             vmem((9 * C, 128), F32),
             vmem((9 * HID, 128), F32),
             vmem((9 * HID, 128), F32),
             vmem((2, HID, 128), F32),
-            vmem((4 * C, 384), BF16),
+            vmem((2 * C, 768), BF16),
             vmem((4 * HID, 384), BF16),
             vmem((384, 256), BF16),
             vmem((4 * HID, 384), BF16),
@@ -610,7 +605,6 @@
             vmem((count, ROWS, 128), F32),
             vmem((count, ROWS, 128), F32),
             vmem((count, ROWS, 384), BF16),
-            vmem((count, ROWS, 128), F32),
             vmem((2 * count, HALF, SIDE + 2 * EDGE, 128), F32),
             vmem((2 * C, 768), F32),
             vmem((256, 384), F32),
@@ -623,65 +617,120 @@
             flops=count * 1_200_000_000, bytes_accessed=count * 2_000_000, transcendentals=count * 196608
         ),
         name="block",
-    )(me, sizes, *(in_vmem if shards > 1 else in_hbm)(bias_rows, even, odd, spread, *pieces))
+    )(
+        *(in_vmem if shards > 1 else in_hbm)(bias_rows, even, odd, masks, spread),
+        *in_hbm(images, *olds),
+        *(in_vmem if shards > 1 else in_hbm)(*pieces),
+    )
 
 
 def finish_kernel(
-    sizes_ref, bias_ref, img_ref, spread_ref, turned_ref, act_ref, back_ref, four_ref, out_ref, grad_ref
+    first,
+    count,
+    masks,
+    bias_ref,
+    img_ref,
+    spread_ref,
+    turned_ref,
+    act_ref,
+    back_ref,
+    four_ref,
+    *refs,
 ):
-    step = pl.program_id(0)
-    mask = pair_inside(sizes_ref, step)
-    wide_mask = jnp.concatenate([mask, mask], axis=1)
+    out_hbm, grad_hbm, out_ref, grad_ref, back, sems = refs[-6:]
+    stores = []
+
+    def store(source, target):
+        copy = pltpu.make_async_copy(source, target, sems.at[len(stores)])
+        copy.start()
+        stores.append(copy)
+
     spot = lax.broadcasted_iota(jnp.int32, (128, 256), 0)
     pix = lax.broadcasted_iota(jnp.int32, (128, 256), 1)
     pool_down = jnp.where(pix // 2 == spot, 0.25, 0.0).astype(BF16)
-    pieces = []
-    for half in range(2):
-        rows = slice(half * 256, (half + 1) * 256)
-        base_mean = dot(pool_down, img_ref[0, :, 0].reshape(ROWS, C)[rows]) + dot(
-            pool_down, img_ref[0, :, 1].reshape(ROWS, C)[rows]
-        )
-        act_mean = dot(pool_down, act_ref[0, rows, :]).astype(BF16)
-        pieces.append(base_mean + GAIN * (dot(act_mean, four_ref[...]) + bias_ref[3:4, :]))
-    result = jnp.where(pooled_inside(sizes_ref, step), jnp.concatenate(pieces, axis=0), 0.0)
-    out_ref[0] = result.reshape(HALF, HALF, C).astype(BF16)
-    spread = 0.25 * spread_ref[0].astype(F32)
-    back = dot(turned_ref[0], back_ref[...])
-    for parity in range(2):
-        _, slope = silu_and_slope(img_ref[0, :, parity].reshape(ROWS, C).astype(F32))
-        slope = slope * wide_mask
-        value = spread + back[:, parity * C : (parity + 1) * C] * slope
-        grad_ref[0, :, parity] = value.reshape(HALF, SIDE, C).astype(BF16)
-
-
-def run_finish(sizes, bias_rows, images, spread, turned, act_three, back_one, fwd_four):
-    count = images.shape[0]
+    back[0] = dot(turned_ref[first], back_ref[...])
+    for slot in range(count):
+        image = first + slot
+        if slot + 1 < count:
+            back[(slot + 1) % 2] = dot(turned_ref[image + 1], back_ref[...])
+        for half in range(2):
+            rows = slice(half * 256, (half + 1) * 256)
+            base_mean = dot(pool_down, img_ref[image, :, 0].reshape(ROWS, C)[rows]) + dot(
+                pool_down, img_ref[image, :, 1].reshape(ROWS, C)[rows]
+            )
+            act_mean = dot(pool_down, act_ref[image, rows, :]).astype(BF16)
+            last = dot(act_mean, four_ref[...]) + bias_ref[3:4, :]
+            pooled = 2.0 * dot(pool_down, masks[image, rows, :].astype(BF16))
+            value = (base_mean + GAIN * last) * jnp.concatenate([pooled, pooled], axis=1)
+            out_ref[slot, half * 8 : (half + 1) * 8] = value.reshape(8, HALF, C).astype(BF16)
+        for start in range(0, ROWS, CHUNK):
+            rows = slice(start, start + CHUNK)
+            pairs = slice(start // SIDE, (start + CHUNK) // SIDE)
+            mask = masks[image, rows, :]
+            wide_mask = jnp.concatenate([mask, mask], axis=1)
+            spread = 0.25 * spread_ref[image, rows, :].astype(F32)
+            for parity in range(2):
+                base = img_ref[image, pairs, parity].reshape(CHUNK, C).astype(F32)
+                _, slope = silu_and_slope(base)
+                lanes = slice(parity * C, (parity + 1) * C)
+                value = spread + back[slot % 2, rows, lanes] * (slope * wide_mask)
+                grad_ref[slot, pairs, parity] = value.reshape(-1, SIDE, C).astype(BF16)
+        store(out_ref.at[slot], out_hbm.at[image])
+        store(grad_ref.at[slot], grad_hbm.at[image])
+    for copy in stores:
+        copy.wait()
+
+
+def run_finish(first, last, before, resident):
+    total = resident[0].shape[0]
+    count = last - first
+    inside = pl.BlockSpec(memory_space=pltpu.VMEM)
+    hbm = pl.BlockSpec(memory_space=pl.ANY)
     return pl.pallas_call(
-        finish_kernel,
-        grid=(count,),
-        in_specs=[
-            pl.BlockSpec(memory_space=pltpu.SMEM),
-            whole((8, C)),
-            block_of((1, HALF, 2, SIDE, C)),
-            block_of((1, ROWS, C)),
-            block_of((1, ROWS, 768)),
-            block_of((1, ROWS, 128)),
-            whole((768, 2 * C)),
-            whole((128, C)),
+        functools.partial(finish_kernel, first, count),
+        in_specs=[*[inside] * len(resident), *[hbm] * len(before)],
+        out_specs=[hbm, hbm],
+        out_shape=[
+            pltpu.HBM((total, HALF, HALF, C), BF16),
+            pltpu.HBM((total, HALF, 2, SIDE, C), BF16),
         ],
-        out_specs=[block_of((1, HALF, HALF, C)), block_of((1, HALF, 2, SIDE, C))],
-        out_shape=[
-            jax.ShapeDtypeStruct((count, HALF, HALF, C), BF16),
-            jax.ShapeDtypeStruct((count, HALF, 2, SIDE, C), BF16),
+        input_output_aliases={len(resident) + which: which for which in range(len(before))},
+        scratch_shapes=[
+            pltpu.VMEM((count, HALF, HALF, C), BF16),
+            pltpu.VMEM((count, HALF, 2, SIDE, C), BF16),
+            pltpu.VMEM((2, ROWS, 2 * C), F32),
+            pltpu.SemaphoreType.DMA((2 * count,)),
         ],
-        compiler_params=pltpu.CompilerParams(
-            dimension_semantics=("arbitrary",), vmem_limit_bytes=60 * 1024 * 1024
-        ),
+        compiler_params=pltpu.CompilerParams(vmem_limit_bytes=FINISH_BYTES),
         cost_estimate=pl.CostEstimate(
             flops=count * 450_000_000, bytes_accessed=count * 2_500_000, transcendentals=count * 262144
         ),
         name="finish",
-    )(sizes, *in_hbm(bias_rows, images, spread, turned, act_three, back_one, fwd_four))
+    )(*resident, *in_hbm(*before))
+
+
+def fold_kernel(got, own_ref, *refs):
+    outs = refs[got:]
+    total = own_ref[...]
+    for ref in refs[:got]:
+        total = total + ref[...].astype(F32)
+    rows = outs[0].shape[0]
+    for which, out in enumerate(outs):
+        out[...] = total[which * rows : (which + 1) * rows].astype(out.dtype)
+
+
+def run_fold(own, received, parts):
+    shape = (own.shape[0] // parts,) + own.shape[1:]
+    inside = pl.BlockSpec(memory_space=pltpu.VMEM)
+    return pl.pallas_call(
+        functools.partial(fold_kernel, len(received)),
+        in_specs=[inside] * (1 + len(received)),
+        out_specs=[inside] * parts,
+        out_shape=[pltpu.VMEM(shape, F32)] + [pltpu.VMEM(shape, BF16)] * (parts - 1),
+        compiler_params=pltpu.CompilerParams(vmem_limit_bytes=FOLD_BYTES),
+        cost_estimate=pl.CostEstimate(flops=500_000, bytes_accessed=1_000_000, transcendentals=0),
+        name="fold",
+    )(*in_vmem(own, *received))
 
 
 def adamw_update(weight, gradient, first_old, second_old, step_rate):
@@ -698,9 +747,13 @@
 RATES = ((9.0 * C) ** (-0.5), (9.0 * HID) ** (-0.5), (9.0 * HID) ** (-0.5), 8.0)
 
 
-def update_kernel(moved_ref, *refs):
+def update_kernel(got, own_ref, *refs):
+    received, refs = refs[:got], refs[got:]
     olds, news, total, rows_of_64 = refs[:15], refs[15:35], refs[35], refs[36]
-    total[...] = jnp.sum(moved_ref[...].astype(F32), axis=0)
+    value = own_ref[0]
+    for ref in received:
+        value = value + ref[0].astype(F32)
+    total[...] = value
     one, first, two, four = shard_layout(COMPACT[0] // olds[0].shape[0])
 
     def joined(rows):
@@ -734,20 +787,20 @@
             ref[...] = value.reshape(ref.shape)
 
 
-def run_update(moved, olds):
+def run_update(own, received, olds):
     shapes = []
     for which in range(5):
         shape = olds[3 * which].shape
         low_shape = shape if which < 4 else shape[1:]
         shapes += [jax.ShapeDtypeStruct(shape, F32)] * 3 + [jax.ShapeDtypeStruct(low_shape, BF16)]
     return pl.pallas_call(
-        update_kernel,
+        functools.partial(update_kernel, len(received)),
         out_shape=shapes,
-        scratch_shapes=[pltpu.VMEM(moved.shape[1:], F32), pltpu.VMEM((80, 128), F32)],
-        compiler_params=pltpu.CompilerParams(vmem_limit_bytes=UPDATE_MB * 1024 * 1024),
+        scratch_shapes=[pltpu.VMEM(own.shape[1:], F32), pltpu.VMEM((80, 128), F32)],
+        compiler_params=pltpu.CompilerParams(vmem_limit_bytes=FOLD_BYTES),
         cost_estimate=pl.CostEstimate(flops=500_000, bytes_accessed=700_000, transcendentals=8192),
         name="update",
-    )(*in_vmem(moved), *in_hbm(*olds))
+    )(*in_vmem(own, *received, *olds))
 
 
 def exchange(value, mask, count):
@@ -780,6 +833,15 @@
         top = low
     groups.append((0, 1))
     return groups
+
+
+def sent_mask(devices, place):
+    mask = 0
+    for low, top in bit_groups(devices)[:-1]:
+        width = top - low
+        mask = mask | ((place & ((1 << width) - 1)) << low)
+        place = place >> width
+    return mask
 
 
 def place_mask(devices, place):
@@ -830,8 +892,6 @@
         and devices >= 8
         and devices & (devices - 1) == 0
     )
-    me = lax.axis_index("dp") * lax.axis_size("fsdp") + lax.axis_index("fsdp")
-    me = jnp.reshape(me, (1,)).astype(jnp.int32)
     shards = devices if packed else 1
     held = shard_held(shards)
     beside = (
@@ -857,23 +917,33 @@
         both = jnp.concatenate([part.reshape(two, HID) for part in parts[1:3]], axis=1)
         full = jnp.concatenate([rows, both, parts[3].reshape(four, 128)], axis=0)
         pieces = [jnp.pad(full, ((0, held - full.shape[0]), (0, 0)))[None]]
-    (spread, bias_rows), (even, odd) = beside
-    keep, send, turned, act_three, back_one, fwd_four = run_block(
-        shards, me, image_sizes, bias_rows, even, odd, spread, pieces
-    )
-    if packed:
-        merged = (keep + exchange(send, 1, devices).astype(F32)).astype(BF16)
-        merged, turned = lax.optimization_barrier((merged, turned))
-        groups = [list(range(core, devices, 2)) for core in range(2)]
-        moved = lax.all_to_all(merged, AXES, 0, 0, axis_index_groups=groups, tiled=False)
-    block_out, image_grad = run_finish(
-        image_sizes, bias_rows, images, spread, turned, act_three, back_one, fwd_four
-    )
-    image_grad = image_grad.reshape(count, SIDE, SIDE, C)
+    (spread, bias_rows), (even, odd, masks) = beside
+    flat = []
     if packed:
         flat = [array.reshape(-1, 128) for three in olds for array in three]
         flat += [array.reshape(1, BIASES) for array in (biases, first_bias, second_bias)]
-        updates = [array.reshape(-1) for array in run_update(moved, flat)]
+    keep, send, turned, act_three, back_one, fwd_four, base, *flat = run_block(
+        shards, bias_rows, even, odd, masks, spread, images, flat, pieces
+    )
+    resident = [masks, bias_rows, base, spread, turned, act_three, back_one, fwd_four]
+    outs = ()
+    if packed:
+        own, received = keep, [exchange(send, 1, devices)]
+        groups = bit_groups(devices)[:-1][::-1]
+        cuts = [0] + [FINISH_SPLIT] * (len(groups) - 1) + [count]
+        for which, (low, top) in enumerate(groups):
+            own, *sent = run_fold(own, received, 1 << (top - low))
+            sent, resident, outs = lax.optimization_barrier((sent, resident, outs))
+            received = [exchange(part, (at + 1) << low, devices) for at, part in enumerate(sent)]
+            if cuts[which] < cuts[which + 1]:
+                outs = run_finish(cuts[which], cuts[which + 1], outs, in_vmem(*resident))
+            received, outs = lax.optimization_barrier((received, outs))
+    else:
+        outs = run_finish(0, count, outs, in_hbm(*resident))
+    block_out, image_grad = outs
+    image_grad = image_grad.reshape(count, SIDE, SIDE, C)
+    if packed:
+        updates = [array.reshape(-1) for array in run_update(own, received, flat)]
         return (block_out, image_grad, *updates)
     rows = keep[0]
     one, first, two, four = shard_layout(1)

time: 52.9 us -> 49.3 us (0.932)
  Pallas kernels: 27 us -> 22.5 us
  starting transfers between devices: 14.8 us -> 18.1 us
  waiting for transfers between devices: 9.09 us -> 7.47 us
  other arithmetic: 0.79 us -> 0 us
    ppermute x11 -> x17, starting transfers between devices: 10.1 us -> 18.1 us  [exchange(): return lax.ppermute(value, AXES, [(i, i ^ mask) for i in range(count)])]
    all_to_all x1 -> x0, starting transfers between devices: 4.66 us -> none  [local(): lax.all_to_all(merged, AXES, 0, 0, axis_index_groups=groups, tiled=False)]
    pallas_call x3 -> x6, Pallas kernels: 21.6 us -> 17.1 us  [the longest x1 10.5 us: run_block(): pl.pallas_call(functools.partial(block_kernel, shards, len(olds)), in_spe...]
    all_to_all x1 -> x0, waiting for transfers between devices: 3.11 us -> none  [local(): lax.all_to_all(merged, AXES, 0, 0, axis_index_groups=groups, tiled=False)]
    ppermute x11 -> x17, waiting for transfers between devices: 5.98 us -> 7.47 us  [exchange(): return lax.ppermute(value, AXES, [(i, i ^ mask) for i in range(count)])]
    convert_element_type x1 -> x0, other arithmetic: 0.79 us -> none  [local(): merged = (keep + exchange(send, 1, devices).astype(F32)).astype(BF16)]
  transfers between devices with their start and end apart: 12 -> 17, of which waited for: 7 -> 9; matrix products, arithmetic and copies ran while one was open for 0% -> 0% of each run, Pallas kernels for 22% -> 21%
where the time goes in v4:
time: 49.3 us; the launch traced here: 49 us
  Pallas kernels  22.5 us (46%)
  starting transfers between devices  18.1 us (37%)
  waiting for transfers between devices  7.47 us (15%)
  between operations  0.95 us (2%)
    ppermute x17, starting transfers between devices, exchange(): return lax.ppermute(value, AXES, [(i, i ^ mask) for i in range(count)])  18.1 us
    pallas_call x1, Pallas kernels, run_block(): pl.pallas_call(functools.partial(block_kernel, shards, len(olds)), in_spe...  10.5 us
    ppermute x17, waiting for transfers between devices, exchange(): return lax.ppermute(value, AXES, [(i, i ^ mask) for i in range(count)])  7.47 us
    pallas_call x2, Pallas kernels, run_finish(): pl.pallas_call(functools.partial(finish_kernel, first, count), in_specs=[...  5.69 us
    pallas_call x1, Pallas kernels, run_active(): pl.pallas_call(active_kernel, grid=(count,), in_specs=[pl.BlockSpec(memor...  2.92 us
    pallas_call x1, Pallas kernels, run_spread(): pl.pallas_call(spread_kernel, in_specs=[pl.BlockSpec(memory_space=pltpu.S...  1.55 us
  transfers between devices with their start and end apart: 17, of which 9 were waited for; matrix products, arithmetic and copies ran while one was open for 0% of the time, Pallas kernels for 21%

profile of v4, /device:TPU:0, one launch (start us, length us, event | category | flops | bytes accessed | tf_op | source)
XLA Modules:
  0.0 49.0 jit_solution(4732345607946516612)
XLA Ops:
  0.7 0.9 %pack.1 = bf16[64,128]{1,0:T(8,128)(2,1)S(1)} custom-call(f32[36,128]{1,0:T(8,128)} %bitcast.45, f32[9,128]{1,0:T(8,128)} %bitcast.47, f32[9,128]{1,0:T(8,128)} %bitcast.49, f32[4,128]{1,0:T(4,128)} %bitcast.55), custom_call_target="tpu_custom_call" | custom-call | flops 8192 | bytes 49152 | tf_op jit(solution)/shard_map/pack/pallas_call | solution.py:111
  1.6 5.1 %collective-permute-start.2 = (bf16[1,64,128]{2,1,0:T(8,128)(2,1)S(1)}, bf16[1,64,128]{2,1,0:T(8,128)(2,1)S(1)}, u32[]{:S(2)}, u32[]{:S(2)}) collective-permute-start(bf16[1,64,128]{2,1,0:T(8,128)(2,1)S(1)} %bitcast.38), channel_id=1, source_target_pairs={{0,24},{1,25},{2,26},{3,27},{4,28},{5,29},{6,30},{7,31},{8,16},{9,... | collective-permute-start | bytes 49160 | tf_op jit(solution)/shard_map/ppermute | solution.py:807
  6.7 0.0 collective-permute-start.1
  6.7 0.6 %collective-permute-start = (bf16[1,64,128]{2,1,0:T(8,128)(2,1)S(1)}, bf16[1,64,128]{2,1,0:T(8,128)(2,1)S(1)}, u32[]{:S(2)}, u32[]{:S(2)}) collective-permute-start(bf16[1,64,128]{2,1,0:T(8,128)(2,1)S(1)} %bitcast.40), channel_id=1, source_target_pairs={{0,8},{1,9},{2,10},{3,11},{4,12},{5,13},{6,14},{7,15},{8,0},{9,1},... | collective-permute-start | bytes 49160 | tf_op jit(solution)/shard_map/ppermute | solution.py:807
  7.3 1.6 %spread.1 = (bf16[4,512,256]{2,1,0:T(8,128)(2,1)S(1)}, f32[8,256]{1,0:T(8,128)S(1)}) custom-call(s32[2,4]{1,0:T(2,128)} %bitcast.51, f32[1,448]{1,0:T(1,128)} %bitcast.53, bf16[4,16,16,256]{3,2,1,0:T(8,128)(2,1)} %og_ref.1), custom_call_target="tpu_custom_call" | custom-call | flops 134217728 | bytes 1600000 | tf_op jit(solution)/shard_map/spread/pallas_call | solution.py:198
  8.9 0.0 collective-permute-done.2
  8.9 2.4 %collective-permute-done.1 = bf16[1,64,128]{2,1,0:T(8,128)(2,1)S(1)} collective-permute-done((bf16[1,64,128]{2,1,0:T(8,128)(2,1)S(1)}, bf16[1,64,128]{2,1,0:T(8,128)(2,1)S(1)}, u32[]{:S(2)}, u32[]{:S(2)}) %collective-permute-start.1) | collective-permute-done | bytes 16416 | tf_op jit(solution)/shard_map/ppermute | solution.py:807
  11.3 0.0 collective-permute-done
  11.4 2.5 %collective-permute-start.5 = (bf16[4,64,128]{2,1,0:T(8,128)(2,1)S(1)}, bf16[4,64,128]{2,1,0:T(8,128)(2,1)S(1)}, u32[]{:S(2)}, u32[]{:S(2)}) collective-permute-start(bf16[4,64,128]{2,1,0:T(8,128)(2,1)S(1)} %constant_dynamic-update-slice_fusion.refs_15_), channel_id=1, source_target_pairs={{0,6},{1,7},{2,4},{3,5},{4,2},{5,3},{6,0},{7,1},{8,14},{9,15},{10,... | collective-permute-start | bytes 196616 | tf_op jit(solution)/shard_map/ppermute | solution.py:807
  13.9 0.5 %collective-permute-start.4 = (bf16[4,64,128]{2,1,0:T(8,128)(2,1)S(1)}, bf16[4,64,128]{2,1,0:T(8,128)(2,1)S(1)}, u32[]{:S(2)}, u32[]{:S(2)}) collective-permute-start(bf16[4,64,128]{2,1,0:T(8,128)(2,1)S(1)} %constant_dynamic-update-slice_fusion.refs_15_), channel_id=1, source_target_pairs={{0,4},{1,5},{2,6},{3,7},{4,0},{5,1},{6,2},{7,3},{8,12},{9,13},{10,... | collective-permute-start | bytes 196616 | tf_op jit(solution)/shard_map/ppermute | solution.py:807
  14.4 0.5 %collective-permute-start.3 = (bf16[4,64,128]{2,1,0:T(8,128)(2,1)S(1)}, bf16[4,64,128]{2,1,0:T(8,128)(2,1)S(1)}, u32[]{:S(2)}, u32[]{:S(2)}) collective-permute-start(bf16[4,64,128]{2,1,0:T(8,128)(2,1)S(1)} %constant_dynamic-update-slice_fusion.refs_15_), channel_id=1, source_target_pairs={{0,2},{1,3},{2,0},{3,1},{4,6},{5,7},{6,4},{7,5},{8,10},{9,11},{10,... | collective-permute-start | bytes 196616 | tf_op jit(solution)/shard_map/ppermute | solution.py:807
  14.9 2.9 %active.1 = (bf16[4,512,256]{2,1,0:T(8,128)(2,1)S(1)}, bf16[4,512,256]{2,1,0:T(8,128)(2,1)S(1)}, f32[4,512,128]{2,1,0:T(8,128)S(1)}) custom-call(s32[2,4]{1,0:T(2,128)} %bitcast.52, bf16[4,16,2,32,256]{4,3,2,1,0:T(8,128)(2,1)} %bitcast.43), custom_call_target="tpu_custom_call" | custom-call | flops 12000000 | bytes 4400000 | tf_op jit(solution)/shard_map/active/pallas_call | solution.py:216
  17.8 0.1 collective-permute-start.6
  17.9 0.0 collective-permute-done.5.refs_18_
  17.9 0.2 collective-permute-done.4.refs_17_
  18.1 0.5 %collective-permute-done.3.refs_16_ = bf16[4,64,128]{2,1,0:T(8,128)(2,1)S(1)} collective-permute-done((bf16[4,64,128]{2,1,0:T(8,128)(2,1)S(1)}, bf16[4,64,128]{2,1,0:T(8,128)(2,1)S(1)}, u32[]{:S(2)}, u32[]{:S(2)}) %collective-permute-start.3) | collective-permute-done | bytes 65568 | tf_op jit(solution)/shard_map/ppermute | solution.py:807
  18.6 0.0 collective-permute-start.7
  18.6 0.5 %collective-permute-start.8 = (bf16[4,64,128]{2,1,0:T(8,128)(2,1)S(1)}, bf16[4,64,128]{2,1,0:T(8,128)(2,1)S(1)}, u32[]{:S(2)}, u32[]{:S(2)}) collective-permute-start(bf16[4,64,128]{2,1,0:T(8,128)(2,1)S(1)} %collective-permute-done.4.refs_17_), channel_id=1, source_target_pairs={{0,1},{1,0},{2,3},{3,2},{4,5},{5,4},{6,7},{7,6},{8,9},{9,8},{10,11... | collective-permute-start | bytes 196616 | tf_op jit(solution)/shard_map/ppermute | solution.py:807
  19.2 0.0 collective-permute-start.9
  19.2 0.0 collective-permute-done.6.refs_19_
  19.2 0.7 %collective-permute-done.7.refs_20_ = bf16[4,64,128]{2,1,0:T(8,128)(2,1)S(1)} collective-permute-done((bf16[4,64,128]{2,1,0:T(8,128)(2,1)S(1)}, bf16[4,64,128]{2,1,0:T(8,128)(2,1)S(1)}, u32[]{:S(2)}, u32[]{:S(2)}) %collective-permute-start.7) | collective-permute-done | bytes 65568 | tf_op jit(solution)/shard_map/ppermute | solution.py:807
  19.9 0.2 collective-permute-done.8.refs_21_
  20.1 0.4 collective-permute-done.9.refs_22_
  20.4 10.5 %block.1 = (f32[16,64,128]{2,1,0:T(8,128)S(1)}, bf16[16,64,128]{2,1,0:T(8,128)(2,1)S(1)}, bf16[4,512,768]{2,1,0:T(8,128)(2,1)S(1)}, bf16[4,512,128]{2,1,0:T(8,12...) custom-call(f32[8,256]{1,0:T(8,128)S(1)} %get-tuple-element.180.bias, ...), custom_call_target="tpu_custom_call" | custom-call | flops 4800000000 | bytes 8000000 | tf_op jit(solution)/shard_map/block/pallas_call | solution.py:576
  30.9 0.2 collective-permute-start.10
  31.1 1.4 %collective-permute-done.10.refs_0_ = bf16[16,64,128]{2,1,0:T(8,128)(2,1)S(1)} collective-permute-done((bf16[16,64,128]{2,1,0:T(8,128)(2,1)S(1)}, bf16[16,64,128]{2,1,0:T(8,128)(2,1)S(1)}, u32[]{:S(2)}, u32[]{:S(2)}) %collective-permute-start.10) | collective-permute-done | bytes 262176 | tf_op jit(solution)/shard_map/ppermute | solution.py:807
  32.6 1.1 %collective-permute-start.11 = (bf16[4,64,128]{2,1,0:T(8,128)(2,1)S(1)}, bf16[4,64,128]{2,1,0:T(8,128)(2,1)S(1)}, u32[]{:S(2)}, u32[]{:S(2)}) collective-permute-start(bf16[4,64,128]{2,1,0:T(8,128)(2,1)S(1)} %get-tuple-element.155), channel_id=1, source_target_pairs={{0,2},{1,3},{2,0},{3,1},{4,6},{5,7},{6,4},{7,5},{8,10},{9,11},{10,... | collective-permute-start | bytes 196616 | tf_op jit(solution)/shard_map/ppermute | solution.py:807
  33.6 1.5 %collective-permute-start.12 = (bf16[4,64,128]{2,1,0:T(8,128)(2,1)S(1)}, bf16[4,64,128]{2,1,0:T(8,128)(2,1)S(1)}, u32[]{:S(2)}, u32[]{:S(2)}) collective-permute-start(bf16[4,64,128]{2,1,0:T(8,128)(2,1)S(1)} %get-tuple-element.156), channel_id=1, source_target_pairs={{0,4},{1,5},{2,6},{3,7},{4,0},{5,1},{6,2},{7,3},{8,12},{9,13},{10,... | collective-permute-start | bytes 196616 | tf_op jit(solution)/shard_map/ppermute | solution.py:807
  35.1 1.0 %collective-permute-start.13 = (bf16[4,64,128]{2,1,0:T(8,128)(2,1)S(1)}, bf16[4,64,128]{2,1,0:T(8,128)(2,1)S(1)}, u32[]{:S(2)}, u32[]{:S(2)}) collective-permute-start(bf16[4,64,128]{2,1,0:T(8,128)(2,1)S(1)} %get-tuple-element.157), channel_id=1, source_target_pairs={{0,6},{1,7},{2,4},{3,5},{4,2},{5,3},{6,0},{7,1},{8,14},{9,15},{10,... | collective-permute-start | bytes 196616 | tf_op jit(solution)/shard_map/ppermute | solution.py:807
  36.1 2.8 %finish.2 = (bf16[4,16,16,256]{3,2,1,0:T(8,128)(2,1)}, bf16[4,16,2,32,256]{4,3,2,1,0:T(8,128)(2,1)}) custom-call(f32[4,512,128]{2,1,0:T(8,128)S(1)} %get-tuple-element.179.masks, f32[8,256]{1,0:T(8,128)S(1)} %get-tuple-element.180.bias_ref, bf16[4,16,2,32,256]{4,3,2,1,0:T(8,128)(2,1)S(1)} %get-tuple-element.181.img_ref, ...), custom_call_target="tpu_custom_call" | custom-call | flops 900000000 | bytes 5000000 | tf_op jit(solution)/shard_map/finish/pallas_call | solution.py:689
  39.0 0.0 collective-permute-done.11.refs_0_
  39.0 0.0 collective-permute-done.12.refs_1_
  39.0 1.3 %collective-permute-done.13.refs_2_ = bf16[4,64,128]{2,1,0:T(8,128)(2,1)S(1)} collective-permute-done((bf16[4,64,128]{2,1,0:T(8,128)(2,1)S(1)}, bf16[4,64,128]{2,1,0:T(8,128)(2,1)S(1)}, u32[]{:S(2)}, u32[]{:S(2)}) %collective-permute-start.13) | collective-permute-done | bytes 65568 | tf_op jit(solution)/shard_map/ppermute | solution.py:807
  40.3 0.1 collective-permute-start.14
  40.4 2.1 %collective-permute-start.15 = (bf16[1,64,128]{2,1,0:T(8,128)(2,1)S(1)}, bf16[1,64,128]{2,1,0:T(8,128)(2,1)S(1)}, u32[]{:S(2)}, u32[]{:S(2)}) collective-permute-start(bf16[1,64,128]{2,1,0:T(8,128)(2,1)S(1)} %get-tuple-element.177), channel_id=1, source_target_pairs={{0,16},{1,17},{2,18},{3,19},{4,20},{5,21},{6,22},{7,23},{8,24},{9,... | collective-permute-start | bytes 49160 | tf_op jit(solution)/shard_map/ppermute | solution.py:807
  42.5 2.3 %collective-permute-start.16 = (bf16[1,64,128]{2,1,0:T(8,128)(2,1)S(1)}, bf16[1,64,128]{2,1,0:T(8,128)(2,1)S(1)}, u32[]{:S(2)}, u32[]{:S(2)}) collective-permute-start(bf16[1,64,128]{2,1,0:T(8,128)(2,1)S(1)} %get-tuple-element.178), channel_id=1, source_target_pairs={{0,24},{1,25},{2,26},{3,27},{4,28},{5,29},{6,30},{7,31},{8,16},{9,... | collective-permute-start | bytes 49160 | tf_op jit(solution)/shard_map/ppermute | solution.py:807
  44.8 2.8 %finish.3 = (bf16[4,16,16,256]{3,2,1,0:T(8,128)(2,1)}, bf16[4,16,2,32,256]{4,3,2,1,0:T(8,128)(2,1)}) custom-call(f32[4,512,128]{2,1,0:T(8,128)S(1)} %get-tuple-element.179.masks, f32[8,256]{1,0:T(8,128)S(1)} %get-tuple-element.180.bias_ref, ...), custom_call_target="tpu_custom_call", output_to_operand_aliasing={{0}: (8, {}), {1}: (9, {})} | custom-call | flops 900000000 | bytes 5000000 | tf_op jit(solution)/shard_map/finish/pallas_call | solution.py:689
  47.6 0.0 collective-permute-done.14.refs_0_
  47.7 0.0 collective-permute-done.15.refs_1_
  47.7 0.4 collective-permute-done.16.refs_2_
  48.0 0.8 %update.1 = (f32[36,128]{1,0:T(8,128)}, f32[36,128]{1,0:T(8,128)}, f32[36,128]{1,0:T(8,128)}, bf16[36,128]{1,0:T(8,128)(2,1)}, f32[9,128]{1,0:T(8,128)}, /*index...) custom-call(f32[1,64,128]{2,1,0:T(8,128)S(1)} %get-tuple-element.193, ...), custom_call_target="tpu_custom_call" | custom-call | flops 500000 | bytes 700000 | tf_op jit(solution)/shard_map/update/pallas_call | solution.py:796
  (6 shorter events, 0.1 us)
Async XLA Ops:
  1.6 7.3 %collective-permute-start.2 = (bf16[1,64,128]{2,1,0:T(8,128)(2,1)S(1)}, bf16[1,64,128]{2,1,0:T(8,128)(2,1)S(1)}, u32[]{:S(2)}, u32[]{:S(2)}) collective-permute-start(bf16[1,64,128]{2,1,0:T(8,128)(2,1)S(1)} %bitcast.38), channel_id=1, source_target_pairs={{0,24},{1,25},{2,26},{3,27},{4,28},{5,29},{6,30},{7,31},{8,16},{9,... | collective-permute-start | bytes 49160 | tf_op jit(solution)/shard_map/ppermute | solution.py:807
  6.7 4.6 %collective-permute-start.1 = (bf16[1,64,128]{2,1,0:T(8,128)(2,1)S(1)}, bf16[1,64,128]{2,1,0:T(8,128)(2,1)S(1)}, u32[]{:S(2)}, u32[]{:S(2)}) collective-permute-start(bf16[1,64,128]{2,1,0:T(8,128)(2,1)S(1)} %bitcast.39), channel_id=1, source_target_pairs={{0,16},{1,17},{2,18},{3,19},{4,20},{5,21},{6,22},{7,23},{8,24},{9,... | collective-permute-start | bytes 49160 | tf_op jit(solution)/shard_map/ppermute | solution.py:807
  6.7 4.6 %collective-permute-start = (bf16[1,64,128]{2,1,0:T(8,128)(2,1)S(1)}, bf16[1,64,128]{2,1,0:T(8,128)(2,1)S(1)}, u32[]{:S(2)}, u32[]{:S(2)}) collective-permute-start(bf16[1,64,128]{2,1,0:T(8,128)(2,1)S(1)} %bitcast.40), channel_id=1, source_target_pairs={{0,8},{1,9},{2,10},{3,11},{4,12},{5,13},{6,14},{7,15},{8,0},{9,1},... | collective-permute-start | bytes 49160 | tf_op jit(solution)/shard_map/ppermute | solution.py:807
  11.4 6.6 %collective-permute-start.5 = (bf16[4,64,128]{2,1,0:T(8,128)(2,1)S(1)}, bf16[4,64,128]{2,1,0:T(8,128)(2,1)S(1)}, u32[]{:S(2)}, u32[]{:S(2)}) collective-permute-start(bf16[4,64,128]{2,1,0:T(8,128)(2,1)S(1)} %constant_dynamic-update-slice_fusion.refs_15_), channel_id=1, source_target_pairs={{0,6},{1,7},{2,4},{3,5},{4,2},{5,3},{6,0},{7,1},{8,14},{9,15},{10,... | collective-permute-start | bytes 196616 | tf_op jit(solution)/shard_map/ppermute | solution.py:807
  13.9 4.3 %collective-permute-start.4 = (bf16[4,64,128]{2,1,0:T(8,128)(2,1)S(1)}, bf16[4,64,128]{2,1,0:T(8,128)(2,1)S(1)}, u32[]{:S(2)}, u32[]{:S(2)}) collective-permute-start(bf16[4,64,128]{2,1,0:T(8,128)(2,1)S(1)} %constant_dynamic-update-slice_fusion.refs_15_), channel_id=1, source_target_pairs={{0,4},{1,5},{2,6},{3,7},{4,0},{5,1},{6,2},{7,3},{8,12},{9,13},{10,... | collective-permute-start | bytes 196616 | tf_op jit(solution)/shard_map/ppermute | solution.py:807
  14.4 4.3 %collective-permute-start.3 = (bf16[4,64,128]{2,1,0:T(8,128)(2,1)S(1)}, bf16[4,64,128]{2,1,0:T(8,128)(2,1)S(1)}, u32[]{:S(2)}, u32[]{:S(2)}) collective-permute-start(bf16[4,64,128]{2,1,0:T(8,128)(2,1)S(1)} %constant_dynamic-update-slice_fusion.refs_15_), channel_id=1, source_target_pairs={{0,2},{1,3},{2,0},{3,1},{4,6},{5,7},{6,4},{7,5},{8,10},{9,11},{10,... | collective-permute-start | bytes 196616 | tf_op jit(solution)/shard_map/ppermute | solution.py:807
  17.8 1.3 %collective-permute-start.6 = (bf16[4,64,128]{2,1,0:T(8,128)(2,1)S(1)}, bf16[4,64,128]{2,1,0:T(8,128)(2,1)S(1)}, u32[]{:S(2)}, u32[]{:S(2)}) collective-permute-start(bf16[4,64,128]{2,1,0:T(8,128)(2,1)S(1)} %constant_dynamic-update-slice_fusion.refs_15_), channel_id=1, source_target_pairs={{0,1},{1,0},{2,3},{3,2},{4,5},{5,4},{6,7},{7,6},{8,9},{9,8},{10,11... | collective-permute-start | bytes 196616 | tf_op jit(solution)/shard_map/ppermute | solution.py:807
  18.6 1.3 %collective-permute-start.7 = (bf16[4,64,128]{2,1,0:T(8,128)(2,1)S(1)}, bf16[4,64,128]{2,1,0:T(8,128)(2,1)S(1)}, u32[]{:S(2)}, u32[]{:S(2)}) collective-permute-start(bf16[4,64,128]{2,1,0:T(8,128)(2,1)S(1)} %collective-permute-done.3.refs_16_), channel_id=1, source_target_pairs={{0,1},{1,0},{2,3},{3,2},{4,5},{5,4},{6,7},{7,6},{8,9},{9,8},{10,11... | collective-permute-start | bytes 196616 | tf_op jit(solution)/shard_map/ppermute | solution.py:807
  18.6 1.4 %collective-permute-start.8 = (bf16[4,64,128]{2,1,0:T(8,128)(2,1)S(1)}, bf16[4,64,128]{2,1,0:T(8,128)(2,1)S(1)}, u32[]{:S(2)}, u32[]{:S(2)}) collective-permute-start(bf16[4,64,128]{2,1,0:T(8,128)(2,1)S(1)} %collective-permute-done.4.refs_17_), channel_id=1, source_target_pairs={{0,1},{1,0},{2,3},{3,2},{4,5},{5,4},{6,7},{7,6},{8,9},{9,8},{10,11... | collective-permute-start | bytes 196616 | tf_op jit(solution)/shard_map/ppermute | solution.py:807
  19.2 1.3 %collective-permute-start.9 = (bf16[4,64,128]{2,1,0:T(8,128)(2,1)S(1)}, bf16[4,64,128]{2,1,0:T(8,128)(2,1)S(1)}, u32[]{:S(2)}, u32[]{:S(2)}) collective-permute-start(bf16[4,64,128]{2,1,0:T(8,128)(2,1)S(1)} %collective-permute-done.5.refs_18_), channel_id=1, source_target_pairs={{0,1},{1,0},{2,3},{3,2},{4,5},{5,4},{6,7},{7,6},{8,9},{9,8},{10,11... | collective-permute-start | bytes 196616 | tf_op jit(solution)/shard_map/ppermute | solution.py:807
  30.9 1.6 %collective-permute-start.10 = (bf16[16,64,128]{2,1,0:T(8,128)(2,1)S(1)}, bf16[16,64,128]{2,1,0:T(8,128)(2,1)S(1)}, u32[]{:S(2)}, u32[]{:S(2)}) collective-permute-start(bf16[16,64,128]{2,1,0:T(8,128)(2,1)S(1)} %get-tuple-element.145), channel_id=1, source_target_pairs={{0,1},{1,0},{2,3},{3,2},{4,5},{5,4},{6,7},{7,6},{8,9},{9,8},{10,11... | collective-permute-start | bytes 786440 | tf_op jit(solution)/shard_map/ppermute | solution.py:807
  32.6 6.4 %collective-permute-start.11 = (bf16[4,64,128]{2,1,0:T(8,128)(2,1)S(1)}, bf16[4,64,128]{2,1,0:T(8,128)(2,1)S(1)}, u32[]{:S(2)}, u32[]{:S(2)}) collective-permute-start(bf16[4,64,128]{2,1,0:T(8,128)(2,1)S(1)} %get-tuple-element.155), channel_id=1, source_target_pairs={{0,2},{1,3},{2,0},{3,1},{4,6},{5,7},{6,4},{7,5},{8,10},{9,11},{10,... | collective-permute-start | bytes 196616 | tf_op jit(solution)/shard_map/ppermute | solution.py:807
  33.6 5.4 %collective-permute-start.12 = (bf16[4,64,128]{2,1,0:T(8,128)(2,1)S(1)}, bf16[4,64,128]{2,1,0:T(8,128)(2,1)S(1)}, u32[]{:S(2)}, u32[]{:S(2)}) collective-permute-start(bf16[4,64,128]{2,1,0:T(8,128)(2,1)S(1)} %get-tuple-element.156), channel_id=1, source_target_pairs={{0,4},{1,5},{2,6},{3,7},{4,0},{5,1},{6,2},{7,3},{8,12},{9,13},{10,... | collective-permute-start | bytes 196616 | tf_op jit(solution)/shard_map/ppermute | solution.py:807
  35.1 5.2 %collective-permute-start.13 = (bf16[4,64,128]{2,1,0:T(8,128)(2,1)S(1)}, bf16[4,64,128]{2,1,0:T(8,128)(2,1)S(1)}, u32[]{:S(2)}, u32[]{:S(2)}) collective-permute-start(bf16[4,64,128]{2,1,0:T(8,128)(2,1)S(1)} %get-tuple-element.157), channel_id=1, source_target_pairs={{0,6},{1,7},{2,4},{3,5},{4,2},{5,3},{6,0},{7,1},{8,14},{9,15},{10,... | collective-permute-start | bytes 196616 | tf_op jit(solution)/shard_map/ppermute | solution.py:807
  40.3 7.3 %collective-permute-start.14 = (bf16[1,64,128]{2,1,0:T(8,128)(2,1)S(1)}, bf16[1,64,128]{2,1,0:T(8,128)(2,1)S(1)}, u32[]{:S(2)}, u32[]{:S(2)}) collective-permute-start(bf16[1,64,128]{2,1,0:T(8,128)(2,1)S(1)} %get-tuple-element.176), channel_id=1, source_target_pairs={{0,8},{1,9},{2,10},{3,11},{4,12},{5,13},{6,14},{7,15},{8,0},{9,1},... | collective-permute-start | bytes 49160 | tf_op jit(solution)/shard_map/ppermute | solution.py:807
  40.4 7.2 %collective-permute-start.15 = (bf16[1,64,128]{2,1,0:T(8,128)(2,1)S(1)}, bf16[1,64,128]{2,1,0:T(8,128)(2,1)S(1)}, u32[]{:S(2)}, u32[]{:S(2)}) collective-permute-start(bf16[1,64,128]{2,1,0:T(8,128)(2,1)S(1)} %get-tuple-element.177), channel_id=1, source_target_pairs={{0,16},{1,17},{2,18},{3,19},{4,20},{5,21},{6,22},{7,23},{8,24},{9,... | collective-permute-start | bytes 49160 | tf_op jit(solution)/shard_map/ppermute | solution.py:807
  42.5 5.5 %collective-permute-start.16 = (bf16[1,64,128]{2,1,0:T(8,128)(2,1)S(1)}, bf16[1,64,128]{2,1,0:T(8,128)(2,1)S(1)}, u32[]{:S(2)}, u32[]{:S(2)}) collective-permute-start(bf16[1,64,128]{2,1,0:T(8,128)(2,1)S(1)} %get-tuple-element.178), channel_id=1, source_target_pairs={{0,24},{1,25},{2,26},{3,27},{4,28},{5,29},{6,30},{7,31},{8,16},{9,... | collective-permute-start | bytes 49160 | tf_op jit(solution)/shard_map/ppermute | solution.py:807

commit v5 on v4

--- a/solution.py
+++ b/solution.py
@@ -22,12 +22,13 @@
 EPSILON = 1e-08
 AXES = ("dp", "fsdp")
 UNROLL = 16
+SPARE = 8
 SPREAD_BYTES = 58 * 1024 * 1024
 ACTIVE_BYTES = 56 * 1024 * 1024
 BLOCK_BYTES = 40 * 1024 * 1024
 FINISH_BYTES = 24 * 1024 * 1024
 FOLD_BYTES = 24 * 1024 * 1024
-FINISH_SPLIT = 2
+FINISH_SPLIT = 3
 CHUNK = 64
 LAG = 1
 MERGE = 2
@@ -359,7 +360,7 @@
             around = jnp.concatenate([blocks[3], blocks[0]], axis=0).T
             back[lanes, 0:128] = (0.5 * here).astype(BF16)
             back[lanes, 128:256] = (0.5 * around).astype(BF16)
-    four = jnp.concatenate([taps_four[0], taps_four[1]], axis=1)
+    four = jnp.concatenate([taps_four[0, 0:HID], taps_four[1, 0:HID]], axis=1)
     both = jnp.concatenate([four, four], axis=0)
     fwd_four_ref[...] = both.astype(BF16)
     back_four[...] = (0.5 * both).T.astype(BF16)
@@ -445,7 +446,9 @@
         turn(back * (GAIN * 0.25) * slope, 2, around_grad)
         yield
         back = back_through(around_grad[:, 0:384], back_three[...])
-        add_to(sum_four, dot_rows(spread_ref[slot], act_three_ref[slot]), slot)
+        part = dot_rows(act_three_ref[slot], spread_ref[slot])
+        for half in (slice(0, HID), slice(HID, 2 * HID)):
+            add_to(sum_four.at[half, :], part[half, :], slot)
         add_to(sum_three, dot_rows(second[...], around_grad[:, 0:384]), slot)
         yield
         turn(back_sum(back) * slope_two[slot], 1, around_grad)
@@ -503,10 +506,9 @@
             ):
                 at = (row_tap * 3 + col_tap) * HID
                 taps[at : at + HID, :] = value
-    last = sum_four[...].T * (GAIN * 0.25)
-    last = last[0:HID, :] + last[HID:128, :]
-    taps_four[0] = last[:, 0:128]
-    taps_four[1] = last[:, 128:256]
+    last = (sum_four[0:HID, :] + sum_four[HID:128, :]) * (GAIN * 0.25)
+    taps_four[0, 0:HID] = last[:, 0:128]
+    taps_four[1, 0:HID] = last[:, 128:256]
     sums = sum_bias[...]
     tail = sums[:, 0:128]
     tail = tail + swap_halves(tail)
@@ -557,7 +559,8 @@
     lax.fori_loop(0, shards, collect, 0, unroll=UNROLL if shards > 1 else 1)
     rows = keep_ref.shape[0] * held
     keep_ref[...] = stage[0:rows, :].reshape(keep_ref.shape).astype(keep_ref.dtype)
-    send_ref[...] = stage[shards * held - rows :, :].reshape(send_ref.shape).astype(BF16)
+    sent = stage[shards * held - rows : shards * held, :]
+    send_ref[...] = sent.reshape(send_ref.shape).astype(BF16)
     for fetch in fetches:
         fetch.wait()
 
@@ -589,11 +592,11 @@
         ],
         scratch_shapes=[
             pltpu.SemaphoreType.DMA((1 + len(olds),)),
-            vmem((shards * held, 128), F32),
-            vmem((9 * C, 128), F32),
-            vmem((9 * HID, 128), F32),
-            vmem((9 * HID, 128), F32),
-            vmem((2, HID, 128), F32),
+            vmem((shards * held + SPARE, 128), F32),
+            vmem((9 * C + SPARE, 128), F32),
+            vmem((9 * HID + SPARE, 128), F32),
+            vmem((9 * HID + SPARE, 128), F32),
+            vmem((2, HID + SPARE, 128), F32),
             vmem((2 * C, 768), BF16),
             vmem((4 * HID, 384), BF16),
             vmem((384, 256), BF16),
@@ -609,7 +612,7 @@
             vmem((2 * C, 768), F32),
             vmem((256, 384), F32),
             vmem((256, 384), F32),
-            vmem((C, 128), F32),
+            vmem((128, C), F32),
             vmem((8, C), F32),
         ],
         compiler_params=pltpu.CompilerParams(vmem_limit_bytes=BLOCK_BYTES),

time: 49.3 us -> 49.2 us (level)
  no operation moved by 1% of the time
where the time goes in v5:
time: 49.2 us; the launch traced here: 48.9 us
  Pallas kernels  22.4 us (46%)
  starting transfers between devices  18.1 us (37%)
  waiting for transfers between devices  7.42 us (15%)
  between operations  0.95 us (2%)
    ppermute x17, starting transfers between devices, exchange(): return lax.ppermute(value, AXES, [(i, i ^ mask) for i in range(count)])  18.1 us
    pallas_call x1, Pallas kernels, run_block(): pl.pallas_call(functools.partial(block_kernel, shards, len(olds)), in_spe...  10.4 us
    ppermute x17, waiting for transfers between devices, exchange(): return lax.ppermute(value, AXES, [(i, i ^ mask) for i in range(count)])  7.42 us
    pallas_call x2, Pallas kernels, run_finish(): pl.pallas_call(functools.partial(finish_kernel, first, count), in_specs=[...  5.73 us
    pallas_call x1, Pallas kernels, run_active(): pl.pallas_call(active_kernel, grid=(count,), in_specs=[pl.BlockSpec(memor...  2.92 us
    pallas_call x1, Pallas kernels, run_spread(): pl.pallas_call(spread_kernel, in_specs=[pl.BlockSpec(memory_space=pltpu.S...  1.55 us
  transfers between devices with their start and end apart: 17, of which 9 were waited for; matrix products, arithmetic and copies ran while one was open for 0% of the time, Pallas kernels for 21%

profile of v5, /device:TPU:0, one launch (start us, length us, event | category | flops | bytes accessed | tf_op | source)
XLA Modules:
  0.0 48.9 jit_solution(5757794377611814743)
XLA Ops:
  0.7 0.9 %pack.1 = bf16[64,128]{1,0:T(8,128)(2,1)S(1)} custom-call(f32[36,128]{1,0:T(8,128)} %bitcast.45, f32[9,128]{1,0:T(8,128)} %bitcast.47, f32[9,128]{1,0:T(8,128)} %bitcast.49, f32[4,128]{1,0:T(4,128)} %bitcast.55), custom_call_target="tpu_custom_call" | custom-call | flops 8192 | bytes 49152 | tf_op jit(solution)/shard_map/pack/pallas_call | solution.py:112
  1.6 5.1 %collective-permute-start.2 = (bf16[1,64,128]{2,1,0:T(8,128)(2,1)S(1)}, bf16[1,64,128]{2,1,0:T(8,128)(2,1)S(1)}, u32[]{:S(2)}, u32[]{:S(2)}) collective-permute-start(bf16[1,64,128]{2,1,0:T(8,128)(2,1)S(1)} %bitcast.38), channel_id=1, source_target_pairs={{0,24},{1,25},{2,26},{3,27},{4,28},{5,29},{6,30},{7,31},{8,16},{9,... | collective-permute-start | bytes 49160 | tf_op jit(solution)/shard_map/ppermute | solution.py:810
  6.7 0.0 collective-permute-start.1
  6.7 0.6 %collective-permute-start = (bf16[1,64,128]{2,1,0:T(8,128)(2,1)S(1)}, bf16[1,64,128]{2,1,0:T(8,128)(2,1)S(1)}, u32[]{:S(2)}, u32[]{:S(2)}) collective-permute-start(bf16[1,64,128]{2,1,0:T(8,128)(2,1)S(1)} %bitcast.40), channel_id=1, source_target_pairs={{0,8},{1,9},{2,10},{3,11},{4,12},{5,13},{6,14},{7,15},{8,0},{9,1},... | collective-permute-start | bytes 49160 | tf_op jit(solution)/shard_map/ppermute | solution.py:810
  7.3 1.6 %spread.1 = (bf16[4,512,256]{2,1,0:T(8,128)(2,1)S(1)}, f32[8,256]{1,0:T(8,128)S(1)}) custom-call(s32[2,4]{1,0:T(2,128)} %bitcast.51, f32[1,448]{1,0:T(1,128)} %bitcast.53, bf16[4,16,16,256]{3,2,1,0:T(8,128)(2,1)} %og_ref.1), custom_call_target="tpu_custom_call" | custom-call | flops 134217728 | bytes 1600000 | tf_op jit(solution)/shard_map/spread/pallas_call | solution.py:199
  8.9 0.0 collective-permute-done.2
  8.9 2.4 %collective-permute-done.1 = bf16[1,64,128]{2,1,0:T(8,128)(2,1)S(1)} collective-permute-done((bf16[1,64,128]{2,1,0:T(8,128)(2,1)S(1)}, bf16[1,64,128]{2,1,0:T(8,128)(2,1)S(1)}, u32[]{:S(2)}, u32[]{:S(2)}) %collective-permute-start.1) | collective-permute-done | bytes 16416 | tf_op jit(solution)/shard_map/ppermute | solution.py:810
  11.3 0.0 collective-permute-done
  11.4 2.5 %collective-permute-start.5 = (bf16[4,64,128]{2,1,0:T(8,128)(2,1)S(1)}, bf16[4,64,128]{2,1,0:T(8,128)(2,1)S(1)}, u32[]{:S(2)}, u32[]{:S(2)}) collective-permute-start(bf16[4,64,128]{2,1,0:T(8,128)(2,1)S(1)} %constant_dynamic-update-slice_fusion.refs_15_), channel_id=1, source_target_pairs={{0,6},{1,7},{2,4},{3,5},{4,2},{5,3},{6,0},{7,1},{8,14},{9,15},{10,... | collective-permute-start | bytes 196616 | tf_op jit(solution)/shard_map/ppermute | solution.py:810
  13.9 0.5 %collective-permute-start.4 = (bf16[4,64,128]{2,1,0:T(8,128)(2,1)S(1)}, bf16[4,64,128]{2,1,0:T(8,128)(2,1)S(1)}, u32[]{:S(2)}, u32[]{:S(2)}) collective-permute-start(bf16[4,64,128]{2,1,0:T(8,128)(2,1)S(1)} %constant_dynamic-update-slice_fusion.refs_15_), channel_id=1, source_target_pairs={{0,4},{1,5},{2,6},{3,7},{4,0},{5,1},{6,2},{7,3},{8,12},{9,13},{10,... | collective-permute-start | bytes 196616 | tf_op jit(solution)/shard_map/ppermute | solution.py:810
  14.4 0.5 %collective-permute-start.3 = (bf16[4,64,128]{2,1,0:T(8,128)(2,1)S(1)}, bf16[4,64,128]{2,1,0:T(8,128)(2,1)S(1)}, u32[]{:S(2)}, u32[]{:S(2)}) collective-permute-start(bf16[4,64,128]{2,1,0:T(8,128)(2,1)S(1)} %constant_dynamic-update-slice_fusion.refs_15_), channel_id=1, source_target_pairs={{0,2},{1,3},{2,0},{3,1},{4,6},{5,7},{6,4},{7,5},{8,10},{9,11},{10,... | collective-permute-start | bytes 196616 | tf_op jit(solution)/shard_map/ppermute | solution.py:810
  14.9 2.9 %active.1 = (bf16[4,512,256]{2,1,0:T(8,128)(2,1)S(1)}, bf16[4,512,256]{2,1,0:T(8,128)(2,1)S(1)}, f32[4,512,128]{2,1,0:T(8,128)S(1)}) custom-call(s32[2,4]{1,0:T(2,128)} %bitcast.52, bf16[4,16,2,32,256]{4,3,2,1,0:T(8,128)(2,1)} %bitcast.43), custom_call_target="tpu_custom_call" | custom-call | flops 12000000 | bytes 4400000 | tf_op jit(solution)/shard_map/active/pallas_call | solution.py:217
  17.8 0.1 collective-permute-start.6
  17.9 0.0 collective-permute-done.5.refs_18_
  17.9 0.2 collective-permute-done.4.refs_17_
  18.1 0.5 %collective-permute-done.3.refs_16_ = bf16[4,64,128]{2,1,0:T(8,128)(2,1)S(1)} collective-permute-done((bf16[4,64,128]{2,1,0:T(8,128)(2,1)S(1)}, bf16[4,64,128]{2,1,0:T(8,128)(2,1)S(1)}, u32[]{:S(2)}, u32[]{:S(2)}) %collective-permute-start.3) | collective-permute-done | bytes 65568 | tf_op jit(solution)/shard_map/ppermute | solution.py:810
  18.6 0.0 collective-permute-start.7
  18.6 0.5 %collective-permute-start.8 = (bf16[4,64,128]{2,1,0:T(8,128)(2,1)S(1)}, bf16[4,64,128]{2,1,0:T(8,128)(2,1)S(1)}, u32[]{:S(2)}, u32[]{:S(2)}) collective-permute-start(bf16[4,64,128]{2,1,0:T(8,128)(2,1)S(1)} %collective-permute-done.4.refs_17_), channel_id=1, source_target_pairs={{0,1},{1,0},{2,3},{3,2},{4,5},{5,4},{6,7},{7,6},{8,9},{9,8},{10,11... | collective-permute-start | bytes 196616 | tf_op jit(solution)/shard_map/ppermute | solution.py:810
  19.2 0.0 collective-permute-start.9
  19.2 0.0 collective-permute-done.6.refs_19_
  19.2 0.7 %collective-permute-done.7.refs_20_ = bf16[4,64,128]{2,1,0:T(8,128)(2,1)S(1)} collective-permute-done((bf16[4,64,128]{2,1,0:T(8,128)(2,1)S(1)}, bf16[4,64,128]{2,1,0:T(8,128)(2,1)S(1)}, u32[]{:S(2)}, u32[]{:S(2)}) %collective-permute-start.7) | collective-permute-done | bytes 65568 | tf_op jit(solution)/shard_map/ppermute | solution.py:810
  19.9 0.2 collective-permute-done.8.refs_21_
  20.1 0.4 collective-permute-done.9.refs_22_
  20.4 10.4 %block.1 = (f32[16,64,128]{2,1,0:T(8,128)S(1)}, bf16[16,64,128]{2,1,0:T(8,128)(2,1)S(1)}, bf16[4,512,768]{2,1,0:T(8,128)(2,1)S(1)}, bf16[4,512,128]{2,1,0:T(8,12...) custom-call(f32[8,256]{1,0:T(8,128)S(1)} %get-tuple-element.180.bias, ...), custom_call_target="tpu_custom_call" | custom-call | flops 4800000000 | bytes 8000000 | tf_op jit(solution)/shard_map/block/pallas_call | solution.py:579
  30.8 0.2 collective-permute-start.10
  31.0 1.4 %collective-permute-done.10.refs_0_ = bf16[16,64,128]{2,1,0:T(8,128)(2,1)S(1)} collective-permute-done((bf16[16,64,128]{2,1,0:T(8,128)(2,1)S(1)}, bf16[16,64,128]{2,1,0:T(8,128)(2,1)S(1)}, u32[]{:S(2)}, u32[]{:S(2)}) %collective-permute-start.10) | collective-permute-done | bytes 262176 | tf_op jit(solution)/shard_map/ppermute | solution.py:810
  32.5 1.1 %collective-permute-start.11 = (bf16[4,64,128]{2,1,0:T(8,128)(2,1)S(1)}, bf16[4,64,128]{2,1,0:T(8,128)(2,1)S(1)}, u32[]{:S(2)}, u32[]{:S(2)}) collective-permute-start(bf16[4,64,128]{2,1,0:T(8,128)(2,1)S(1)} %get-tuple-element.155), channel_id=1, source_target_pairs={{0,2},{1,3},{2,0},{3,1},{4,6},{5,7},{6,4},{7,5},{8,10},{9,11},{10,... | collective-permute-start | bytes 196616 | tf_op jit(solution)/shard_map/ppermute | solution.py:810
  33.5 1.5 %collective-permute-start.12 = (bf16[4,64,128]{2,1,0:T(8,128)(2,1)S(1)}, bf16[4,64,128]{2,1,0:T(8,128)(2,1)S(1)}, u32[]{:S(2)}, u32[]{:S(2)}) collective-permute-start(bf16[4,64,128]{2,1,0:T(8,128)(2,1)S(1)} %get-tuple-element.156), channel_id=1, source_target_pairs={{0,4},{1,5},{2,6},{3,7},{4,0},{5,1},{6,2},{7,3},{8,12},{9,13},{10,... | collective-permute-start | bytes 196616 | tf_op jit(solution)/shard_map/ppermute | solution.py:810
  35.0 1.0 %collective-permute-start.13 = (bf16[4,64,128]{2,1,0:T(8,128)(2,1)S(1)}, bf16[4,64,128]{2,1,0:T(8,128)(2,1)S(1)}, u32[]{:S(2)}, u32[]{:S(2)}) collective-permute-start(bf16[4,64,128]{2,1,0:T(8,128)(2,1)S(1)} %get-tuple-element.157), channel_id=1, source_target_pairs={{0,6},{1,7},{2,4},{3,5},{4,2},{5,3},{6,0},{7,1},{8,14},{9,15},{10,... | collective-permute-start | bytes 196616 | tf_op jit(solution)/shard_map/ppermute | solution.py:810
  36.0 3.8 %finish.2 = (bf16[4,16,16,256]{3,2,1,0:T(8,128)(2,1)}, bf16[4,16,2,32,256]{4,3,2,1,0:T(8,128)(2,1)}) custom-call(f32[4,512,128]{2,1,0:T(8,128)S(1)} %get-tuple-element.179.masks, f32[8,256]{1,0:T(8,128)S(1)} %get-tuple-element.180.bias_ref, bf16[4,16,2,32,256]{4,3,2,1,0:T(8,128)(2,1)S(1)} %get-tuple-element.181.img_ref, ...), custom_call_target="tpu_custom_call" | custom-call | flops 1350000000 | bytes 7500000 | tf_op jit(solution)/shard_map/finish/pallas_call | solution.py:692
  39.8 0.0 collective-permute-done.11.refs_0_
  39.9 0.0 collective-permute-done.12.refs_1_
  39.9 0.3 collective-permute-done.13.refs_2_
  40.2 0.1 collective-permute-start.14
  40.3 2.1 %collective-permute-start.15 = (bf16[1,64,128]{2,1,0:T(8,128)(2,1)S(1)}, bf16[1,64,128]{2,1,0:T(8,128)(2,1)S(1)}, u32[]{:S(2)}, u32[]{:S(2)}) collective-permute-start(bf16[1,64,128]{2,1,0:T(8,128)(2,1)S(1)} %get-tuple-element.177), channel_id=1, source_target_pairs={{0,16},{1,17},{2,18},{3,19},{4,20},{5,21},{6,22},{7,23},{8,24},{9,... | collective-permute-start | bytes 49160 | tf_op jit(solution)/shard_map/ppermute | solution.py:810
  42.4 2.3 %collective-permute-start.16 = (bf16[1,64,128]{2,1,0:T(8,128)(2,1)S(1)}, bf16[1,64,128]{2,1,0:T(8,128)(2,1)S(1)}, u32[]{:S(2)}, u32[]{:S(2)}) collective-permute-start(bf16[1,64,128]{2,1,0:T(8,128)(2,1)S(1)} %get-tuple-element.178), channel_id=1, source_target_pairs={{0,24},{1,25},{2,26},{3,27},{4,28},{5,29},{6,30},{7,31},{8,16},{9,... | collective-permute-start | bytes 49160 | tf_op jit(solution)/shard_map/ppermute | solution.py:810
  44.7 1.9 %finish.3 = (bf16[4,16,16,256]{3,2,1,0:T(8,128)(2,1)}, bf16[4,16,2,32,256]{4,3,2,1,0:T(8,128)(2,1)}) custom-call(f32[4,512,128]{2,1,0:T(8,128)S(1)} %get-tuple-element.179.masks, f32[8,256]{1,0:T(8,128)S(1)} %get-tuple-element.180.bias_ref, ...), custom_call_target="tpu_custom_call", output_to_operand_aliasing={{0}: (8, {}), {1}: (9, {})} | custom-call | flops 450000000 | bytes 2500000 | tf_op jit(solution)/shard_map/finish/pallas_call | solution.py:692
  46.6 0.0 collective-permute-done.14.refs_0_
  46.6 0.0 collective-permute-done.15.refs_1_
  46.6 1.3 %collective-permute-done.16.refs_2_ = bf16[1,64,128]{2,1,0:T(8,128)(2,1)S(1)} collective-permute-done((bf16[1,64,128]{2,1,0:T(8,128)(2,1)S(1)}, bf16[1,64,128]{2,1,0:T(8,128)(2,1)S(1)}, u32[]{:S(2)}, u32[]{:S(2)}) %collective-permute-start.16) | collective-permute-done | bytes 16416 | tf_op jit(solution)/shard_map/ppermute | solution.py:810
  47.9 0.8 %update.1 = (f32[36,128]{1,0:T(8,128)}, f32[36,128]{1,0:T(8,128)}, f32[36,128]{1,0:T(8,128)}, bf16[36,128]{1,0:T(8,128)(2,1)}, f32[9,128]{1,0:T(8,128)}, /*index...) custom-call(f32[1,64,128]{2,1,0:T(8,128)S(1)} %get-tuple-element.193, ...), custom_call_target="tpu_custom_call" | custom-call | flops 500000 | bytes 700000 | tf_op jit(solution)/shard_map/update/pallas_call | solution.py:799
  (6 shorter events, 0.1 us)
Async XLA Ops:
  1.6 7.3 %collective-permute-start.2 = (bf16[1,64,128]{2,1,0:T(8,128)(2,1)S(1)}, bf16[1,64,128]{2,1,0:T(8,128)(2,1)S(1)}, u32[]{:S(2)}, u32[]{:S(2)}) collective-permute-start(bf16[1,64,128]{2,1,0:T(8,128)(2,1)S(1)} %bitcast.38), channel_id=1, source_target_pairs={{0,24},{1,25},{2,26},{3,27},{4,28},{5,29},{6,30},{7,31},{8,16},{9,... | collective-permute-start | bytes 49160 | tf_op jit(solution)/shard_map/ppermute | solution.py:810
  6.7 4.6 %collective-permute-start.1 = (bf16[1,64,128]{2,1,0:T(8,128)(2,1)S(1)}, bf16[1,64,128]{2,1,0:T(8,128)(2,1)S(1)}, u32[]{:S(2)}, u32[]{:S(2)}) collective-permute-start(bf16[1,64,128]{2,1,0:T(8,128)(2,1)S(1)} %bitcast.39), channel_id=1, source_target_pairs={{0,16},{1,17},{2,18},{3,19},{4,20},{5,21},{6,22},{7,23},{8,24},{9,... | collective-permute-start | bytes 49160 | tf_op jit(solution)/shard_map/ppermute | solution.py:810
  6.7 4.6 %collective-permute-start = (bf16[1,64,128]{2,1,0:T(8,128)(2,1)S(1)}, bf16[1,64,128]{2,1,0:T(8,128)(2,1)S(1)}, u32[]{:S(2)}, u32[]{:S(2)}) collective-permute-start(bf16[1,64,128]{2,1,0:T(8,128)(2,1)S(1)} %bitcast.40), channel_id=1, source_target_pairs={{0,8},{1,9},{2,10},{3,11},{4,12},{5,13},{6,14},{7,15},{8,0},{9,1},... | collective-permute-start | bytes 49160 | tf_op jit(solution)/shard_map/ppermute | solution.py:810
  11.4 6.6 %collective-permute-start.5 = (bf16[4,64,128]{2,1,0:T(8,128)(2,1)S(1)}, bf16[4,64,128]{2,1,0:T(8,128)(2,1)S(1)}, u32[]{:S(2)}, u32[]{:S(2)}) collective-permute-start(bf16[4,64,128]{2,1,0:T(8,128)(2,1)S(1)} %constant_dynamic-update-slice_fusion.refs_15_), channel_id=1, source_target_pairs={{0,6},{1,7},{2,4},{3,5},{4,2},{5,3},{6,0},{7,1},{8,14},{9,15},{10,... | collective-permute-start | bytes 196616 | tf_op jit(solution)/shard_map/ppermute | solution.py:810
  13.9 4.3 %collective-permute-start.4 = (bf16[4,64,128]{2,1,0:T(8,128)(2,1)S(1)}, bf16[4,64,128]{2,1,0:T(8,128)(2,1)S(1)}, u32[]{:S(2)}, u32[]{:S(2)}) collective-permute-start(bf16[4,64,128]{2,1,0:T(8,128)(2,1)S(1)} %constant_dynamic-update-slice_fusion.refs_15_), channel_id=1, source_target_pairs={{0,4},{1,5},{2,6},{3,7},{4,0},{5,1},{6,2},{7,3},{8,12},{9,13},{10,... | collective-permute-start | bytes 196616 | tf_op jit(solution)/shard_map/ppermute | solution.py:810
  14.4 4.3 %collective-permute-start.3 = (bf16[4,64,128]{2,1,0:T(8,128)(2,1)S(1)}, bf16[4,64,128]{2,1,0:T(8,128)(2,1)S(1)}, u32[]{:S(2)}, u32[]{:S(2)}) collective-permute-start(bf16[4,64,128]{2,1,0:T(8,128)(2,1)S(1)} %constant_dynamic-update-slice_fusion.refs_15_), channel_id=1, source_target_pairs={{0,2},{1,3},{2,0},{3,1},{4,6},{5,7},{6,4},{7,5},{8,10},{9,11},{10,... | collective-permute-start | bytes 196616 | tf_op jit(solution)/shard_map/ppermute | solution.py:810
  17.8 1.3 %collective-permute-start.6 = (bf16[4,64,128]{2,1,0:T(8,128)(2,1)S(1)}, bf16[4,64,128]{2,1,0:T(8,128)(2,1)S(1)}, u32[]{:S(2)}, u32[]{:S(2)}) collective-permute-start(bf16[4,64,128]{2,1,0:T(8,128)(2,1)S(1)} %constant_dynamic-update-slice_fusion.refs_15_), channel_id=1, source_target_pairs={{0,1},{1,0},{2,3},{3,2},{4,5},{5,4},{6,7},{7,6},{8,9},{9,8},{10,11... | collective-permute-start | bytes 196616 | tf_op jit(solution)/shard_map/ppermute | solution.py:810
  18.6 1.3 %collective-permute-start.7 = (bf16[4,64,128]{2,1,0:T(8,128)(2,1)S(1)}, bf16[4,64,128]{2,1,0:T(8,128)(2,1)S(1)}, u32[]{:S(2)}, u32[]{:S(2)}) collective-permute-start(bf16[4,64,128]{2,1,0:T(8,128)(2,1)S(1)} %collective-permute-done.3.refs_16_), channel_id=1, source_target_pairs={{0,1},{1,0},{2,3},{3,2},{4,5},{5,4},{6,7},{7,6},{8,9},{9,8},{10,11... | collective-permute-start | bytes 196616 | tf_op jit(solution)/shard_map/ppermute | solution.py:810
  18.6 1.4 %collective-permute-start.8 = (bf16[4,64,128]{2,1,0:T(8,128)(2,1)S(1)}, bf16[4,64,128]{2,1,0:T(8,128)(2,1)S(1)}, u32[]{:S(2)}, u32[]{:S(2)}) collective-permute-start(bf16[4,64,128]{2,1,0:T(8,128)(2,1)S(1)} %collective-permute-done.4.refs_17_), channel_id=1, source_target_pairs={{0,1},{1,0},{2,3},{3,2},{4,5},{5,4},{6,7},{7,6},{8,9},{9,8},{10,11... | collective-permute-start | bytes 196616 | tf_op jit(solution)/shard_map/ppermute | solution.py:810
  19.2 1.3 %collective-permute-start.9 = (bf16[4,64,128]{2,1,0:T(8,128)(2,1)S(1)}, bf16[4,64,128]{2,1,0:T(8,128)(2,1)S(1)}, u32[]{:S(2)}, u32[]{:S(2)}) collective-permute-start(bf16[4,64,128]{2,1,0:T(8,128)(2,1)S(1)} %collective-permute-done.5.refs_18_), channel_id=1, source_target_pairs={{0,1},{1,0},{2,3},{3,2},{4,5},{5,4},{6,7},{7,6},{8,9},{9,8},{10,11... | collective-permute-start | bytes 196616 | tf_op jit(solution)/shard_map/ppermute | solution.py:810
  30.8 1.6 %collective-permute-start.10 = (bf16[16,64,128]{2,1,0:T(8,128)(2,1)S(1)}, bf16[16,64,128]{2,1,0:T(8,128)(2,1)S(1)}, u32[]{:S(2)}, u32[]{:S(2)}) collective-permute-start(bf16[16,64,128]{2,1,0:T(8,128)(2,1)S(1)} %get-tuple-element.145), channel_id=1, source_target_pairs={{0,1},{1,0},{2,3},{3,2},{4,5},{5,4},{6,7},{7,6},{8,9},{9,8},{10,11... | collective-permute-start | bytes 786440 | tf_op jit(solution)/shard_map/ppermute | solution.py:810
  32.5 7.4 %collective-permute-start.11 = (bf16[4,64,128]{2,1,0:T(8,128)(2,1)S(1)}, bf16[4,64,128]{2,1,0:T(8,128)(2,1)S(1)}, u32[]{:S(2)}, u32[]{:S(2)}) collective-permute-start(bf16[4,64,128]{2,1,0:T(8,128)(2,1)S(1)} %get-tuple-element.155), channel_id=1, source_target_pairs={{0,2},{1,3},{2,0},{3,1},{4,6},{5,7},{6,4},{7,5},{8,10},{9,11},{10,... | collective-permute-start | bytes 196616 | tf_op jit(solution)/shard_map/ppermute | solution.py:810
  33.5 6.3 %collective-permute-start.12 = (bf16[4,64,128]{2,1,0:T(8,128)(2,1)S(1)}, bf16[4,64,128]{2,1,0:T(8,128)(2,1)S(1)}, u32[]{:S(2)}, u32[]{:S(2)}) collective-permute-start(bf16[4,64,128]{2,1,0:T(8,128)(2,1)S(1)} %get-tuple-element.156), channel_id=1, source_target_pairs={{0,4},{1,5},{2,6},{3,7},{4,0},{5,1},{6,2},{7,3},{8,12},{9,13},{10,... | collective-permute-start | bytes 196616 | tf_op jit(solution)/shard_map/ppermute | solution.py:810
  35.0 5.2 %collective-permute-start.13 = (bf16[4,64,128]{2,1,0:T(8,128)(2,1)S(1)}, bf16[4,64,128]{2,1,0:T(8,128)(2,1)S(1)}, u32[]{:S(2)}, u32[]{:S(2)}) collective-permute-start(bf16[4,64,128]{2,1,0:T(8,128)(2,1)S(1)} %get-tuple-element.157), channel_id=1, source_target_pairs={{0,6},{1,7},{2,4},{3,5},{4,2},{5,3},{6,0},{7,1},{8,14},{9,15},{10,... | collective-permute-start | bytes 196616 | tf_op jit(solution)/shard_map/ppermute | solution.py:810
  40.2 6.4 %collective-permute-start.14 = (bf16[1,64,128]{2,1,0:T(8,128)(2,1)S(1)}, bf16[1,64,128]{2,1,0:T(8,128)(2,1)S(1)}, u32[]{:S(2)}, u32[]{:S(2)}) collective-permute-start(bf16[1,64,128]{2,1,0:T(8,128)(2,1)S(1)} %get-tuple-element.176), channel_id=1, source_target_pairs={{0,8},{1,9},{2,10},{3,11},{4,12},{5,13},{6,14},{7,15},{8,0},{9,1},... | collective-permute-start | bytes 49160 | tf_op jit(solution)/shard_map/ppermute | solution.py:810
  40.3 6.3 %collective-permute-start.15 = (bf16[1,64,128]{2,1,0:T(8,128)(2,1)S(1)}, bf16[1,64,128]{2,1,0:T(8,128)(2,1)S(1)}, u32[]{:S(2)}, u32[]{:S(2)}) collective-permute-start(bf16[1,64,128]{2,1,0:T(8,128)(2,1)S(1)} %get-tuple-element.177), channel_id=1, source_target_pairs={{0,16},{1,17},{2,18},{3,19},{4,20},{5,21},{6,22},{7,23},{8,24},{9,... | collective-permute-start | bytes 49160 | tf_op jit(solution)/shard_map/ppermute | solution.py:810
  42.4 5.5 %collective-permute-start.16 = (bf16[1,64,128]{2,1,0:T(8,128)(2,1)S(1)}, bf16[1,64,128]{2,1,0:T(8,128)(2,1)S(1)}, u32[]{:S(2)}, u32[]{:S(2)}) collective-permute-start(bf16[1,64,128]{2,1,0:T(8,128)(2,1)S(1)} %get-tuple-element.178), channel_id=1, source_target_pairs={{0,24},{1,25},{2,26},{3,27},{4,28},{5,29},{6,30},{7,31},{8,16},{9,... | collective-permute-start | bytes 49160 | tf_op jit(solution)/shard_map/ppermute | solution.py:810

commit v6 on v5

--- a/solution.py
+++ b/solution.py
@@ -31,7 +31,7 @@
 FINISH_SPLIT = 3
 CHUNK = 64
 LAG = 1
-MERGE = 2
+MERGE = 1
 EDGE = 8
 KEEP_TYPE = jnp.float32
 

time: 49.2 us -> 49.2 us (level)
  no operation moved by 1% of the time
where the time goes in v6:
time: 49.2 us; the launch traced here: 49 us
  Pallas kernels  22.4 us (46%)
  starting transfers between devices  18.1 us (37%)
  waiting for transfers between devices  7.42 us (15%)
  between operations  0.95 us (2%)
    ppermute x17, starting transfers between devices, exchange(): return lax.ppermute(value, AXES, [(i, i ^ mask) for i in range(count)])  18.1 us
    pallas_call x1, Pallas kernels, run_block(): pl.pallas_call(functools.partial(block_kernel, shards, len(olds)), in_spe...  10.4 us
    ppermute x17, waiting for transfers between devices, exchange(): return lax.ppermute(value, AXES, [(i, i ^ mask) for i in range(count)])  7.42 us
    pallas_call x2, Pallas kernels, run_finish(): pl.pallas_call(functools.partial(finish_kernel, first, count), in_specs=[...  5.73 us
    pallas_call x1, Pallas kernels, run_active(): pl.pallas_call(active_kernel, grid=(count,), in_specs=[pl.BlockSpec(memor...  2.92 us
    pallas_call x1, Pallas kernels, run_spread(): pl.pallas_call(spread_kernel, in_specs=[pl.BlockSpec(memory_space=pltpu.S...  1.55 us
  transfers between devices with their start and end apart: 17, of which 9 were waited for; matrix products, arithmetic and copies ran while one was open for 0% of the time, Pallas kernels for 21%

profile of v6, /device:TPU:0, one launch (start us, length us, event | category | flops | bytes accessed | tf_op | source)
XLA Modules:
  0.0 49.0 jit_solution(5143842794278998020)
XLA Ops:
  0.7 0.9 %pack.1 = bf16[64,128]{1,0:T(8,128)(2,1)S(1)} custom-call(f32[36,128]{1,0:T(8,128)} %bitcast.45, f32[9,128]{1,0:T(8,128)} %bitcast.47, f32[9,128]{1,0:T(8,128)} %bitcast.49, f32[4,128]{1,0:T(4,128)} %bitcast.55), custom_call_target="tpu_custom_call" | custom-call | flops 8192 | bytes 49152 | tf_op jit(solution)/shard_map/pack/pallas_call | solution.py:112
  1.6 5.1 %collective-permute-start.2 = (bf16[1,64,128]{2,1,0:T(8,128)(2,1)S(1)}, bf16[1,64,128]{2,1,0:T(8,128)(2,1)S(1)}, u32[]{:S(2)}, u32[]{:S(2)}) collective-permute-start(bf16[1,64,128]{2,1,0:T(8,128)(2,1)S(1)} %bitcast.38), channel_id=1, source_target_pairs={{0,24},{1,25},{2,26},{3,27},{4,28},{5,29},{6,30},{7,31},{8,16},{9,... | collective-permute-start | bytes 49160 | tf_op jit(solution)/shard_map/ppermute | solution.py:810
  6.7 0.0 collective-permute-start.1
  6.7 0.6 %collective-permute-start = (bf16[1,64,128]{2,1,0:T(8,128)(2,1)S(1)}, bf16[1,64,128]{2,1,0:T(8,128)(2,1)S(1)}, u32[]{:S(2)}, u32[]{:S(2)}) collective-permute-start(bf16[1,64,128]{2,1,0:T(8,128)(2,1)S(1)} %bitcast.40), channel_id=1, source_target_pairs={{0,8},{1,9},{2,10},{3,11},{4,12},{5,13},{6,14},{7,15},{8,0},{9,1},... | collective-permute-start | bytes 49160 | tf_op jit(solution)/shard_map/ppermute | solution.py:810
  7.3 1.6 %spread.1 = (bf16[4,512,256]{2,1,0:T(8,128)(2,1)S(1)}, f32[8,256]{1,0:T(8,128)S(1)}) custom-call(s32[2,4]{1,0:T(2,128)} %bitcast.51, f32[1,448]{1,0:T(1,128)} %bitcast.53, bf16[4,16,16,256]{3,2,1,0:T(8,128)(2,1)} %og_ref.1), custom_call_target="tpu_custom_call" | custom-call | flops 134217728 | bytes 1600000 | tf_op jit(solution)/shard_map/spread/pallas_call | solution.py:199
  8.9 0.0 collective-permute-done.2
  8.9 2.4 %collective-permute-done.1 = bf16[1,64,128]{2,1,0:T(8,128)(2,1)S(1)} collective-permute-done((bf16[1,64,128]{2,1,0:T(8,128)(2,1)S(1)}, bf16[1,64,128]{2,1,0:T(8,128)(2,1)S(1)}, u32[]{:S(2)}, u32[]{:S(2)}) %collective-permute-start.1) | collective-permute-done | bytes 16416 | tf_op jit(solution)/shard_map/ppermute | solution.py:810
  11.3 0.0 collective-permute-done
  11.4 2.5 %collective-permute-start.5 = (bf16[4,64,128]{2,1,0:T(8,128)(2,1)S(1)}, bf16[4,64,128]{2,1,0:T(8,128)(2,1)S(1)}, u32[]{:S(2)}, u32[]{:S(2)}) collective-permute-start(bf16[4,64,128]{2,1,0:T(8,128)(2,1)S(1)} %constant_dynamic-update-slice_fusion.refs_15_), channel_id=1, source_target_pairs={{0,6},{1,7},{2,4},{3,5},{4,2},{5,3},{6,0},{7,1},{8,14},{9,15},{10,... | collective-permute-start | bytes 196616 | tf_op jit(solution)/shard_map/ppermute | solution.py:810
  13.9 0.5 %collective-permute-start.4 = (bf16[4,64,128]{2,1,0:T(8,128)(2,1)S(1)}, bf16[4,64,128]{2,1,0:T(8,128)(2,1)S(1)}, u32[]{:S(2)}, u32[]{:S(2)}) collective-permute-start(bf16[4,64,128]{2,1,0:T(8,128)(2,1)S(1)} %constant_dynamic-update-slice_fusion.refs_15_), channel_id=1, source_target_pairs={{0,4},{1,5},{2,6},{3,7},{4,0},{5,1},{6,2},{7,3},{8,12},{9,13},{10,... | collective-permute-start | bytes 196616 | tf_op jit(solution)/shard_map/ppermute | solution.py:810
  14.4 0.5 %collective-permute-start.3 = (bf16[4,64,128]{2,1,0:T(8,128)(2,1)S(1)}, bf16[4,64,128]{2,1,0:T(8,128)(2,1)S(1)}, u32[]{:S(2)}, u32[]{:S(2)}) collective-permute-start(bf16[4,64,128]{2,1,0:T(8,128)(2,1)S(1)} %constant_dynamic-update-slice_fusion.refs_15_), channel_id=1, source_target_pairs={{0,2},{1,3},{2,0},{3,1},{4,6},{5,7},{6,4},{7,5},{8,10},{9,11},{10,... | collective-permute-start | bytes 196616 | tf_op jit(solution)/shard_map/ppermute | solution.py:810
  14.9 2.9 %active.1 = (bf16[4,512,256]{2,1,0:T(8,128)(2,1)S(1)}, bf16[4,512,256]{2,1,0:T(8,128)(2,1)S(1)}, f32[4,512,128]{2,1,0:T(8,128)S(1)}) custom-call(s32[2,4]{1,0:T(2,128)} %bitcast.52, bf16[4,16,2,32,256]{4,3,2,1,0:T(8,128)(2,1)} %bitcast.43), custom_call_target="tpu_custom_call" | custom-call | flops 12000000 | bytes 4400000 | tf_op jit(solution)/shard_map/active/pallas_call | solution.py:217
  17.8 0.1 collective-permute-start.6
  17.9 0.0 collective-permute-done.5.refs_18_
  17.9 0.2 collective-permute-done.4.refs_17_
  18.1 0.5 %collective-permute-done.3.refs_16_ = bf16[4,64,128]{2,1,0:T(8,128)(2,1)S(1)} collective-permute-done((bf16[4,64,128]{2,1,0:T(8,128)(2,1)S(1)}, bf16[4,64,128]{2,1,0:T(8,128)(2,1)S(1)}, u32[]{:S(2)}, u32[]{:S(2)}) %collective-permute-start.3) | collective-permute-done | bytes 65568 | tf_op jit(solution)/shard_map/ppermute | solution.py:810
  18.6 0.0 collective-permute-start.7
  18.6 0.5 %collective-permute-start.8 = (bf16[4,64,128]{2,1,0:T(8,128)(2,1)S(1)}, bf16[4,64,128]{2,1,0:T(8,128)(2,1)S(1)}, u32[]{:S(2)}, u32[]{:S(2)}) collective-permute-start(bf16[4,64,128]{2,1,0:T(8,128)(2,1)S(1)} %collective-permute-done.4.refs_17_), channel_id=1, source_target_pairs={{0,1},{1,0},{2,3},{3,2},{4,5},{5,4},{6,7},{7,6},{8,9},{9,8},{10,11... | collective-permute-start | bytes 196616 | tf_op jit(solution)/shard_map/ppermute | solution.py:810
  19.2 0.0 collective-permute-start.9
  19.2 0.0 collective-permute-done.6.refs_19_
  19.2 0.7 %collective-permute-done.7.refs_20_ = bf16[4,64,128]{2,1,0:T(8,128)(2,1)S(1)} collective-permute-done((bf16[4,64,128]{2,1,0:T(8,128)(2,1)S(1)}, bf16[4,64,128]{2,1,0:T(8,128)(2,1)S(1)}, u32[]{:S(2)}, u32[]{:S(2)}) %collective-permute-start.7) | collective-permute-done | bytes 65568 | tf_op jit(solution)/shard_map/ppermute | solution.py:810
  19.9 0.2 collective-permute-done.8.refs_21_
  20.1 0.4 collective-permute-done.9.refs_22_
  20.4 10.4 %block.1 = (f32[16,64,128]{2,1,0:T(8,128)S(1)}, bf16[16,64,128]{2,1,0:T(8,128)(2,1)S(1)}, bf16[4,512,768]{2,1,0:T(8,128)(2,1)S(1)}, bf16[4,512,128]{2,1,0:T(8,12...) custom-call(f32[8,256]{1,0:T(8,128)S(1)} %get-tuple-element.180.bias, ...), custom_call_target="tpu_custom_call" | custom-call | flops 4800000000 | bytes 8000000 | tf_op jit(solution)/shard_map/block/pallas_call | solution.py:579
  30.8 0.2 collective-permute-start.10
  31.1 1.4 %collective-permute-done.10.refs_0_ = bf16[16,64,128]{2,1,0:T(8,128)(2,1)S(1)} collective-permute-done((bf16[16,64,128]{2,1,0:T(8,128)(2,1)S(1)}, bf16[16,64,128]{2,1,0:T(8,128)(2,1)S(1)}, u32[]{:S(2)}, u32[]{:S(2)}) %collective-permute-start.10) | collective-permute-done | bytes 262176 | tf_op jit(solution)/shard_map/ppermute | solution.py:810
  32.5 1.1 %collective-permute-start.11 = (bf16[4,64,128]{2,1,0:T(8,128)(2,1)S(1)}, bf16[4,64,128]{2,1,0:T(8,128)(2,1)S(1)}, u32[]{:S(2)}, u32[]{:S(2)}) collective-permute-start(bf16[4,64,128]{2,1,0:T(8,128)(2,1)S(1)} %get-tuple-element.155), channel_id=1, source_target_pairs={{0,2},{1,3},{2,0},{3,1},{4,6},{5,7},{6,4},{7,5},{8,10},{9,11},{10,... | collective-permute-start | bytes 196616 | tf_op jit(solution)/shard_map/ppermute | solution.py:810
  33.6 1.5 %collective-permute-start.12 = (bf16[4,64,128]{2,1,0:T(8,128)(2,1)S(1)}, bf16[4,64,128]{2,1,0:T(8,128)(2,1)S(1)}, u32[]{:S(2)}, u32[]{:S(2)}) collective-permute-start(bf16[4,64,128]{2,1,0:T(8,128)(2,1)S(1)} %get-tuple-element.156), channel_id=1, source_target_pairs={{0,4},{1,5},{2,6},{3,7},{4,0},{5,1},{6,2},{7,3},{8,12},{9,13},{10,... | collective-permute-start | bytes 196616 | tf_op jit(solution)/shard_map/ppermute | solution.py:810
  35.1 1.0 %collective-permute-start.13 = (bf16[4,64,128]{2,1,0:T(8,128)(2,1)S(1)}, bf16[4,64,128]{2,1,0:T(8,128)(2,1)S(1)}, u32[]{:S(2)}, u32[]{:S(2)}) collective-permute-start(bf16[4,64,128]{2,1,0:T(8,128)(2,1)S(1)} %get-tuple-element.157), channel_id=1, source_target_pairs={{0,6},{1,7},{2,4},{3,5},{4,2},{5,3},{6,0},{7,1},{8,14},{9,15},{10,... | collective-permute-start | bytes 196616 | tf_op jit(solution)/shard_map/ppermute | solution.py:810
  36.1 3.8 %finish.2 = (bf16[4,16,16,256]{3,2,1,0:T(8,128)(2,1)}, bf16[4,16,2,32,256]{4,3,2,1,0:T(8,128)(2,1)}) custom-call(f32[4,512,128]{2,1,0:T(8,128)S(1)} %get-tuple-element.179.masks, f32[8,256]{1,0:T(8,128)S(1)} %get-tuple-element.180.bias_ref, bf16[4,16,2,32,256]{4,3,2,1,0:T(8,128)(2,1)S(1)} %get-tuple-element.181.img_ref, ...), custom_call_target="tpu_custom_call" | custom-call | flops 1350000000 | bytes 7500000 | tf_op jit(solution)/shard_map/finish/pallas_call | solution.py:692
  39.9 0.0 collective-permute-done.11.refs_0_
  39.9 0.0 collective-permute-done.12.refs_1_
  39.9 0.3 collective-permute-done.13.refs_2_
  40.3 0.1 collective-permute-start.14
  40.4 2.1 %collective-permute-start.15 = (bf16[1,64,128]{2,1,0:T(8,128)(2,1)S(1)}, bf16[1,64,128]{2,1,0:T(8,128)(2,1)S(1)}, u32[]{:S(2)}, u32[]{:S(2)}) collective-permute-start(bf16[1,64,128]{2,1,0:T(8,128)(2,1)S(1)} %get-tuple-element.177), channel_id=1, source_target_pairs={{0,16},{1,17},{2,18},{3,19},{4,20},{5,21},{6,22},{7,23},{8,24},{9,... | collective-permute-start | bytes 49160 | tf_op jit(solution)/shard_map/ppermute | solution.py:810
  42.4 2.3 %collective-permute-start.16 = (bf16[1,64,128]{2,1,0:T(8,128)(2,1)S(1)}, bf16[1,64,128]{2,1,0:T(8,128)(2,1)S(1)}, u32[]{:S(2)}, u32[]{:S(2)}) collective-permute-start(bf16[1,64,128]{2,1,0:T(8,128)(2,1)S(1)} %get-tuple-element.178), channel_id=1, source_target_pairs={{0,24},{1,25},{2,26},{3,27},{4,28},{5,29},{6,30},{7,31},{8,16},{9,... | collective-permute-start | bytes 49160 | tf_op jit(solution)/shard_map/ppermute | solution.py:810
  44.7 1.9 %finish.3 = (bf16[4,16,16,256]{3,2,1,0:T(8,128)(2,1)}, bf16[4,16,2,32,256]{4,3,2,1,0:T(8,128)(2,1)}) custom-call(f32[4,512,128]{2,1,0:T(8,128)S(1)} %get-tuple-element.179.masks, f32[8,256]{1,0:T(8,128)S(1)} %get-tuple-element.180.bias_ref, ...), custom_call_target="tpu_custom_call", output_to_operand_aliasing={{0}: (8, {}), {1}: (9, {})} | custom-call | flops 450000000 | bytes 2500000 | tf_op jit(solution)/shard_map/finish/pallas_call | solution.py:692
  46.7 0.0 collective-permute-done.14.refs_0_
  46.7 0.0 collective-permute-done.15.refs_1_
  46.7 1.3 %collective-permute-done.16.refs_2_ = bf16[1,64,128]{2,1,0:T(8,128)(2,1)S(1)} collective-permute-done((bf16[1,64,128]{2,1,0:T(8,128)(2,1)S(1)}, bf16[1,64,128]{2,1,0:T(8,128)(2,1)S(1)}, u32[]{:S(2)}, u32[]{:S(2)}) %collective-permute-start.16) | collective-permute-done | bytes 16416 | tf_op jit(solution)/shard_map/ppermute | solution.py:810
  48.0 0.8 %update.1 = (f32[36,128]{1,0:T(8,128)}, f32[36,128]{1,0:T(8,128)}, f32[36,128]{1,0:T(8,128)}, bf16[36,128]{1,0:T(8,128)(2,1)}, f32[9,128]{1,0:T(8,128)}, /*index...) custom-call(f32[1,64,128]{2,1,0:T(8,128)S(1)} %get-tuple-element.193, ...), custom_call_target="tpu_custom_call" | custom-call | flops 500000 | bytes 700000 | tf_op jit(solution)/shard_map/update/pallas_call | solution.py:799
  (6 shorter events, 0.1 us)
Async XLA Ops:
  1.6 7.3 %collective-permute-start.2 = (bf16[1,64,128]{2,1,0:T(8,128)(2,1)S(1)}, bf16[1,64,128]{2,1,0:T(8,128)(2,1)S(1)}, u32[]{:S(2)}, u32[]{:S(2)}) collective-permute-start(bf16[1,64,128]{2,1,0:T(8,128)(2,1)S(1)} %bitcast.38), channel_id=1, source_target_pairs={{0,24},{1,25},{2,26},{3,27},{4,28},{5,29},{6,30},{7,31},{8,16},{9,... | collective-permute-start | bytes 49160 | tf_op jit(solution)/shard_map/ppermute | solution.py:810
  6.7 4.6 %collective-permute-start.1 = (bf16[1,64,128]{2,1,0:T(8,128)(2,1)S(1)}, bf16[1,64,128]{2,1,0:T(8,128)(2,1)S(1)}, u32[]{:S(2)}, u32[]{:S(2)}) collective-permute-start(bf16[1,64,128]{2,1,0:T(8,128)(2,1)S(1)} %bitcast.39), channel_id=1, source_target_pairs={{0,16},{1,17},{2,18},{3,19},{4,20},{5,21},{6,22},{7,23},{8,24},{9,... | collective-permute-start | bytes 49160 | tf_op jit(solution)/shard_map/ppermute | solution.py:810
  6.7 4.6 %collective-permute-start = (bf16[1,64,128]{2,1,0:T(8,128)(2,1)S(1)}, bf16[1,64,128]{2,1,0:T(8,128)(2,1)S(1)}, u32[]{:S(2)}, u32[]{:S(2)}) collective-permute-start(bf16[1,64,128]{2,1,0:T(8,128)(2,1)S(1)} %bitcast.40), channel_id=1, source_target_pairs={{0,8},{1,9},{2,10},{3,11},{4,12},{5,13},{6,14},{7,15},{8,0},{9,1},... | collective-permute-start | bytes 49160 | tf_op jit(solution)/shard_map/ppermute | solution.py:810
  11.4 6.6 %collective-permute-start.5 = (bf16[4,64,128]{2,1,0:T(8,128)(2,1)S(1)}, bf16[4,64,128]{2,1,0:T(8,128)(2,1)S(1)}, u32[]{:S(2)}, u32[]{:S(2)}) collective-permute-start(bf16[4,64,128]{2,1,0:T(8,128)(2,1)S(1)} %constant_dynamic-update-slice_fusion.refs_15_), channel_id=1, source_target_pairs={{0,6},{1,7},{2,4},{3,5},{4,2},{5,3},{6,0},{7,1},{8,14},{9,15},{10,... | collective-permute-start | bytes 196616 | tf_op jit(solution)/shard_map/ppermute | solution.py:810
  13.9 4.3 %collective-permute-start.4 = (bf16[4,64,128]{2,1,0:T(8,128)(2,1)S(1)}, bf16[4,64,128]{2,1,0:T(8,128)(2,1)S(1)}, u32[]{:S(2)}, u32[]{:S(2)}) collective-permute-start(bf16[4,64,128]{2,1,0:T(8,128)(2,1)S(1)} %constant_dynamic-update-slice_fusion.refs_15_), channel_id=1, source_target_pairs={{0,4},{1,5},{2,6},{3,7},{4,0},{5,1},{6,2},{7,3},{8,12},{9,13},{10,... | collective-permute-start | bytes 196616 | tf_op jit(solution)/shard_map/ppermute | solution.py:810
  14.4 4.3 %collective-permute-start.3 = (bf16[4,64,128]{2,1,0:T(8,128)(2,1)S(1)}, bf16[4,64,128]{2,1,0:T(8,128)(2,1)S(1)}, u32[]{:S(2)}, u32[]{:S(2)}) collective-permute-start(bf16[4,64,128]{2,1,0:T(8,128)(2,1)S(1)} %constant_dynamic-update-slice_fusion.refs_15_), channel_id=1, source_target_pairs={{0,2},{1,3},{2,0},{3,1},{4,6},{5,7},{6,4},{7,5},{8,10},{9,11},{10,... | collective-permute-start | bytes 196616 | tf_op jit(solution)/shard_map/ppermute | solution.py:810
  17.8 1.3 %collective-permute-start.6 = (bf16[4,64,128]{2,1,0:T(8,128)(2,1)S(1)}, bf16[4,64,128]{2,1,0:T(8,128)(2,1)S(1)}, u32[]{:S(2)}, u32[]{:S(2)}) collective-permute-start(bf16[4,64,128]{2,1,0:T(8,128)(2,1)S(1)} %constant_dynamic-update-slice_fusion.refs_15_), channel_id=1, source_target_pairs={{0,1},{1,0},{2,3},{3,2},{4,5},{5,4},{6,7},{7,6},{8,9},{9,8},{10,11... | collective-permute-start | bytes 196616 | tf_op jit(solution)/shard_map/ppermute | solution.py:810
  18.6 1.3 %collective-permute-start.7 = (bf16[4,64,128]{2,1,0:T(8,128)(2,1)S(1)}, bf16[4,64,128]{2,1,0:T(8,128)(2,1)S(1)}, u32[]{:S(2)}, u32[]{:S(2)}) collective-permute-start(bf16[4,64,128]{2,1,0:T(8,128)(2,1)S(1)} %collective-permute-done.3.refs_16_), channel_id=1, source_target_pairs={{0,1},{1,0},{2,3},{3,2},{4,5},{5,4},{6,7},{7,6},{8,9},{9,8},{10,11... | collective-permute-start | bytes 196616 | tf_op jit(solution)/shard_map/ppermute | solution.py:810
  18.6 1.4 %collective-permute-start.8 = (bf16[4,64,128]{2,1,0:T(8,128)(2,1)S(1)}, bf16[4,64,128]{2,1,0:T(8,128)(2,1)S(1)}, u32[]{:S(2)}, u32[]{:S(2)}) collective-permute-start(bf16[4,64,128]{2,1,0:T(8,128)(2,1)S(1)} %collective-permute-done.4.refs_17_), channel_id=1, source_target_pairs={{0,1},{1,0},{2,3},{3,2},{4,5},{5,4},{6,7},{7,6},{8,9},{9,8},{10,11... | collective-permute-start | bytes 196616 | tf_op jit(solution)/shard_map/ppermute | solution.py:810
  19.2 1.3 %collective-permute-start.9 = (bf16[4,64,128]{2,1,0:T(8,128)(2,1)S(1)}, bf16[4,64,128]{2,1,0:T(8,128)(2,1)S(1)}, u32[]{:S(2)}, u32[]{:S(2)}) collective-permute-start(bf16[4,64,128]{2,1,0:T(8,128)(2,1)S(1)} %collective-permute-done.5.refs_18_), channel_id=1, source_target_pairs={{0,1},{1,0},{2,3},{3,2},{4,5},{5,4},{6,7},{7,6},{8,9},{9,8},{10,11... | collective-permute-start | bytes 196616 | tf_op jit(solution)/shard_map/ppermute | solution.py:810
  30.8 1.6 %collective-permute-start.10 = (bf16[16,64,128]{2,1,0:T(8,128)(2,1)S(1)}, bf16[16,64,128]{2,1,0:T(8,128)(2,1)S(1)}, u32[]{:S(2)}, u32[]{:S(2)}) collective-permute-start(bf16[16,64,128]{2,1,0:T(8,128)(2,1)S(1)} %get-tuple-element.145), channel_id=1, source_target_pairs={{0,1},{1,0},{2,3},{3,2},{4,5},{5,4},{6,7},{7,6},{8,9},{9,8},{10,11... | collective-permute-start | bytes 786440 | tf_op jit(solution)/shard_map/ppermute | solution.py:810
  32.5 7.4 %collective-permute-start.11 = (bf16[4,64,128]{2,1,0:T(8,128)(2,1)S(1)}, bf16[4,64,128]{2,1,0:T(8,128)(2,1)S(1)}, u32[]{:S(2)}, u32[]{:S(2)}) collective-permute-start(bf16[4,64,128]{2,1,0:T(8,128)(2,1)S(1)} %get-tuple-element.155), channel_id=1, source_target_pairs={{0,2},{1,3},{2,0},{3,1},{4,6},{5,7},{6,4},{7,5},{8,10},{9,11},{10,... | collective-permute-start | bytes 196616 | tf_op jit(solution)/shard_map/ppermute | solution.py:810
  33.6 6.3 %collective-permute-start.12 = (bf16[4,64,128]{2,1,0:T(8,128)(2,1)S(1)}, bf16[4,64,128]{2,1,0:T(8,128)(2,1)S(1)}, u32[]{:S(2)}, u32[]{:S(2)}) collective-permute-start(bf16[4,64,128]{2,1,0:T(8,128)(2,1)S(1)} %get-tuple-element.156), channel_id=1, source_target_pairs={{0,4},{1,5},{2,6},{3,7},{4,0},{5,1},{6,2},{7,3},{8,12},{9,13},{10,... | collective-permute-start | bytes 196616 | tf_op jit(solution)/shard_map/ppermute | solution.py:810
  35.1 5.2 %collective-permute-start.13 = (bf16[4,64,128]{2,1,0:T(8,128)(2,1)S(1)}, bf16[4,64,128]{2,1,0:T(8,128)(2,1)S(1)}, u32[]{:S(2)}, u32[]{:S(2)}) collective-permute-start(bf16[4,64,128]{2,1,0:T(8,128)(2,1)S(1)} %get-tuple-element.157), channel_id=1, source_target_pairs={{0,6},{1,7},{2,4},{3,5},{4,2},{5,3},{6,0},{7,1},{8,14},{9,15},{10,... | collective-permute-start | bytes 196616 | tf_op jit(solution)/shard_map/ppermute | solution.py:810
  40.3 6.4 %collective-permute-start.14 = (bf16[1,64,128]{2,1,0:T(8,128)(2,1)S(1)}, bf16[1,64,128]{2,1,0:T(8,128)(2,1)S(1)}, u32[]{:S(2)}, u32[]{:S(2)}) collective-permute-start(bf16[1,64,128]{2,1,0:T(8,128)(2,1)S(1)} %get-tuple-element.176), channel_id=1, source_target_pairs={{0,8},{1,9},{2,10},{3,11},{4,12},{5,13},{6,14},{7,15},{8,0},{9,1},... | collective-permute-start | bytes 49160 | tf_op jit(solution)/shard_map/ppermute | solution.py:810
  40.4 6.3 %collective-permute-start.15 = (bf16[1,64,128]{2,1,0:T(8,128)(2,1)S(1)}, bf16[1,64,128]{2,1,0:T(8,128)(2,1)S(1)}, u32[]{:S(2)}, u32[]{:S(2)}) collective-permute-start(bf16[1,64,128]{2,1,0:T(8,128)(2,1)S(1)} %get-tuple-element.177), channel_id=1, source_target_pairs={{0,16},{1,17},{2,18},{3,19},{4,20},{5,21},{6,22},{7,23},{8,24},{9,... | collective-permute-start | bytes 49160 | tf_op jit(solution)/shard_map/ppermute | solution.py:810
  42.4 5.5 %collective-permute-start.16 = (bf16[1,64,128]{2,1,0:T(8,128)(2,1)S(1)}, bf16[1,64,128]{2,1,0:T(8,128)(2,1)S(1)}, u32[]{:S(2)}, u32[]{:S(2)}) collective-permute-start(bf16[1,64,128]{2,1,0:T(8,128)(2,1)S(1)} %get-tuple-element.178), channel_id=1, source_target_pairs={{0,24},{1,25},{2,26},{3,27},{4,28},{5,29},{6,30},{7,31},{8,16},{9,... | collective-permute-start | bytes 49160 | tf_op jit(solution)/shard_map/ppermute | solution.py:810
